TPU v7x, 32 devices: a whole 2x2x4 slice. The times are simulated.
32 devices in a mesh: groups: 2 (over y), width: 4 (over z), tokens: 4 (over x, core).
Axes of the slice: x: 2, y: 2, z: 4, core: 2. Of those that a mesh axis runs over, the one named last changes fastest.
Arguments:
- layer_inputs: bfloat16 [4096, 27648], P(('groups', 'tokens'), 'width'), parts along dimension 0, may hold values from -6 to 6
- output_grads: bfloat16 [4096, 5120], P(('groups', 'tokens'), 'width'), parts along dimension 0, may hold values from -6 to 6
- proj_in: bfloat16 [32, 27648], P(None, 'width'), may hold values from -0.0390625 to 0.0390625
- proj_out: bfloat16 [32, 5120], P(None, 'width'), may hold values from -0.078125 to 0.078125
- prior_gram: float32 [2048, 1024], P(('groups', 'tokens'), 'width'), parts along dimension 0, may hold values from 0 to 512, as said below
- query_bank: float32 [256, 1024], P(('groups', 'tokens')), parts along dimension 0, may hold values from -6 to 6
- slab_sequence: int32 [32], P('groups'), parts along dimension 0, may hold values from 0 to 15, each once
- seq_lengths: int32 [32], P('groups'), parts along dimension 0, may hold values from 16 to 128
- query_ids: int32 [256], P('groups'), parts along dimension 0, may hold values from 0 to 127, as said below
Outputs:
- scores: float32 [256, 16], P(('groups', 'tokens'), 'width'), parts along dimension 0
There are 2 independent parts, one for each index of `groups`. A program takes and returns all parts, laid end to end along the dimension named above; an argument that names none is the same for every part. Nothing has to cross between parts.
Inputs may be any that keep to these rules, and one draw needn't show every extreme that they name: `prior_gram`: symmetric and positive semidefinite. `slab_sequence`: each sequence number names exactly one slab. `query_ids`: ids may repeat.
All inputs are finite; a program needn't handle non-finite values.
Results may differ from a plain program's by a relative error of at most 0.0003.
Values sent between devices are 32-bit elements; how exact they have to be, the bound alone decides.
No kernel may reach another device: no remote copies, remote signals or barrier semaphores. Data moves between devices by JAX's collectives and lax.ppermute only.
A program may use at most 128 MiB of HBM per device.

v0:
```python
import jax
import jax.numpy as jnp
from jax import lax
from jax.sharding import PartitionSpec as P

R_IN = 32
SEQ_LEN = 128
K = 1024


damping_ratio = 0.1
highest = lax.Precision.HIGHEST


def slab_sums(projected, first_row, local_lengths, slab_count):
    row_count = projected.shape[1]
    position = first_row + jnp.arange(row_count, dtype=jnp.int32)
    slab_index = position // SEQ_LEN
    offset = position - slab_index * SEQ_LEN
    owners = jnp.arange(slab_count, dtype=jnp.int32)
    weights = jnp.where(
        (slab_index[None, :] == owners[:, None]) & (offset[None, :] < local_lengths[:, None]),
        1.0,
        0.0,
    ).astype(jnp.float32)
    masked = weights[:, None, :] * projected[None, :R_IN, :]
    products = lax.dot_general(
        masked, projected[R_IN:, :], (((2,), (1,)), ((), ())), precision=highest
    )
    return products.reshape(slab_count, K)


def local(
    layer_inputs,
    output_grads,
    proj_in,
    proj_out,
    prior_gram,
    query_bank,
    slab_sequence,
    seq_lengths,
    query_ids,
):
    width_count = lax.axis_size("width")
    token_count = lax.axis_size("tokens")
    tok_rows = layer_inputs.shape[0]
    slab_count = tok_rows // SEQ_LEN
    sequence_count = slab_sequence.shape[0]
    contract = (((1,), (1,)), ((), ()))
    projected = jnp.concatenate(
        [
            lax.dot_general(proj_in, layer_inputs, contract, preferred_element_type=jnp.float32),
            lax.dot_general(proj_out, output_grads, contract, preferred_element_type=jnp.float32),
        ],
        axis=0,
    )
    local_slabs = lax.dynamic_slice_in_dim(
        slab_sequence, lax.axis_index("tokens") * slab_count, slab_count
    )
    seq_numbers = jnp.arange(sequence_count, dtype=jnp.int32)
    local_lengths = jnp.sum(
        jnp.where(local_slabs[:, None] == seq_numbers[None, :], seq_lengths[None, :], 0), axis=1
    )
    shared = lax.psum_scatter(projected, "width", scatter_dimension=1, tiled=True)
    partial_value = slab_sums(
        shared, lax.axis_index("width") * shared.shape[1], local_lengths, slab_count
    )
    vectors = lax.psum(partial_value, "width")
    prior_block = lax.all_gather(prior_gram, "width", axis=1, tiled=True)
    prior_full = lax.all_gather(prior_block, "tokens", axis=0, tiled=True)
    all_grads = lax.all_gather(vectors, "tokens", axis=0, tiled=True)
    gram_total = (
        prior_full
        + lax.dot_general(all_grads, all_grads, (((0,), (0,)), ((), ())), precision=highest)
        / sequence_count
    )
    damped = gram_total + damping_ratio * jnp.trace(gram_total) / K * jnp.eye(K, dtype=jnp.float32)
    factor = jnp.linalg.cholesky(damped)
    column_count = sequence_count // width_count
    column_ids = lax.axis_index("width") * column_count + jnp.arange(column_count, dtype=jnp.int32)
    chooser = (slab_sequence[:, None] == column_ids[None, :]).astype(jnp.float32)
    chosen = lax.dot_general(chooser, all_grads, (((0,), (0,)), ((), ())), precision=highest)
    solved = jax.scipy.linalg.cho_solve((factor, True), chosen.T)
    query_count = query_ids.shape[0] // token_count
    local_ids = lax.dynamic_slice_in_dim(
        query_ids, lax.axis_index("tokens") * query_count, query_count
    )
    bank_block = jnp.dot(query_bank, solved, precision=highest)
    all_scores = lax.all_gather(bank_block, "tokens", axis=0, tiled=True)
    bank_index = jnp.arange(all_scores.shape[0], dtype=jnp.int32)
    onehot = (local_ids[:, None] == bank_index[None, :]).astype(jnp.float32)
    return jnp.dot(onehot, all_scores, precision=highest)


def solution(mesh):
    return jax.shard_map(
        local,
        mesh=mesh,
        in_specs=(
            P(("groups", "tokens"), "width"),
            P(("groups", "tokens"), "width"),
            P(None, "width"),
            P(None, "width"),
            P(("groups", "tokens"), "width"),
            P(("groups", "tokens"), None),
            P("groups"),
            P("groups"),
            P("groups"),
        ),
        out_specs=P(("groups", "tokens"), "width"),
        check_vma=False,
    )
```

profile of v0, /device:TPU:0, one launch (start us, length us, event | category | flops | bytes accessed | tf_op | source)
XLA Modules:
  0.0 469.3 jit_solution(13355141404350422266)
XLA Ops:
  6.5 1.9 copy.69
  8.5 1.4 fusion.108
  9.9 5.3 %fusion.107 = f32[32,512]{1,0:T(8,128)S(1)} fusion(bf16[32,6912]{1,0:T(8,128)(2,1)} %param.11, bf16[512,6912]{1,0:T(8,128)(2,1)} %param.9), kind=kOutput, calls=%fused_computation.243 | convolution fusion | flops 226492416 | bytes 7585792 | tf_op jit(solution)/shard_map/dot_general | solution.py:52
  16.0 23.6 %all-gather.5.cloned.1.call-done = f32[256,1024]{0,1:T(8,128)} async-done(((f32[256,256]{0,1:T(8,128)}), f32[256,1024]{0,1:T(8,128)}) %all-gather.5.cloned.1.call-update) | async-done | bytes 1048592 | tf_op jit(solution)/shard_map/all_gather | solution.py:69
  40.1 20.4 %reduce-scatter.2.cloned.1.call-done = f32[64,128]{1,0:T(8,128)} async-done(((f32[64,512]{1,0:T(8,128)}), f32[64,128]{1,0:T(8,128)}) %reduce-scatter.2.cloned.1.call-update) | async-done | bytes 32784 | tf_op jit(solution)/shard_map/reduce_scatter | solution.py:64
  62.2 15.9 %psum.7 = f32[4,1024]{1,0:T(4,128)S(1)} all-reduce(f32[4,1024]{1,0:T(4,128)S(1)} %reshape.176), channel_id=1, replica_groups=mesh['groups'=2,'width'=4,'tokens'=4] {'width'}, use_global_device_ids=true, to_apply=%region_2.3 | all-reduce | flops 4096 | bytes 32768 | tf_op jit(solution)/shard_map/psum | solution.py:68
  78.1 5.6 %all-gather = f32[4,4,1024]{2,1,0:T(4,128)S(1)} all-gather(f32[1,4,1024]{2,1,0:T(4,128)S(1)} %bitcast.145), channel_id=1, replica_groups=mesh['groups'=2,'width'=4,'tokens'=4] {'tokens'}, dimensions={0}, use_global_device_ids=true | all-gather | bytes 81920 | tf_op jit(solution)/shard_map/all_gather | solution.py:71
  84.0 11.2 %all-gather.7.cloned.1.call-done = f32[1024,1024]{0,1:T(8,128)} async-done(((f32[256,1024]{0,1:T(8,128)}), f32[1024,1024]{0,1:T(8,128)}) %all-gather.7.cloned.1.call-update) | async-done | bytes 4194320 | tf_op jit(solution)/shard_map/all_gather | solution.py:70
  95.2 8.0 %select_reduce_fusion = (f32[]{:T(128)}, f32[1024,1024]{0,1:T(8,128)}) fusion(f32[1024,1024]{0,1:T(8,128)} %all-gather.7.cloned.1.call-done, f32[16,1024]{1,0:T(8,128)S(1)} %reshape.201), kind=kOutput, calls=%fused_computation.6 | convolution fusion | flops 206569472 | bytes 8454148 | tf_op jit(solution)/shard_map/dot_general | solution.py:74
  103.7 4.8 %select_add_fusion = f32[1024,1024]{0,1:T(8,128)} fusion(f32[1024,1024]{0,1:T(8,128)} %get-tuple-element.71, f32[]{:T(128)S(6)} %div.35), kind=kLoop, calls=%fused_computation.5 | loop fusion | flops 3145728 | bytes 8388612 | tf_op jit(solution)/shard_map/add | solution.py:77
  108.6 5.6 %copy.71 = f32[1024,1024]{1,0:T(8,128)} copy(f32[1024,1024]{0,1:T(8,128)} %select_add_fusion) | data formatting | bytes 8388608 | tf_op jit(solution)/shard_map/add | solution.py:77
  114.2 4.5 fusion
  118.7 1.9 copy-done.2
  120.6 11.7 %cholesky.222 = f32[128,128]{1,0:T(8,128)S(1)} custom-call(f32[128,128]{1,0:T(8,128)S(1)} %cholesky.577), custom_call_target="Cholesky" | custom-call | tf_op jit(solution)/shard_map/jit(cholesky)/cholesky | solution.py:78
  132.5 9.8 %custom-call.66 = f32[1,128,128]{1,2,0:T(8,128)S(1)} custom-call(f32[1,128,128]{2,1,0:T(8,128)S(1)} %get-tuple-element.52), custom_call_target="InvertDiagBlocksLowerTriangular" | custom-call | tf_op jit(solution)/shard_map/jit(cholesky)/cholesky | solution.py:78
  142.3 1.5 fusion.9
  144.0 1.6 convolution_subtract_fusion
  145.6 11.7 %cholesky.243 = f32[128,128]{1,0:T(8,128)S(1)} custom-call(f32[128,128]{1,0:T(8,128)S(1)} %cholesky.581), custom_call_target="Cholesky" | custom-call | tf_op jit(solution)/shard_map/jit(cholesky)/cholesky | solution.py:78
  157.9 9.8 %custom-call.67 = f32[1,128,128]{1,2,0:T(8,128)S(1)} custom-call(f32[1,128,128]{2,1,0:T(8,128)S(1)} %get-tuple-element.50), custom_call_target="InvertDiagBlocksLowerTriangular" | custom-call | tf_op jit(solution)/shard_map/jit(cholesky)/cholesky | solution.py:78
  168.9 2.0 copy-done.1
  170.8 2.4 convolution_subtract_fusion.1
  173.3 11.7 %cholesky.466 = f32[128,128]{1,0:T(8,128)S(1)} custom-call(f32[128,128]{1,0:T(8,128)S(1)} %cholesky.586), custom_call_target="Cholesky" | custom-call | tf_op jit(solution)/shard_map/jit(cholesky)/cholesky | solution.py:78
  185.8 9.8 %custom-call.68 = f32[1,128,128]{1,2,0:T(8,128)S(1)} custom-call(f32[1,128,128]{2,1,0:T(8,128)S(1)} %get-tuple-element.48), custom_call_target="InvertDiagBlocksLowerTriangular" | custom-call | tf_op jit(solution)/shard_map/jit(cholesky)/cholesky | solution.py:78
  195.6 1.3 convolution_dynamic-update-slice_fusion.1
  196.8 3.3 convolution_subtract_fusion.2
  200.1 11.7 %cholesky.485 = f32[128,128]{1,0:T(8,128)S(1)} custom-call(f32[128,128]{1,0:T(8,128)S(1)} %cholesky.591), custom_call_target="Cholesky" | custom-call | tf_op jit(solution)/shard_map/jit(cholesky)/cholesky | solution.py:78
  212.6 9.8 %custom-call.69 = f32[1,128,128]{1,2,0:T(8,128)S(1)} custom-call(f32[1,128,128]{2,1,0:T(8,128)S(1)} %get-tuple-element.46), custom_call_target="InvertDiagBlocksLowerTriangular" | custom-call | tf_op jit(solution)/shard_map/jit(cholesky)/cholesky | solution.py:78
  222.5 1.1 convolution_dynamic-update-slice_fusion.2
  223.6 3.2 convolution_subtract_fusion.3
  226.8 11.9 %cholesky.504 = f32[128,128]{1,0:T(8,128)S(1)} custom-call(f32[128,128]{1,0:T(8,128)S(1)} %cholesky.596), custom_call_target="Cholesky" | custom-call | tf_op jit(solution)/shard_map/jit(cholesky)/cholesky | solution.py:78
  239.4 9.8 %custom-call.70 = f32[1,128,128]{1,2,0:T(8,128)S(1)} custom-call(f32[1,128,128]{2,1,0:T(8,128)S(1)} %get-tuple-element.44), custom_call_target="InvertDiagBlocksLowerTriangular" | custom-call | tf_op jit(solution)/shard_map/jit(cholesky)/cholesky | solution.py:78
  249.3 1.1 convolution_dynamic-update-slice_fusion.3
  250.4 3.1 convolution_subtract_fusion.4
  253.5 11.7 %cholesky.524 = f32[128,128]{1,0:T(8,128)S(1)} custom-call(f32[128,128]{1,0:T(8,128)S(1)} %cholesky.601), custom_call_target="Cholesky" | custom-call | tf_op jit(solution)/shard_map/jit(cholesky)/cholesky | solution.py:78
  265.9 9.8 %custom-call.71 = f32[1,128,128]{1,2,0:T(8,128)S(1)} custom-call(f32[1,128,128]{2,1,0:T(8,128)S(1)} %get-tuple-element.42), custom_call_target="InvertDiagBlocksLowerTriangular" | custom-call | tf_op jit(solution)/shard_map/jit(cholesky)/cholesky | solution.py:78
  276.8 3.1 convolution_subtract_fusion.5
  279.8 11.7 %cholesky.544 = f32[128,128]{1,0:T(8,128)S(1)} custom-call(f32[128,128]{1,0:T(8,128)S(1)} %cholesky.606), custom_call_target="Cholesky" | custom-call | tf_op jit(solution)/shard_map/jit(cholesky)/cholesky | solution.py:78
  292.3 9.8 %custom-call.72 = f32[1,128,128]{1,2,0:T(8,128)S(1)} custom-call(f32[1,128,128]{2,1,0:T(8,128)S(1)} %get-tuple-element.40), custom_call_target="InvertDiagBlocksLowerTriangular" | custom-call | tf_op jit(solution)/shard_map/jit(cholesky)/cholesky | solution.py:78
  303.1 2.1 convolution_subtract_fusion.6
  305.2 11.7 %cholesky.562 = f32[128,128]{1,0:T(8,128)S(1)} custom-call(f32[128,128]{1,0:T(8,128)S(1)} %convolution_subtract_fusion.6), custom_call_target="Cholesky" | custom-call | tf_op jit(solution)/shard_map/jit(cholesky)/cholesky | solution.py:78
  328.0 4.8 %select_select_fusion = f32[1024,1024]{0,1:T(8,128)} fusion(f32[1024,1024]{0,1:T(8,128)} %constant_dynamic-update-slice_fusion.48, pred[]{:T(512)S(6)} %cholesky.576), kind=kLoop, calls=%fused_computation.2 | loop fusion | flops 4194304 | bytes 8388609 | tf_op jit(solution)/shard_map/jit(_cho_solve)/triangular_solve | solution.py:83
  332.8 23.7 %while.1 = (s32[]{:T(128)}, f32[1024,1024]{0,1:T(8,128)}, s32[8,2]{0,1:T(2,128)S(1)}, f32[8,128,128]{2,1,0:T(8,128)S(1)}, s32[]{:T(128)}) while((s32[]{:T(128)}, f32[1024,1024]{0,1:T(8,128)}, s32[8,2]{0,1:T(2,128)S(1)}, f32[8,128,128]{2,1,0:T(8,128)S(1)}, s32[]{:T(128)}) %tuple.53), condition=%wide.while_cond, body=%wide.while_body.sunk | while | flops 2 | bytes 393329 | solution.py:83
  333.4 2.2 dynamic-slice.7
  336.4 2.2 dynamic-slice.7
  339.4 2.2 dynamic-slice.7
  342.4 2.2 dynamic-slice.7
  345.4 2.2 dynamic-slice.7
  348.3 2.2 dynamic-slice.7
  351.3 2.2 dynamic-slice.7
  354.3 2.2 dynamic-slice.7
  356.6 78.8 %custom-call.73 = f32[8,128,128]{1,2,0:T(8,128)S(1)} custom-call(f32[8,128,128]{2,1,0:T(8,128)S(1)} %get-tuple-element.12), custom_call_target="InvertDiagBlocksLowerTriangular" | custom-call | tf_op jit(solution)/shard_map/jit(_cho_solve)/triangular_solve | solution.py:83
  436.7 1.1 convolution_subtract_fusion.17
  438.0 1.2 convolution_subtract_fusion.16
  439.3 1.2 convolution_subtract_fusion.15
  440.7 1.3 convolution_subtract_fusion.14
  442.2 1.3 convolution_subtract_fusion.20
  443.7 1.4 convolution_subtract_fusion.8
  446.7 1.1 convolution_subtract_fusion.12
  448.1 1.2 convolution_subtract_fusion.11
  449.5 1.3 convolution_subtract_fusion.10
  451.1 1.4 convolution_subtract_fusion.9
  452.8 1.4 convolution_subtract_fusion.19
  454.5 1.5 convolution_subtract_fusion.7
  456.5 5.2 %all-gather.1 = f32[4,32,4]{1,2,0:T(4,128)S(1)} all-gather(f32[1,32,4]{1,2,0:T(4,128)S(1)} %convolution_bitcast_fusion), channel_id=1, replica_groups=mesh['groups'=2,'width'=4,'tokens'=4] {'tokens'}, dimensions={0}, use_global_device_ids=true | all-gather | bytes 2560 | tf_op jit(solution)/shard_map/all_gather | solution.py:89
  (153 shorter events, 29.5 us)
Async XLA Ops:
  6.5 2.0 copy-start
  6.5 33.1 %all-gather.5.cloned.1.call-start = ((), (), s32[]{:S(2)}) async-start(), calls=%async_computation.1 | async-start | bytes 1310720 | tf_op jit(solution)/shard_map/all_gather | solution.py:69
  8.4 52.1 %reduce-scatter.2.cloned.1.call-start = ((), (), s32[]{:S(2)}) async-start(), calls=%async_computation.3 | async-start | bytes 163840 | tf_op jit(solution)/shard_map/reduce_scatter | solution.py:64
  9.9 29.8 %copy-start.6 = (s32[16]{0:T(128)S(1)}, s32[16]{0:T(128)}, u32[]{:S(2)}) copy-start(s32[16]{0:T(128)} %param.15) | copy-start | bytes 196
  9.9 29.9 %copy-start.4 = (s32[128]{0:T(128)S(1)}, s32[128]{0:T(128)}, u32[]{:S(2)}) copy-start(s32[128]{0:T(128)} %param.17) | copy-start | bytes 1540
  9.9 29.9 %copy-start.5 = (s32[16]{0:T(128)S(1)}, s32[16]{0:T(128)}, u32[]{:S(2)}) copy-start(s32[16]{0:T(128)} %param.16) | copy-start | bytes 196
  15.9 79.3 %all-gather.7.cloned.1.call-start = ((), (), s32[]{:S(2)}) async-start(), calls=%async_computation.2 | async-start | bytes 5242880 | tf_op jit(solution)/shard_map/all_gather | solution.py:70
  118.7 1.9 copy-start.2
  168.9 2.0 copy-start.1
  332.8 123.5 %copy-start.3 = (f32[32,1024]{1,0:T(8,128)S(1)}, f32[32,1024]{1,0:T(8,128)}, u32[]{:S(2)}) copy-start(f32[32,1024]{1,0:T(8,128)} %param.14) | copy-start | bytes 393220
Sparse Core Ops, SparseCore 0:
  8.9 30.6 all-gather.4
  41.8 18.6 reduce-scatter.1
  62.1 33.0 all-gather.6
where the time goes:
time: 475 us; the launch traced here: 469 us
  other arithmetic  262 us (55%)
  matrix products  63.4 us (13%)
  waiting for transfers between devices  55.3 us (12%)
  local copies, waits for them, and re-layouts  42.2 us (9%)
  blocking collectives  26.7 us (6%)
  between operations  19.4 us (4%)
    another operation x31, other arithmetic, local(): factor = jnp.linalg.cholesky(damped)  168 us
    another operation x3, other arithmetic, local(): solved = jax.scipy.linalg.cho_solve((factor, True), chosen.T)  83.6 us
    another operation x14, matrix products, local(): factor = jnp.linalg.cholesky(damped)  26.1 us
    all_gather x1, waiting for transfers between devices, local(): prior_block = lax.all_gather(prior_gram, 'width', axis=1, tiled=True)  23.6 us
    another operation x40, local copies, waits for them, and re-layouts  23.5 us
    another operation x30, matrix products, local(): solved = jax.scipy.linalg.cho_solve((factor, True), chosen.T)  20.6 us
    reduce_scatter x1, waiting for transfers between devices, local(): lax.psum_scatter(projected, 'width', scatter_dimension=1, tiled=True)  20.4 us
    psum x1, blocking collectives, local(): vectors = lax.psum(partial_value, 'width')  15.9 us
  transfers between devices with their start and end apart: 3, of which 3 were waited for; matrix products, arithmetic and copies ran while one was open for 2% of the time, Pallas kernels for 0%

commit v1 on v0

--- a/solution.py
+++ b/solution.py
@@ -1,15 +1,175 @@
 import jax
 import jax.numpy as jnp
 from jax import lax
+from jax.experimental import pallas as pl
+from jax.experimental.pallas import tpu as pltpu
 from jax.sharding import PartitionSpec as P
 
 R_IN = 32
 SEQ_LEN = 128
 K = 1024
+BLOCK = 128
+PIVOTS = 16
+TERMS = 6
+f32 = jnp.float32
 
 
 damping_ratio = 0.1
 highest = lax.Precision.HIGHEST
+
+
+def split_terms(value):
+    high = value.astype(jnp.bfloat16)
+    rest = value - high.astype(f32)
+    mid = rest.astype(jnp.bfloat16)
+    low = (rest - mid.astype(f32)).astype(jnp.bfloat16)
+    return high, mid, low
+
+
+def left_terms(value, axis):
+    high, mid, low = split_terms(value)
+    return jnp.concatenate([high, high, mid, mid, high, low], axis)
+
+
+def right_terms(value, axis):
+    high, mid, low = split_terms(value)
+    return jnp.concatenate([high, mid, high, mid, low, high], axis)
+
+
+def both_terms(value, axis):
+    high, mid, low = split_terms(value)
+    return (
+        jnp.concatenate([high, high, mid, mid, high, low], axis),
+        jnp.concatenate([high, mid, high, mid, low, high], axis),
+    )
+
+
+def contract(a, b, a_dim, b_dim):
+    return lax.dot_general(a, b, (((a_dim,), (b_dim,)), ((), ())), preferred_element_type=f32)
+
+
+def eye_mask():
+    shape = (BLOCK, BLOCK)
+    return lax.broadcasted_iota(jnp.int32, shape, 0) == lax.broadcasted_iota(jnp.int32, shape, 1)
+
+
+def factor_block(work):
+    work[:, BLOCK:] = eye_mask().astype(f32)
+    tiles = PIVOTS // 8
+    row = lax.broadcasted_iota(jnp.int32, (8, 2 * BLOCK), 0)
+    for group in range(BLOCK // PIVOTS):
+        base = group * PIVOTS
+        rows = [work[base + 8 * h : base + 8 * h + 8, :] for h in range(tiles)]
+        columns = [
+            [
+                jnp.broadcast_to(
+                    work[base + 8 * h : base + 8 * h + 8, base + j : base + j + 1], (8, BLOCK)
+                )
+                for h in range(tiles)
+            ]
+            for j in range(PIVOTS)
+        ]
+        for j in range(PIVOTS):
+            hj, jj = divmod(j, 8)
+            scale = lax.rsqrt(jnp.broadcast_to(columns[j][hj][jj : jj + 1, :], (8, BLOCK)))
+            lower = [columns[j][h] * scale for h in range(hj, tiles)]
+            pivot_row = jnp.broadcast_to(rows[hj][jj : jj + 1, :], (8, 2 * BLOCK)) * jnp.concatenate(
+                [scale, scale], 1
+            )
+            for l in range(j + 1, PIVOTS):
+                entry = jnp.broadcast_to(columns[l][hj][jj : jj + 1, :], (8, BLOCK)) * scale
+                for h in range(hj, tiles):
+                    columns[l][h] = columns[l][h] - lower[h - hj] * entry
+            for h in range(hj, tiles):
+                wide = jnp.concatenate([lower[h - hj], lower[h - hj]], 1)
+                changed = rows[h] - wide * pivot_row
+                if h == hj:
+                    changed = jnp.where(
+                        row > jj, changed, jnp.where(row == jj, pivot_row, rows[h])
+                    )
+                rows[h] = changed
+        done = jnp.concatenate(rows, 0)
+        work[base : base + PIVOTS, :] = done
+        if base + PIVOTS < BLOCK:
+            left, right = both_terms(done, 0)
+            change = contract(left[:, :BLOCK], right, 0, 0)
+            work[base + PIVOTS :, :] = work[base + PIVOTS :, :] - change[base + PIVOTS :, :]
+
+
+def solve_kernel(prior_ref, grads_ref, query_ref, out_ref, gram, extra, work, left_ref, right_ref):
+    size = gram.shape[0]
+    blocks = size // BLOCK
+    part_rows, part_cols = prior_ref.shape[2:]
+    sequences = grads_ref.shape[0]
+    grads = grads_ref[...]
+    on_diagonal = eye_mask()
+
+    def prior_block(i, j):
+        r, c = i * BLOCK, j * BLOCK
+        return prior_ref[
+            r // part_rows,
+            c // part_cols,
+            r % part_rows : r % part_rows + BLOCK,
+            c % part_cols : c % part_cols + BLOCK,
+        ]
+
+    diagonal = jnp.zeros((BLOCK, BLOCK), f32)
+    for i in range(blocks):
+        diagonal = diagonal + jnp.where(on_diagonal, prior_block(i, i), 0.0)
+    trace = jnp.sum(diagonal) + jnp.sum(grads * grads) / sequences
+    damping = damping_ratio * trace / size
+    left, right = both_terms(grads, 0)
+    for i in range(blocks):
+        low = i * BLOCK
+        product = contract(left[:, low : low + BLOCK], right[:, low:], 0, 0) / sequences
+        for j in range(i, blocks):
+            value = prior_block(i, j) + product[:, (j - i) * BLOCK : (j - i + 1) * BLOCK]
+            if i == j:
+                value = value + jnp.where(on_diagonal, damping, 0.0)
+            gram[low : low + BLOCK, j * BLOCK : (j + 1) * BLOCK] = value
+    extra[:sequences, :] = grads
+    extra[sequences:, :] = query_ref[...]
+    scores = jnp.zeros(out_ref.shape, f32)
+    for k in range(blocks):
+        low, high = k * BLOCK, (k + 1) * BLOCK
+        work[:, :BLOCK] = gram[low:high, low:high]
+        factor_block(work)
+        inverse_left, inverse_right = both_terms(work[:, BLOCK:], 1)
+        solved = contract(left_terms(extra[:, low:high], 1), inverse_right, 1, 1)
+        solved_left, solved_right = both_terms(solved, 1)
+        scores = scores + contract(solved_left[sequences:], solved_right[:sequences], 1, 1)
+        if k == blocks - 1:
+            break
+        panel = contract(inverse_left, right_terms(gram[low:high, high:], 0), 1, 0)
+        panel_left, panel_right = both_terms(panel, 0)
+        left_ref[:, high:] = panel_left
+        right_ref[:, high:] = panel_right
+        extra[:, high:] = extra[:, high:] - contract(solved_left, panel_right, 1, 0)
+        for i in range(high, size, BLOCK):
+            gram[i : i + BLOCK, i:] = gram[i : i + BLOCK, i:] - contract(
+                left_ref[:, i : i + BLOCK], right_ref[:, i:], 0, 0
+            )
+    out_ref[...] = scores
+
+
+def solve(prior_parts, grads, queries):
+    size = grads.shape[1]
+    rows = grads.shape[0] + queries.shape[0]
+    return pl.pallas_call(
+        solve_kernel,
+        out_shape=jax.ShapeDtypeStruct((queries.shape[0], grads.shape[0]), f32),
+        scratch_shapes=[
+            pltpu.VMEM((size, size), f32),
+            pltpu.VMEM((rows, size), f32),
+            pltpu.VMEM((BLOCK, 2 * BLOCK), f32),
+            pltpu.VMEM((TERMS * BLOCK, size), jnp.bfloat16),
+            pltpu.VMEM((TERMS * BLOCK, size), jnp.bfloat16),
+        ],
+        compiler_params=pltpu.CompilerParams(vmem_limit_bytes=48 * 2**20),
+        cost_estimate=pl.CostEstimate(
+            flops=4 * size**3, bytes_accessed=4 * size * size, transcendentals=size
+        ),
+    )(prior_parts, grads, queries)
 
 
 def slab_sums(projected, first_row, local_lengths, slab_count):
@@ -46,11 +206,11 @@
     tok_rows = layer_inputs.shape[0]
     slab_count = tok_rows // SEQ_LEN
     sequence_count = slab_sequence.shape[0]
-    contract = (((1,), (1,)), ((), ()))
+    features = (((1,), (1,)), ((), ()))
     projected = jnp.concatenate(
         [
-            lax.dot_general(proj_in, layer_inputs, contract, preferred_element_type=jnp.float32),
-            lax.dot_general(proj_out, output_grads, contract, preferred_element_type=jnp.float32),
+            lax.dot_general(proj_in, layer_inputs, features, preferred_element_type=jnp.float32),
+            lax.dot_general(proj_out, output_grads, features, preferred_element_type=jnp.float32),
         ],
         axis=0,
     )
@@ -66,26 +226,20 @@
         shared, lax.axis_index("width") * shared.shape[1], local_lengths, slab_count
     )
     vectors = lax.psum(partial_value, "width")
-    prior_block = lax.all_gather(prior_gram, "width", axis=1, tiled=True)
-    prior_full = lax.all_gather(prior_block, "tokens", axis=0, tiled=True)
+    prior_block = lax.all_gather(prior_gram, "width", axis=0)
+    prior_parts = lax.all_gather(prior_block, "tokens", axis=0)
+    if prior_gram.shape[1] % BLOCK or prior_gram.shape[0] % BLOCK:
+        prior_parts = prior_parts.transpose(0, 2, 1, 3).reshape(1, 1, K, K)
     all_grads = lax.all_gather(vectors, "tokens", axis=0, tiled=True)
-    gram_total = (
-        prior_full
-        + lax.dot_general(all_grads, all_grads, (((0,), (0,)), ((), ())), precision=highest)
-        / sequence_count
-    )
-    damped = gram_total + damping_ratio * jnp.trace(gram_total) / K * jnp.eye(K, dtype=jnp.float32)
-    factor = jnp.linalg.cholesky(damped)
+    bank_block = solve(prior_parts, all_grads, query_bank)
     column_count = sequence_count // width_count
     column_ids = lax.axis_index("width") * column_count + jnp.arange(column_count, dtype=jnp.int32)
     chooser = (slab_sequence[:, None] == column_ids[None, :]).astype(jnp.float32)
-    chosen = lax.dot_general(chooser, all_grads, (((0,), (0,)), ((), ())), precision=highest)
-    solved = jax.scipy.linalg.cho_solve((factor, True), chosen.T)
+    bank_block = jnp.dot(bank_block, chooser, precision=highest)
     query_count = query_ids.shape[0] // token_count
     local_ids = lax.dynamic_slice_in_dim(
         query_ids, lax.axis_index("tokens") * query_count, query_count
     )
-    bank_block = jnp.dot(query_bank, solved, precision=highest)
     all_scores = lax.all_gather(bank_block, "tokens", axis=0, tiled=True)
     bank_index = jnp.arange(all_scores.shape[0], dtype=jnp.int32)
     onehot = (local_ids[:, None] == bank_index[None, :]).astype(jnp.float32)

time: 475 us -> 146 us (0.31); the launches traced: 469 us -> 146 us
  other arithmetic: 262 us -> 0.95 us
  matrix products: 63.4 us -> 8.65 us
  local copies, waits for them, and re-layouts: 42.2 us -> 3.85 us
  Pallas kernels: 0 us -> 35.9 us
  between operations: 19.4 us -> 13.2 us
    another operation x34 -> x0, other arithmetic: 252 us -> none  [the longest x31 168 us: local(): factor = jnp.linalg.cholesky(damped)]
    another operation x44 -> x0, matrix products: 46.7 us -> none  [the longest x14 26.1 us: local(): factor = jnp.linalg.cholesky(damped)]
    pallas_call x0 -> x1, Pallas kernels: none -> 35.9 us  [solve(): pl.pallas_call(solve_kernel, out_shape=jax.ShapeDtypeStruct((queries.shap...]
    another operation x70 -> x0, local copies, waits for them, and re-layouts: 29.4 us -> none
    dot_general x5 -> x3, matrix products: 15.1 us -> 6.96 us  [the longest x1 5.34 us: local(): lax.dot_general(proj_in, layer_inputs, features, preferred_element_type=j...]
    add x1 -> x0, local copies, waits for them, and re-layouts: 5.62 us -> none  [local(): gram_total + damping_ratio * jnp.trace(gram_total) / K * jnp.eye(K, dtype...]
    add x1 -> x0, other arithmetic: 4.83 us -> none  [local(): gram_total + damping_ratio * jnp.trace(gram_total) / K * jnp.eye(K, dtype...]
  transfers between devices with their start and end apart: 3 -> 3, of which waited for: 3 -> 3; matrix products, arithmetic and copies ran while one was open for 2% -> 7% of each run, Pallas kernels for 0% -> 0%
where the time goes in v1:
time: 146 us
  waiting for transfers between devices  56.9 us (39%)
  Pallas kernels  35.9 us (25%)
  blocking collectives  26.6 us (18%)
  between operations  13.2 us (9%)
  matrix products  8.65 us (6%)
  local copies, waits for them, and re-layouts  3.85 us (3%)
    pallas_call x1, Pallas kernels, solve(): pl.pallas_call(solve_kernel, out_shape=jax.ShapeDtypeStruct((queries.shap...  35.9 us
    all_gather x1, waiting for transfers between devices, local(): prior_block = lax.all_gather(prior_gram, 'width', axis=0)  24.2 us
    reduce_scatter x1, waiting for transfers between devices, local(): lax.psum_scatter(projected, 'width', scatter_dimension=1, tiled=True)  20.5 us
    psum x1, blocking collectives, local(): vectors = lax.psum(partial_value, 'width')  15.9 us
    all_gather x1, waiting for transfers between devices, local(): prior_parts = lax.all_gather(prior_block, 'tokens', axis=0)  11.4 us
    all_gather x1, blocking collectives, local(): all_grads = lax.all_gather(vectors, 'tokens', axis=0, tiled=True)  5.55 us
    dot_general x1, matrix products, local(): lax.dot_general(proj_in, layer_inputs, features, preferred_element_type=j...  5.34 us
    all_gather x1, blocking collectives, local(): all_scores = lax.all_gather(bank_block, 'tokens', axis=0, tiled=True)  5.17 us
  transfers between devices with their start and end apart: 3, of which 3 were waited for; matrix products, arithmetic and copies ran while one was open for 7% of the time, Pallas kernels for 0%

profile of v1, /device:TPU:0, one launch (start us, length us, event | category | flops | bytes accessed | tf_op | source)
XLA Modules:
  0.0 146.1 jit_solution(4088559833274183675)
XLA Ops:
  6.5 0.0 copy-start
  6.5 0.0 all-gather.7.cloned.1.call-start
  6.5 0.7 all-gather.7.cloned.1.call-update
  7.3 0.0 reduce-scatter.2.cloned.1.call-start
  7.3 0.5 copy-done
  7.9 1.4 fusion.12
  9.2 0.0 copy-start.5
  9.2 0.0 copy-start.3
  9.2 0.0 copy-start.4
  9.2 0.0 copy-start.2
  9.3 5.3 %fusion.11 = f32[32,512]{1,0:T(8,128)S(1)} fusion(bf16[32,6912]{1,0:T(8,128)(2,1)} %param.11, bf16[512,6912]{1,0:T(8,128)(2,1)} %param.9), kind=kOutput, calls=%fused_computation.25 | convolution fusion | flops 226492416 | bytes 7585792 | tf_op jit(solution)/shard_map/dot_general | solution.py:212
  14.6 0.7 pad_maximum_fusion
  15.3 0.0 reduce-scatter.2.cloned.1.call-update
  15.3 0.0 all-gather.9.cloned.1.call-start
  15.4 24.2 %all-gather.7.cloned.1.call-done = f32[1024,256]{1,0:T(8,128)} async-done(((f32[256,256]{1,0:T(8,128)}), f32[1024,256]{1,0:T(8,128)}) %all-gather.7.cloned.1.call-update) | async-done | bytes 1048592 | tf_op jit(solution)/shard_map/all_gather | solution.py:229
  39.6 0.0 all-gather.9.cloned.1.call-update
  39.6 0.0 copy-done.5
  39.6 0.1 dynamic_slice.7
  39.7 0.0 copy-done.3
  39.7 0.1 dynamic_slice.6
  39.8 0.0 copy-done.4
  39.8 0.2 select_reduce_fusion
  40.0 0.1 fusion.10
  40.1 20.5 %reduce-scatter.2.cloned.1.call-done = f32[64,128]{1,0:T(8,128)} async-done(((f32[64,512]{1,0:T(8,128)}), f32[64,128]{1,0:T(8,128)}) %reduce-scatter.2.cloned.1.call-update) | async-done | bytes 32784 | tf_op jit(solution)/shard_map/reduce_scatter | solution.py:224
  60.5 0.7 slice.8
  61.3 0.9 fusion
  62.2 0.1 reshape.77
  62.3 15.9 %psum.7 = f32[4,1024]{1,0:T(4,128)S(1)} all-reduce(f32[4,1024]{1,0:T(4,128)S(1)} %reshape.77), channel_id=1, replica_groups=mesh['groups'=2,'width'=4,'tokens'=4] {'width'}, use_global_device_ids=true, to_apply=%region_2.3 | all-reduce | flops 4096 | bytes 32768 | tf_op jit(solution)/shard_map/psum | solution.py:228
  78.2 5.6 %all-gather.2 = f32[4,4,1024]{2,1,0:T(4,128)S(1)} all-gather(f32[1,4,1024]{2,1,0:T(4,128)S(1)} %bitcast.18), channel_id=1, replica_groups=mesh['groups'=2,'width'=4,'tokens'=4] {'tokens'}, dimensions={0}, use_global_device_ids=true | all-gather | bytes 81920 | tf_op jit(solution)/shard_map/all_gather | solution.py:233
  83.8 11.4 %all-gather.9.cloned.1.call-done = f32[16,256,256]{2,1,0:T(8,128)} async-done(((f32[4,256,256]{2,1,0:T(8,128)}), f32[16,256,256]{2,1,0:T(8,128)}) %all-gather.9.cloned.1.call-update) | async-done | bytes 4194320 | tf_op jit(solution)/shard_map/all_gather | solution.py:230
  95.2 0.0 copy-done.2
  95.2 0.0 copy-start.1
  95.2 2.2 %copy-done.1 = f32[16,256,256]{2,1,0:T(8,128)S(1)} copy-done((f32[16,256,256]{2,1,0:T(8,128)S(1)}, f32[16,256,256]{2,1,0:T(8,128)}, u32[]{:S(2)}) %copy-start.1) | copy-done | bytes 4194328
  97.4 35.9 %shard_map.91 = f32[32,16]{1,0:T(8,128)S(1)} custom-call(f32[4,4,256,256]{3,2,1,0:T(8,128)S(1)} %bitcast.16, f32[16,1024]{1,0:T(8,128)S(1)} %reshape.81.grads_ref, f32[32,1024]{1,0:T(8,128)S(1)} %copy-done.2), custom_call_target="tpu_custom_call" | custom-call | flops 4294967296 | bytes 4194304 | tf_op jit(solution)/shard_map/pallas_call | solution.py:158
  133.3 0.3 convolution_bitcast_fusion
  133.5 5.2 %all-gather.3 = f32[4,32,4]{1,2,0:T(4,128)S(1)} all-gather(f32[1,32,4]{1,2,0:T(4,128)S(1)} %convolution_bitcast_fusion), channel_id=1, replica_groups=mesh['groups'=2,'width'=4,'tokens'=4] {'tokens'}, dimensions={0}, use_global_device_ids=true | all-gather | bytes 2560 | tf_op jit(solution)/shard_map/all_gather | solution.py:243
  138.7 0.1 reshape.83
  138.8 0.8 fusion.4
  (4 shorter events, 0.0 us)
Async XLA Ops:
  6.5 1.3 copy-start
  6.5 33.0 %all-gather.7.cloned.1.call-start = ((), (), s32[]{:S(2)}) async-start(), calls=%async_computation.2 | async-start | bytes 1310720 | tf_op jit(solution)/shard_map/all_gather | solution.py:229
  7.3 53.3 %reduce-scatter.2.cloned.1.call-start = ((), (), s32[]{:S(2)}) async-start(), calls=%async_computation.1 | async-start | bytes 163840 | tf_op jit(solution)/shard_map/reduce_scatter | solution.py:224
  9.2 30.4 %copy-start.5 = (s32[16]{0:T(128)S(1)}, s32[16]{0:T(128)}, u32[]{:S(2)}) copy-start(s32[16]{0:T(128)} %param.15) | copy-start | bytes 196
  9.2 30.5 %copy-start.3 = (s32[128]{0:T(128)S(1)}, s32[128]{0:T(128)}, u32[]{:S(2)}) copy-start(s32[128]{0:T(128)} %param.17) | copy-start | bytes 1540
  9.2 30.6 %copy-start.4 = (s32[16]{0:T(128)S(1)}, s32[16]{0:T(128)}, u32[]{:S(2)}) copy-start(s32[16]{0:T(128)} %param.16) | copy-start | bytes 196
  9.2 86.0 %copy-start.2 = (f32[32,1024]{1,0:T(8,128)S(1)}, f32[32,1024]{1,0:T(8,128)}, u32[]{:S(2)}) copy-start(f32[32,1024]{1,0:T(8,128)} %query_ref.1) | copy-start | bytes 393220
  15.3 79.9 %all-gather.9.cloned.1.call-start = ((), (), s32[]{:S(2)}) async-start(), calls=%async_computation.3 | async-start | bytes 5242880 | tf_op jit(solution)/shard_map/all_gather | solution.py:230
  95.2 2.2 %copy-start.1 = (f32[16,256,256]{2,1,0:T(8,128)S(1)}, f32[16,256,256]{2,1,0:T(8,128)}, u32[]{:S(2)}) copy-start(f32[16,256,256]{2,1,0:T(8,128)} %all-gather.9.cloned.1.call-done) | copy-start | bytes 12582916
Sparse Core Ops, SparseCore 0:
  8.9 30.6 all-gather.6
  41.8 18.6 reduce-scatter.1
  62.2 32.9 all-gather.8

commit v2 on v1

--- a/solution.py
+++ b/solution.py
@@ -1,3 +1,5 @@
+import functools
+
 import jax
 import jax.numpy as jnp
 from jax import lax
@@ -96,40 +98,114 @@
             work[base + PIVOTS :, :] = work[base + PIVOTS :, :] - change[base + PIVOTS :, :]
 
 
-def solve_kernel(prior_ref, grads_ref, query_ref, out_ref, gram, extra, work, left_ref, right_ref):
+def half_payload(prior, row_part, col_part):
+    first, second = prior[:BLOCK, :BLOCK], prior[BLOCK:, BLOCK:]
+    upper = eye_mask() | (
+        lax.broadcasted_iota(jnp.int32, (BLOCK, BLOCK), 0)
+        < lax.broadcasted_iota(jnp.int32, (BLOCK, BLOCK), 1)
+    )
+    packed = jnp.concatenate([jnp.where(upper, first, second), prior[:BLOCK, BLOCK:]], 1)
+    half = jnp.where(
+        row_part == col_part,
+        packed,
+        jnp.where(row_part < col_part, prior[:BLOCK, :], prior[:, BLOCK:].T),
+    )
+    diagonal = jnp.sum(jnp.where(eye_mask(), second, 0.0), axis=0)
+    return jnp.concatenate([half, jnp.zeros((8, 2 * BLOCK), f32).at[0, :BLOCK].set(diagonal)], 0)
+
+
+def exchange(value, axis):
+    count = lax.axis_size(axis)
+    return [value] + [
+        lax.ppermute(value, axis, [(i, i ^ s) for i in range(count)]) for s in range(1, count)
+    ]
+
+
+def solve_kernel(halves, ids_ref, *refs):
+    if halves:
+        parts_ref, grads_ref, choose_ref, out_ref = refs[:4]
+        gram, extra, work, left_ref, right_ref, tails, bank, sems = refs[4:]
+    else:
+        prior_ref, bank_ref, grads_ref, choose_ref, out_ref = refs[:5]
+        gram, extra, work, left_ref, right_ref, bank, sems = refs[5:]
     size = gram.shape[0]
     blocks = size // BLOCK
-    part_rows, part_cols = prior_ref.shape[2:]
     sequences = grads_ref.shape[0]
+    bank_chunks, bank_rows, chunk = bank.shape[1:]
+    copies = []
+
+    def start(source, target):
+        copy = pltpu.make_async_copy(source, target, sems.at[len(copies)])
+        copy.start()
+        copies.append(copy)
+
+    if halves:
+        parts = parts_ref.shape[0]
+        span = BLOCK + 8
+        me = lax.axis_index("width")
+        for i in range(parts):
+            for j in range(parts):
+                place = lax.bitwise_xor(me, j) * span
+                low, high = min(i, j), max(i, j)
+                row = 2 * BLOCK * low + (BLOCK if i > j else 0)
+                start(
+                    parts_ref.at[i, pl.ds(place, BLOCK), :],
+                    gram.at[row : row + BLOCK, 2 * BLOCK * high : 2 * BLOCK * (high + 1)],
+                )
+                if i == j:
+                    start(parts_ref.at[i, pl.ds(place + BLOCK, 8), :], tails.at[i])
+            for c in range(bank_chunks):
+                first = parts * span + c * bank_rows
+                start(parts_ref.at[i, first : first + bank_rows, :], bank.at[i, c])
+    else:
+        start(prior_ref, gram)
+        start(bank_ref, bank)
     grads = grads_ref[...]
+    left, right = both_terms(grads, 0)
     on_diagonal = eye_mask()
-
-    def prior_block(i, j):
-        r, c = i * BLOCK, j * BLOCK
-        return prior_ref[
-            r // part_rows,
-            c // part_cols,
-            r % part_rows : r % part_rows + BLOCK,
-            c % part_cols : c % part_cols + BLOCK,
-        ]
-
+    for copy in copies:
+        copy.wait()
+    for q in range(ids_ref.shape[0]):
+        part, row = ids_ref[q] // bank_rows, ids_ref[q] % bank_rows
+        for c in range(bank_chunks):
+            extra[sequences + q : sequences + q + 1, c * chunk : (c + 1) * chunk] = bank[
+                part, c, pl.ds(row, 1), :
+            ]
+    extra[:sequences, :] = grads
     diagonal = jnp.zeros((BLOCK, BLOCK), f32)
-    for i in range(blocks):
-        diagonal = diagonal + jnp.where(on_diagonal, prior_block(i, i), 0.0)
+    if halves:
+        upper = lax.broadcasted_iota(jnp.int32, (BLOCK, BLOCK), 0) <= lax.broadcasted_iota(
+            jnp.int32, (BLOCK, BLOCK), 1
+        )
+        for i in range(parts):
+            low = 2 * BLOCK * i
+            mid, high = low + BLOCK, low + 2 * BLOCK
+            packed = gram[low:mid, low:mid]
+            turned = packed.T
+            gram[low:mid, low:mid] = jnp.where(upper, packed, turned)
+            second = jnp.where(
+                on_diagonal, tails[i, 0:1, :BLOCK], jnp.where(upper, turned, packed)
+            )
+            gram[mid:high, mid:high] = second
+            diagonal = diagonal + jnp.where(on_diagonal, packed + second, 0.0)
+    else:
+        for low in range(0, size, BLOCK):
+            diagonal = diagonal + jnp.where(
+                on_diagonal, gram[low : low + BLOCK, low : low + BLOCK], 0.0
+            )
     trace = jnp.sum(diagonal) + jnp.sum(grads * grads) / sequences
     damping = damping_ratio * trace / size
-    left, right = both_terms(grads, 0)
-    for i in range(blocks):
-        low = i * BLOCK
-        product = contract(left[:, low : low + BLOCK], right[:, low:], 0, 0) / sequences
-        for j in range(i, blocks):
-            value = prior_block(i, j) + product[:, (j - i) * BLOCK : (j - i + 1) * BLOCK]
-            if i == j:
-                value = value + jnp.where(on_diagonal, damping, 0.0)
-            gram[low : low + BLOCK, j * BLOCK : (j + 1) * BLOCK] = value
-    extra[:sequences, :] = grads
-    extra[sequences:, :] = query_ref[...]
-    scores = jnp.zeros(out_ref.shape, f32)
+    for low in range(0, size, BLOCK):
+        high = low + BLOCK
+        product = contract(left[:, low:high], right[:, low:], 0, 0) / sequences
+        gram[low:high, low:high] = (
+            gram[low:high, low:high]
+            + product[:, :BLOCK]
+            + jnp.where(on_diagonal, damping, 0.0)
+        )
+        if high < size:
+            gram[low:high, high:] = gram[low:high, high:] + product[:, BLOCK:]
+    scores = jnp.zeros((ids_ref.shape[0], sequences), f32)
     for k in range(blocks):
         low, high = k * BLOCK, (k + 1) * BLOCK
         work[:, :BLOCK] = gram[low:high, low:high]
@@ -149,45 +225,37 @@
             gram[i : i + BLOCK, i:] = gram[i : i + BLOCK, i:] - contract(
                 left_ref[:, i : i + BLOCK], right_ref[:, i:], 0, 0
             )
-    out_ref[...] = scores
-
-
-def solve(prior_parts, grads, queries):
-    size = grads.shape[1]
-    rows = grads.shape[0] + queries.shape[0]
+    out_ref[...] = jnp.dot(scores, choose_ref[...], precision=highest)
+
+
+def solve(halves, ids, prior_operands, bank_shape, grads, choose):
+    sequences, size = grads.shape
+    rows = sequences + ids.shape[0]
+    copies = 1 + bank_shape[0] * (bank_shape[0] + 1 + bank_shape[1])
+    vmem = pl.BlockSpec(memory_space=pltpu.VMEM)
+    scratch = [
+        pltpu.VMEM((size, size), f32),
+        pltpu.VMEM((rows, size), f32),
+        pltpu.VMEM((BLOCK, 2 * BLOCK), f32),
+        pltpu.VMEM((TERMS * BLOCK, size), jnp.bfloat16),
+        pltpu.VMEM((TERMS * BLOCK, size), jnp.bfloat16),
+    ]
+    if halves:
+        scratch.append(pltpu.VMEM((bank_shape[0], 8, 2 * BLOCK), f32))
     return pl.pallas_call(
-        solve_kernel,
-        out_shape=jax.ShapeDtypeStruct((queries.shape[0], grads.shape[0]), f32),
-        scratch_shapes=[
-            pltpu.VMEM((size, size), f32),
-            pltpu.VMEM((rows, size), f32),
-            pltpu.VMEM((BLOCK, 2 * BLOCK), f32),
-            pltpu.VMEM((TERMS * BLOCK, size), jnp.bfloat16),
-            pltpu.VMEM((TERMS * BLOCK, size), jnp.bfloat16),
-        ],
+        functools.partial(solve_kernel, halves),
+        out_shape=jax.ShapeDtypeStruct((ids.shape[0], choose.shape[1]), f32),
+        in_specs=[pl.BlockSpec(memory_space=pltpu.SMEM)]
+        + [pl.BlockSpec(memory_space=pl.ANY)] * len(prior_operands)
+        + [vmem, vmem],
+        out_specs=vmem,
+        scratch_shapes=scratch
+        + [pltpu.VMEM(bank_shape, f32), pltpu.SemaphoreType.DMA((copies,))],
         compiler_params=pltpu.CompilerParams(vmem_limit_bytes=48 * 2**20),
         cost_estimate=pl.CostEstimate(
             flops=4 * size**3, bytes_accessed=4 * size * size, transcendentals=size
         ),
-    )(prior_parts, grads, queries)
-
-
-def slab_sums(projected, first_row, local_lengths, slab_count):
-    row_count = projected.shape[1]
-    position = first_row + jnp.arange(row_count, dtype=jnp.int32)
-    slab_index = position // SEQ_LEN
-    offset = position - slab_index * SEQ_LEN
-    owners = jnp.arange(slab_count, dtype=jnp.int32)
-    weights = jnp.where(
-        (slab_index[None, :] == owners[:, None]) & (offset[None, :] < local_lengths[:, None]),
-        1.0,
-        0.0,
-    ).astype(jnp.float32)
-    masked = weights[:, None, :] * projected[None, :R_IN, :]
-    products = lax.dot_general(
-        masked, projected[R_IN:, :], (((2,), (1,)), ((), ())), precision=highest
-    )
-    return products.reshape(slab_count, K)
+    )(ids, *prior_operands, grads, choose)
 
 
 def local(
@@ -203,47 +271,55 @@
 ):
     width_count = lax.axis_size("width")
     token_count = lax.axis_size("tokens")
-    tok_rows = layer_inputs.shape[0]
-    slab_count = tok_rows // SEQ_LEN
+    width_index = lax.axis_index("width")
+    token_index = lax.axis_index("tokens")
+    slab_count = layer_inputs.shape[0] // SEQ_LEN
     sequence_count = slab_sequence.shape[0]
+    bank_rows = query_bank.shape[0]
+    halves = prior_gram.shape == (2 * BLOCK, 2 * BLOCK)
+
+    if halves:
+        pieces = exchange(half_payload(prior_gram, token_index, width_index), "width")
+        chunks = query_bank.shape[1] // (2 * BLOCK)
+        pieces += [query_bank[:, c * 2 * BLOCK : (c + 1) * 2 * BLOCK] for c in range(chunks)]
+        prior_operands = (lax.all_gather(jnp.concatenate(pieces, 0), "tokens", axis=0),)
+        bank_shape = (token_count, chunks, bank_rows, 2 * BLOCK)
+    else:
+        prior_block = lax.all_gather(prior_gram, "width", axis=1, tiled=True)
+        prior_full = lax.all_gather(prior_block, "tokens", axis=0, tiled=True)
+        bank_shape = (token_count, 1, bank_rows, query_bank.shape[1])
+        bank_full = lax.all_gather(query_bank, "tokens", axis=0, tiled=True)
+        prior_operands = (prior_full, bank_full.reshape(bank_shape))
+
     features = (((1,), (1,)), ((), ()))
     projected = jnp.concatenate(
         [
-            lax.dot_general(proj_in, layer_inputs, features, preferred_element_type=jnp.float32),
-            lax.dot_general(proj_out, output_grads, features, preferred_element_type=jnp.float32),
+            lax.dot_general(proj_in, layer_inputs, features, preferred_element_type=f32),
+            lax.dot_general(proj_out, output_grads, features, preferred_element_type=f32),
         ],
         axis=0,
     )
-    local_slabs = lax.dynamic_slice_in_dim(
-        slab_sequence, lax.axis_index("tokens") * slab_count, slab_count
-    )
+    total = sum(exchange(projected, "width"))
+    local_slabs = lax.dynamic_slice_in_dim(slab_sequence, token_index * slab_count, slab_count)
     seq_numbers = jnp.arange(sequence_count, dtype=jnp.int32)
     local_lengths = jnp.sum(
         jnp.where(local_slabs[:, None] == seq_numbers[None, :], seq_lengths[None, :], 0), axis=1
     )
-    shared = lax.psum_scatter(projected, "width", scatter_dimension=1, tiled=True)
-    partial_value = slab_sums(
-        shared, lax.axis_index("width") * shared.shape[1], local_lengths, slab_count
-    )
-    vectors = lax.psum(partial_value, "width")
-    prior_block = lax.all_gather(prior_gram, "width", axis=0)
-    prior_parts = lax.all_gather(prior_block, "tokens", axis=0)
-    if prior_gram.shape[1] % BLOCK or prior_gram.shape[0] % BLOCK:
-        prior_parts = prior_parts.transpose(0, 2, 1, 3).reshape(1, 1, K, K)
+    offset = jnp.arange(SEQ_LEN, dtype=jnp.int32)
+    valid = (offset[None, :] < local_lengths[:, None]).reshape(1, -1)
+    total_in = jnp.where(valid, total[:R_IN], 0.0).reshape(R_IN, slab_count, SEQ_LEN)
+    total_out = total[R_IN:].reshape(-1, slab_count, SEQ_LEN)
+    vectors = lax.dot_general(
+        total_in, total_out, (((2,), (2,)), ((1,), (1,))), precision=highest
+    ).reshape(slab_count, K)
     all_grads = lax.all_gather(vectors, "tokens", axis=0, tiled=True)
-    bank_block = solve(prior_parts, all_grads, query_bank)
+
     column_count = sequence_count // width_count
-    column_ids = lax.axis_index("width") * column_count + jnp.arange(column_count, dtype=jnp.int32)
-    chooser = (slab_sequence[:, None] == column_ids[None, :]).astype(jnp.float32)
-    bank_block = jnp.dot(bank_block, chooser, precision=highest)
+    column_ids = width_index * column_count + jnp.arange(column_count, dtype=jnp.int32)
+    choose = (slab_sequence[:, None] == column_ids[None, :]).astype(f32)
     query_count = query_ids.shape[0] // token_count
-    local_ids = lax.dynamic_slice_in_dim(
-        query_ids, lax.axis_index("tokens") * query_count, query_count
-    )
-    all_scores = lax.all_gather(bank_block, "tokens", axis=0, tiled=True)
-    bank_index = jnp.arange(all_scores.shape[0], dtype=jnp.int32)
-    onehot = (local_ids[:, None] == bank_index[None, :]).astype(jnp.float32)
-    return jnp.dot(onehot, all_scores, precision=highest)
+    local_ids = lax.dynamic_slice_in_dim(query_ids, token_index * query_count, query_count)
+    return solve(halves, local_ids, prior_operands, bank_shape, all_grads, choose)
 
 
 def solution(mesh):

time: 146 us -> 104 us (0.71)
  waiting for transfers between devices: 56.9 us -> 21.6 us
  blocking collectives: 26.6 us -> 5.57 us
  starting transfers between devices: 0.08 us -> 10.3 us
  Pallas kernels: 35.9 us -> 38.7 us
  matrix products: 8.65 us -> 5.88 us
  local copies, waits for them, and re-layouts: 3.85 us -> 5.41 us
    all_gather x2 -> x1, waiting for transfers between devices: 35.7 us -> 1.9 us  [local(): lax.all_gather(jnp.concatenate(pieces, 0), 'tokens', axis=0)]
    reduce_scatter x1 -> x0, waiting for transfers between devices: 20.5 us -> none  [local(): lax.psum_scatter(projected, 'width', scatter_dimension=1, tiled=True)]
    ppermute x0 -> x6, waiting for transfers between devices: none -> 19.7 us  [exchange(): lax.ppermute(value, axis, [(i, i ^ s) for i in range(count)])]
    psum x1 -> x0, blocking collectives: 15.9 us -> none  [local(): vectors = lax.psum(partial_value, 'width')]
    ppermute x0 -> x6, starting transfers between devices: none -> 10.3 us  [exchange(): lax.ppermute(value, axis, [(i, i ^ s) for i in range(count)])]
    all_gather x1 -> x0, blocking collectives: 5.17 us -> none  [local(): all_scores = lax.all_gather(bank_block, 'tokens', axis=0, tiled=True)]
    pallas_call x1, Pallas kernels: 35.9 us -> 38.7 us  [solve(): pl.pallas_call(functools.partial(solve_kernel, halves), out_shape=jax.Sha...]
    dot_general x4 -> x2, matrix products: 7.3 us -> 5.41 us  [the longest x1 5.19 us: local(): lax.dot_general(proj_in, layer_inputs, features, preferred_element_type=f32)]
  transfers between devices with their start and end apart: 3 -> 7, of which waited for: 3 -> 5; matrix products, arithmetic and copies ran while one was open for 7% -> 6% of each run, Pallas kernels for 0% -> 0%
where the time goes in v2:
time: 104 us; the launch traced here: 103 us
  Pallas kernels  38.7 us (37%)
  waiting for transfers between devices  21.6 us (21%)
  between operations  13.6 us (13%)
  starting transfers between devices  10.3 us (10%)
  matrix products  5.88 us (6%)
  blocking collectives  5.57 us (5%)
  local copies, waits for them, and re-layouts  5.41 us (5%)
  other arithmetic  2.4 us (2%)
    pallas_call x1, Pallas kernels, solve(): pl.pallas_call(functools.partial(solve_kernel, halves), out_shape=jax.Sha...  38.7 us
    ppermute x6, waiting for transfers between devices, exchange(): lax.ppermute(value, axis, [(i, i ^ s) for i in range(count)])  19.7 us
    ppermute x6, starting transfers between devices, exchange(): lax.ppermute(value, axis, [(i, i ^ s) for i in range(count)])  10.3 us
    all_gather x1, blocking collectives, local(): all_grads = lax.all_gather(vectors, 'tokens', axis=0, tiled=True)  5.57 us
    dot_general x1, matrix products, local(): lax.dot_general(proj_in, layer_inputs, features, preferred_element_type=f32)  5.19 us
    unnamed x27, local copies, waits for them, and re-layouts  3.69 us
  transfers between devices with their start and end apart: 7, of which 5 were waited for; matrix products, arithmetic and copies ran while one was open for 6% of the time, Pallas kernels for 0%

profile of v2, /device:TPU:0, one launch (start us, length us, event | category | flops | bytes accessed | tf_op | source)
XLA Modules:
  0.0 103.5 jit_solution(981573945013757769)
XLA Ops:
  6.5 0.0 copy-start
  6.5 0.0 copy-start.4
  6.5 0.0 copy-start.5
  6.5 0.0 copy-start.3
  6.5 0.0 all-gather.4.cloned.1.call-start
  6.6 1.1 %fusion.2 = (f32[128]{0:T(128)S(1)}, f32[128,128]{1,0:T(8,128)S(1)}, f32[128,128]{1,0:T(8,128)S(1)}) fusion(f32[256,256]{1,0:T(8,128)} %param.15), kind=kLoop, calls=%fused_computation.9 | loop fusion | flops 98176 | bytes 328192 | tf_op jit(solution)/shard_map/reduce_sum | solution.py:113
  7.7 0.9 slice.53
  8.6 0.1 copy.22
  8.7 0.9 constant_dynamic-update-slice_fusion.4
  9.7 3.1 %collective-permute-start = (f32[136,256]{1,0:T(8,128)S(1)}, f32[136,256]{1,0:T(8,128)S(1)}, u32[]{:S(2)}, u32[]{:S(2)}) collective-permute-start(f32[136,256]{1,0:T(8,128)S(1)} %pad_maximum_fusion), channel_id=1, source_target_pairs={{0,4},{4,0},{8,12},{12,8},{1,5},{5,1},{9,13},{13,9},{2,6},{6,2},{1... | collective-permute-start | bytes 417800 | tf_op jit(solution)/shard_map/ppermute | solution.py:120
  12.7 2.6 %collective-permute-start.1 = (f32[136,256]{1,0:T(8,128)S(1)}, f32[136,256]{1,0:T(8,128)S(1)}, u32[]{:S(2)}, u32[]{:S(2)}) collective-permute-start(f32[136,256]{1,0:T(8,128)S(1)} %pad_maximum_fusion), channel_id=1, source_target_pairs={{0,8},{4,12},{8,0},{12,4},{1,9},{5,13},{9,1},{13,5},{2,10},{6,14},... | collective-permute-start | bytes 417800 | tf_op jit(solution)/shard_map/ppermute | solution.py:120
  15.3 0.0 collective-permute-start.2
  15.3 2.9 %collective-permute-done = f32[136,256]{1,0:T(8,128)S(1)} collective-permute-done((f32[136,256]{1,0:T(8,128)S(1)}, f32[136,256]{1,0:T(8,128)S(1)}, u32[]{:S(2)}, u32[]{:S(2)}) %collective-permute-start) | collective-permute-done | bytes 139296 | tf_op jit(solution)/shard_map/ppermute | solution.py:120
  18.2 8.0 %collective-permute-done.1 = f32[136,256]{1,0:T(8,128)S(1)} collective-permute-done((f32[136,256]{1,0:T(8,128)S(1)}, f32[136,256]{1,0:T(8,128)S(1)}, u32[]{:S(2)}, u32[]{:S(2)}) %collective-permute-start.1) | collective-permute-done | bytes 139296 | tf_op jit(solution)/shard_map/ppermute | solution.py:120
  26.2 0.0 collective-permute-done.2
  26.3 0.8 slice_dynamic-update-slice_fusion.3
  27.0 0.0 copy-done.4
  27.1 0.0 copy-start.2
  27.1 0.8 copy-done.2
  27.9 0.0 all-gather.4.cloned.1.call-update
  27.9 0.0 copy-done
  27.9 0.0 copy-done.5
  28.0 0.5 fusion.12
  28.4 0.0 copy-done.3
  28.4 0.0 copy-start.6
  28.5 0.0 copy-start.7
  28.5 0.0 copy-start.8
  28.5 5.2 %fusion.11 = f32[32,512]{1,0:T(8,128)S(1)} fusion(bf16[32,6912]{1,0:T(8,128)(2,1)S(1)} %copy-done.3, bf16[512,6912]{1,0:T(8,128)(2,1)} %param.11), kind=kOutput, calls=%fused_computation.35 | convolution fusion | flops 226492416 | bytes 7585792 | tf_op jit(solution)/shard_map/dot_general | solution.py:297
  33.7 2.2 %collective-permute-start.3 = (f32[64,512]{1,0:T(8,128)S(1)}, f32[64,512]{1,0:T(8,128)S(1)}, u32[]{:S(2)}, u32[]{:S(2)}) collective-permute-start(f32[64,512]{1,0:T(8,128)S(1)} %pad_maximum_fusion.1), channel_id=1, source_target_pairs={{0,4},{4,0},{8,12},{12,8},{1,5},{5,1},{9,13},{13,9},{2,6},{6,2},{1... | collective-permute-start | bytes 393224 | tf_op jit(solution)/shard_map/ppermute | solution.py:120
  35.8 1.1 %collective-permute-start.4 = (f32[64,512]{1,0:T(8,128)S(1)}, f32[64,512]{1,0:T(8,128)S(1)}, u32[]{:S(2)}, u32[]{:S(2)}) collective-permute-start(f32[64,512]{1,0:T(8,128)S(1)} %pad_maximum_fusion.1), channel_id=1, source_target_pairs={{0,8},{4,12},{8,0},{12,4},{1,9},{5,13},{9,1},{13,5},{2,10},{6,14},... | collective-permute-start | bytes 393224 | tf_op jit(solution)/shard_map/ppermute | solution.py:120
  36.9 1.4 %collective-permute-start.5 = (f32[64,512]{1,0:T(8,128)S(1)}, f32[64,512]{1,0:T(8,128)S(1)}, u32[]{:S(2)}, u32[]{:S(2)}) collective-permute-start(f32[64,512]{1,0:T(8,128)S(1)} %pad_maximum_fusion.1), channel_id=1, source_target_pairs={{0,12},{4,8},{8,4},{12,0},{1,13},{5,9},{9,5},{13,1},{2,14},{6,10},... | collective-permute-start | bytes 393224 | tf_op jit(solution)/shard_map/ppermute | solution.py:120
  38.3 0.0 copy-done.6
  38.3 0.1 dynamic_slice.7
  38.4 0.0 copy-done.7
  38.4 0.1 dynamic_slice.6.ids_ref
  38.5 0.0 copy-done.8
  38.5 0.2 select_reduce_fusion
  38.7 0.1 compare_convert_fusion.refs_2_
  38.7 0.1 fusion.9
  38.8 1.4 %collective-permute-done.3 = f32[64,512]{1,0:T(8,128)S(1)} collective-permute-done((f32[64,512]{1,0:T(8,128)S(1)}, f32[64,512]{1,0:T(8,128)S(1)}, u32[]{:S(2)}, u32[]{:S(2)}) %collective-permute-start.3) | collective-permute-done | bytes 131104 | tf_op jit(solution)/shard_map/ppermute | solution.py:120
  40.2 7.4 %collective-permute-done.4 = f32[64,512]{1,0:T(8,128)S(1)} collective-permute-done((f32[64,512]{1,0:T(8,128)S(1)}, f32[64,512]{1,0:T(8,128)S(1)}, u32[]{:S(2)}, u32[]{:S(2)}) %collective-permute-start.4) | collective-permute-done | bytes 131104 | tf_op jit(solution)/shard_map/ppermute | solution.py:120
  47.6 0.0 collective-permute-done.5
  47.7 0.2 fusion.3
  47.9 0.1 reshape.67
  48.0 5.6 %all-gather.1 = f32[4,4,1024]{2,1,0:T(4,128)S(1)} all-gather(f32[1,4,1024]{2,1,0:T(4,128)S(1)} %reshape.67), channel_id=1, replica_groups=mesh['groups'=2,'width'=4,'tokens'=4] {'tokens'}, dimensions={0}, use_global_device_ids=true | all-gather | bytes 81920 | tf_op jit(solution)/shard_map/all_gather | solution.py:315
  53.6 1.9 %all-gather.4.cloned.1.call-done = f32[2688,256]{1,0:T(8,128)} async-done(((f32[672,256]{1,0:T(8,128)}), f32[2688,256]{1,0:T(8,128)}) %all-gather.4.cloned.1.call-update) | async-done | bytes 2752528 | tf_op jit(solution)/shard_map/all_gather | solution.py:285
  55.5 0.0 copy-start.1
  55.5 1.8 %copy-done.1 = f32[2688,256]{1,0:T(8,128)S(1)} copy-done((f32[2688,256]{1,0:T(8,128)S(1)}, f32[2688,256]{1,0:T(8,128)}, u32[]{:S(2)}) %copy-start.1) | copy-done | bytes 2752536
  57.3 38.7 %shard_map.91 = f32[32,4]{1,0:T(8,128)S(1)} custom-call(s32[32]{0:T(128)S(1)} %dynamic_slice.6.ids_ref, f32[4,672,256]{2,1,0:T(8,128)S(1)} %bitcast.23, f32[16,1024]{1,0:T(8,128)S(1)} %reshape.68.refs_1_, f32[16,4]{1,0:T(8,128)S(1)} %compare_convert_fusion.refs_2_), custom_call_target="tpu_custom_call" | custom-call | flops 4294967296 | bytes 4194304 | tf_op jit(solution)/shard_map/pallas_call | solution.py:245
  96.0 0.7 copy.21
  (13 shorter events, 0.1 us)
Async XLA Ops:
  6.5 21.4 %copy-start = (bf16[512,1280]{1,0:T(8,128)(2,1)S(1)}, bf16[512,1280]{1,0:T(8,128)(2,1)}, u32[]{:S(2)}) copy-start(bf16[512,1280]{1,0:T(8,128)(2,1)} %param.12) | copy-start | bytes 3932164
  6.5 20.5 %copy-start.4 = (f32[32,1024]{1,0:T(8,128)S(1)}, f32[32,1024]{1,0:T(8,128)}, u32[]{:S(2)}) copy-start(f32[32,1024]{1,0:T(8,128)} %param.16) | copy-start | bytes 393220
  6.5 21.4 %copy-start.5 = (bf16[32,1280]{1,0:T(8,128)(2,1)S(1)}, bf16[32,1280]{1,0:T(8,128)(2,1)}, u32[]{:S(2)}) copy-start(bf16[32,1280]{1,0:T(8,128)(2,1)} %param.14) | copy-start | bytes 245764
  6.5 21.9 %copy-start.3 = (bf16[32,6912]{1,0:T(8,128)(2,1)S(1)}, bf16[32,6912]{1,0:T(8,128)(2,1)}, u32[]{:S(2)}) copy-start(bf16[32,6912]{1,0:T(8,128)(2,1)} %param.13) | copy-start | bytes 1327108
  6.5 49.0 %all-gather.4.cloned.1.call-start = ((), (), s32[]{:S(2)}) async-start(), calls=%async_computation | async-start | bytes 3440640 | tf_op jit(solution)/shard_map/all_gather | solution.py:285
  9.7 8.5 %collective-permute-start = (f32[136,256]{1,0:T(8,128)S(1)}, f32[136,256]{1,0:T(8,128)S(1)}, u32[]{:S(2)}, u32[]{:S(2)}) collective-permute-start(f32[136,256]{1,0:T(8,128)S(1)} %pad_maximum_fusion), channel_id=1, source_target_pairs={{0,4},{4,0},{8,12},{12,8},{1,5},{5,1},{9,13},{13,9},{2,6},{6,2},{1... | collective-permute-start | bytes 417800 | tf_op jit(solution)/shard_map/ppermute | solution.py:120
  12.7 13.5 %collective-permute-start.1 = (f32[136,256]{1,0:T(8,128)S(1)}, f32[136,256]{1,0:T(8,128)S(1)}, u32[]{:S(2)}, u32[]{:S(2)}) collective-permute-start(f32[136,256]{1,0:T(8,128)S(1)} %pad_maximum_fusion), channel_id=1, source_target_pairs={{0,8},{4,12},{8,0},{12,4},{1,9},{5,13},{9,1},{13,5},{2,10},{6,14},... | collective-permute-start | bytes 417800 | tf_op jit(solution)/shard_map/ppermute | solution.py:120
  15.3 10.9 %collective-permute-start.2 = (f32[136,256]{1,0:T(8,128)S(1)}, f32[136,256]{1,0:T(8,128)S(1)}, u32[]{:S(2)}, u32[]{:S(2)}) collective-permute-start(f32[136,256]{1,0:T(8,128)S(1)} %pad_maximum_fusion), channel_id=1, source_target_pairs={{0,12},{4,8},{8,4},{12,0},{1,13},{5,9},{9,5},{13,1},{2,14},{6,10},... | collective-permute-start | bytes 417800 | tf_op jit(solution)/shard_map/ppermute | solution.py:120
  27.1 0.9 copy-start.2
  28.4 9.9 %copy-start.6 = (s32[16]{0:T(128)S(1)}, s32[16]{0:T(128)}, u32[]{:S(2)}) copy-start(s32[16]{0:T(128)} %param.17) | copy-start | bytes 196
  28.5 9.9 %copy-start.7 = (s32[128]{0:T(128)S(1)}, s32[128]{0:T(128)}, u32[]{:S(2)}) copy-start(s32[128]{0:T(128)} %param.19) | copy-start | bytes 1540
  28.5 10.0 %copy-start.8 = (s32[16]{0:T(128)S(1)}, s32[16]{0:T(128)}, u32[]{:S(2)}) copy-start(s32[16]{0:T(128)} %param.18) | copy-start | bytes 196
  33.7 6.5 %collective-permute-start.3 = (f32[64,512]{1,0:T(8,128)S(1)}, f32[64,512]{1,0:T(8,128)S(1)}, u32[]{:S(2)}, u32[]{:S(2)}) collective-permute-start(f32[64,512]{1,0:T(8,128)S(1)} %pad_maximum_fusion.1), channel_id=1, source_target_pairs={{0,4},{4,0},{8,12},{12,8},{1,5},{5,1},{9,13},{13,9},{2,6},{6,2},{1... | collective-permute-start | bytes 393224 | tf_op jit(solution)/shard_map/ppermute | solution.py:120
  35.8 11.8 %collective-permute-start.4 = (f32[64,512]{1,0:T(8,128)S(1)}, f32[64,512]{1,0:T(8,128)S(1)}, u32[]{:S(2)}, u32[]{:S(2)}) collective-permute-start(f32[64,512]{1,0:T(8,128)S(1)} %pad_maximum_fusion.1), channel_id=1, source_target_pairs={{0,8},{4,12},{8,0},{12,4},{1,9},{5,13},{9,1},{13,5},{2,10},{6,14},... | collective-permute-start | bytes 393224 | tf_op jit(solution)/shard_map/ppermute | solution.py:120
  36.9 10.7 %collective-permute-start.5 = (f32[64,512]{1,0:T(8,128)S(1)}, f32[64,512]{1,0:T(8,128)S(1)}, u32[]{:S(2)}, u32[]{:S(2)}) collective-permute-start(f32[64,512]{1,0:T(8,128)S(1)} %pad_maximum_fusion.1), channel_id=1, source_target_pairs={{0,12},{4,8},{8,4},{12,0},{1,13},{5,9},{9,5},{13,1},{2,14},{6,10},... | collective-permute-start | bytes 393224 | tf_op jit(solution)/shard_map/ppermute | solution.py:120
  55.5 1.8 %copy-start.1 = (f32[2688,256]{1,0:T(8,128)S(1)}, f32[2688,256]{1,0:T(8,128)}, u32[]{:S(2)}) copy-start(f32[2688,256]{1,0:T(8,128)} %all-gather.4.cloned.1.call-done) | copy-start | bytes 8257540
Sparse Core Ops, SparseCore 0:
  28.1 27.3 all-gather.3

commit v3 on v2

--- a/solution.py
+++ b/solution.py
@@ -98,20 +98,57 @@
             work[base + PIVOTS :, :] = work[base + PIVOTS :, :] - change[base + PIVOTS :, :]
 
 
-def half_payload(prior, row_part, col_part):
-    first, second = prior[:BLOCK, :BLOCK], prior[BLOCK:, BLOCK:]
-    upper = eye_mask() | (
-        lax.broadcasted_iota(jnp.int32, (BLOCK, BLOCK), 0)
-        < lax.broadcasted_iota(jnp.int32, (BLOCK, BLOCK), 1)
-    )
-    packed = jnp.concatenate([jnp.where(upper, first, second), prior[:BLOCK, BLOCK:]], 1)
-    half = jnp.where(
-        row_part == col_part,
-        packed,
-        jnp.where(row_part < col_part, prior[:BLOCK, :], prior[:, BLOCK:].T),
-    )
-    diagonal = jnp.sum(jnp.where(eye_mask(), second, 0.0), axis=0)
-    return jnp.concatenate([half, jnp.zeros((8, 2 * BLOCK), f32).at[0, :BLOCK].set(diagonal)], 0)
+def pack_kernel(prior_ref, bank_ref, half_ref, first_ref):
+    row_part, col_part = lax.axis_index("tokens"), lax.axis_index("width")
+    on_diagonal = eye_mask()
+
+    def put(rows, columns, value):
+        half_ref[rows, columns] = value
+        first_ref[rows, columns] = value
+
+    top, left, right = slice(0, BLOCK), slice(0, BLOCK), slice(BLOCK, 2 * BLOCK)
+
+    @pl.when(row_part == col_part)
+    def _():
+        shape = (BLOCK, BLOCK)
+        upper = lax.broadcasted_iota(jnp.int32, shape, 0) <= lax.broadcasted_iota(
+            jnp.int32, shape, 1
+        )
+        put(top, left, jnp.where(upper, prior_ref[:BLOCK, :BLOCK], prior_ref[BLOCK:, BLOCK:]))
+        put(top, right, prior_ref[:BLOCK, BLOCK:])
+
+    @pl.when(row_part < col_part)
+    def _():
+        put(top, slice(None), prior_ref[:BLOCK, :])
+
+    @pl.when(row_part > col_part)
+    def _():
+        put(top, left, prior_ref[:BLOCK, BLOCK:].T)
+        put(top, right, prior_ref[BLOCK:, BLOCK:].T)
+
+    diagonal = jnp.sum(jnp.where(on_diagonal, prior_ref[BLOCK:, BLOCK:], 0.0), axis=0, keepdims=True)
+    tail = slice(BLOCK, BLOCK + 8)
+    put(tail, left, jnp.broadcast_to(diagonal, (8, BLOCK)))
+    put(tail, right, jnp.zeros((8, BLOCK), f32))
+    bank_rows = bank_ref.shape[0]
+    for c in range(bank_ref.shape[1] // (2 * BLOCK)):
+        low = BLOCK + 8 + c * bank_rows
+        first_ref[low : low + bank_rows, :] = bank_ref[:, c * 2 * BLOCK : (c + 1) * 2 * BLOCK]
+
+
+def pack(prior, bank):
+    span = BLOCK + 8
+    rows = span + bank.size // (2 * BLOCK)
+    vmem = pl.BlockSpec(memory_space=pltpu.VMEM)
+    return pl.pallas_call(
+        pack_kernel,
+        out_shape=(
+            jax.ShapeDtypeStruct((span, 2 * BLOCK), f32),
+            jax.ShapeDtypeStruct((rows, 2 * BLOCK), f32),
+        ),
+        in_specs=[vmem, vmem],
+        out_specs=(vmem, vmem),
+    )(prior, bank)
 
 
 def exchange(value, axis):
@@ -123,8 +160,8 @@
 
 def solve_kernel(halves, ids_ref, *refs):
     if halves:
-        parts_ref, grads_ref, choose_ref, out_ref = refs[:4]
-        gram, extra, work, left_ref, right_ref, tails, bank, sems = refs[4:]
+        own_ref, others_ref, grads_ref, choose_ref, out_ref = refs[:5]
+        gram, extra, work, left_ref, right_ref, tails, bank, sems = refs[5:]
     else:
         prior_ref, bank_ref, grads_ref, choose_ref, out_ref = refs[:5]
         gram, extra, work, left_ref, right_ref, bank, sems = refs[5:]
@@ -140,23 +177,25 @@
         copies.append(copy)
 
     if halves:
-        parts = parts_ref.shape[0]
+        parts = own_ref.shape[0]
         span = BLOCK + 8
         me = lax.axis_index("width")
+        for s in range(parts):
+            j = lax.bitwise_xor(me, s)
+            source, place = (own_ref, 0) if s == 0 else (others_ref, (s - 1) * span)
+            for i in range(parts):
+                row = 2 * BLOCK * lax.min(i, j) + jnp.where(i > j, BLOCK, 0)
+                row = pl.multiple_of(row, BLOCK)
+                column = pl.multiple_of(2 * BLOCK * lax.max(i, j), BLOCK)
+                start(
+                    source.at[i, place : place + BLOCK, :],
+                    gram.at[pl.ds(row, BLOCK), pl.ds(column, 2 * BLOCK)],
+                )
+                start(source.at[i, place + BLOCK : place + span, :], tails.at[i, j])
         for i in range(parts):
-            for j in range(parts):
-                place = lax.bitwise_xor(me, j) * span
-                low, high = min(i, j), max(i, j)
-                row = 2 * BLOCK * low + (BLOCK if i > j else 0)
-                start(
-                    parts_ref.at[i, pl.ds(place, BLOCK), :],
-                    gram.at[row : row + BLOCK, 2 * BLOCK * high : 2 * BLOCK * (high + 1)],
-                )
-                if i == j:
-                    start(parts_ref.at[i, pl.ds(place + BLOCK, 8), :], tails.at[i])
             for c in range(bank_chunks):
-                first = parts * span + c * bank_rows
-                start(parts_ref.at[i, first : first + bank_rows, :], bank.at[i, c])
+                first = span + c * bank_rows
+                start(own_ref.at[i, first : first + bank_rows, :], bank.at[i, c])
     else:
         start(prior_ref, gram)
         start(bank_ref, bank)
@@ -184,7 +223,7 @@
             turned = packed.T
             gram[low:mid, low:mid] = jnp.where(upper, packed, turned)
             second = jnp.where(
-                on_diagonal, tails[i, 0:1, :BLOCK], jnp.where(upper, turned, packed)
+                on_diagonal, tails[i, i, 0:1, :BLOCK], jnp.where(upper, turned, packed)
             )
             gram[mid:high, mid:high] = second
             diagonal = diagonal + jnp.where(on_diagonal, packed + second, 0.0)
@@ -225,13 +264,15 @@
             gram[i : i + BLOCK, i:] = gram[i : i + BLOCK, i:] - contract(
                 left_ref[:, i : i + BLOCK], right_ref[:, i:], 0, 0
             )
-    out_ref[...] = jnp.dot(scores, choose_ref[...], precision=highest)
+    out_ref[...] = lax.dot_general(
+        choose_ref[...], scores, (((1,), (1,)), ((), ())), precision=highest
+    )
 
 
 def solve(halves, ids, prior_operands, bank_shape, grads, choose):
     sequences, size = grads.shape
     rows = sequences + ids.shape[0]
-    copies = 1 + bank_shape[0] * (bank_shape[0] + 1 + bank_shape[1])
+    copies = 2 + bank_shape[0] * (2 * bank_shape[0] + bank_shape[1])
     vmem = pl.BlockSpec(memory_space=pltpu.VMEM)
     scratch = [
         pltpu.VMEM((size, size), f32),
@@ -241,17 +282,17 @@
         pltpu.VMEM((TERMS * BLOCK, size), jnp.bfloat16),
     ]
     if halves:
-        scratch.append(pltpu.VMEM((bank_shape[0], 8, 2 * BLOCK), f32))
+        scratch.append(pltpu.VMEM((bank_shape[0], bank_shape[0], 8, 2 * BLOCK), f32))
     return pl.pallas_call(
         functools.partial(solve_kernel, halves),
-        out_shape=jax.ShapeDtypeStruct((ids.shape[0], choose.shape[1]), f32),
+        out_shape=jax.ShapeDtypeStruct((choose.shape[0], ids.shape[0]), f32),
         in_specs=[pl.BlockSpec(memory_space=pltpu.SMEM)]
         + [pl.BlockSpec(memory_space=pl.ANY)] * len(prior_operands)
         + [vmem, vmem],
         out_specs=vmem,
         scratch_shapes=scratch
         + [pltpu.VMEM(bank_shape, f32), pltpu.SemaphoreType.DMA((copies,))],
-        compiler_params=pltpu.CompilerParams(vmem_limit_bytes=48 * 2**20),
+        compiler_params=pltpu.CompilerParams(vmem_limit_bytes=60 * 2**20),
         cost_estimate=pl.CostEstimate(
             flops=4 * size**3, bytes_accessed=4 * size * size, transcendentals=size
         ),
@@ -279,11 +320,10 @@
     halves = prior_gram.shape == (2 * BLOCK, 2 * BLOCK)
 
     if halves:
-        pieces = exchange(half_payload(prior_gram, token_index, width_index), "width")
-        chunks = query_bank.shape[1] // (2 * BLOCK)
-        pieces += [query_bank[:, c * 2 * BLOCK : (c + 1) * 2 * BLOCK] for c in range(chunks)]
-        prior_operands = (lax.all_gather(jnp.concatenate(pieces, 0), "tokens", axis=0),)
-        bank_shape = (token_count, chunks, bank_rows, 2 * BLOCK)
+        half, first = pack(prior_gram, query_bank)
+        own = lax.all_gather(first, "tokens", axis=0)
+        pieces = exchange(half, "width")[1:]
+        bank_shape = (token_count, query_bank.shape[1] // (2 * BLOCK), bank_rows, 2 * BLOCK)
     else:
         prior_block = lax.all_gather(prior_gram, "width", axis=1, tiled=True)
         prior_full = lax.all_gather(prior_block, "tokens", axis=0, tiled=True)
@@ -299,6 +339,10 @@
         ],
         axis=0,
     )
+    if halves:
+        projected, pieces = lax.optimization_barrier((projected, pieces))
+        others = lax.all_gather(jnp.concatenate(pieces, 0), "tokens", axis=0)
+        prior_operands = (own, others)
     total = sum(exchange(projected, "width"))
     local_slabs = lax.dynamic_slice_in_dim(slab_sequence, token_index * slab_count, slab_count)
     seq_numbers = jnp.arange(sequence_count, dtype=jnp.int32)
@@ -316,10 +360,10 @@
 
     column_count = sequence_count // width_count
     column_ids = width_index * column_count + jnp.arange(column_count, dtype=jnp.int32)
-    choose = (slab_sequence[:, None] == column_ids[None, :]).astype(f32)
+    choose = (column_ids[:, None] == slab_sequence[None, :]).astype(f32)
     query_count = query_ids.shape[0] // token_count
     local_ids = lax.dynamic_slice_in_dim(query_ids, token_index * query_count, query_count)
-    return solve(halves, local_ids, prior_operands, bank_shape, all_grads, choose)
+    return solve(halves, local_ids, prior_operands, bank_shape, all_grads, choose).T
 
 
 def solution(mesh):

time: 104 us -> 98.2 us (0.944)
  waiting for transfers between devices: 21.6 us -> 17.1 us
  local copies, waits for them, and re-layouts: 5.41 us -> 1.43 us
  Pallas kernels: 38.7 us -> 42.2 us
    ppermute x6, waiting for transfers between devices: 19.7 us -> 14.6 us  [exchange(): lax.ppermute(value, axis, [(i, i ^ s) for i in range(count)])]
    unnamed x27 -> x12, local copies, waits for them, and re-layouts: 3.69 us -> 0.77 us
    pallas_call x0 -> x1, Pallas kernels: none -> 1.9 us  [pack(): pl.pallas_call(pack_kernel, out_shape=(jax.ShapeDtypeStruct((span, 2 * BL...]
    pallas_call x1, Pallas kernels: 38.7 us -> 40.3 us  [solve(): pl.pallas_call(functools.partial(solve_kernel, halves), out_shape=jax.Sha...]
    reduce_sum x1 -> x0, other arithmetic: 1.07 us -> none  [half_payload(): diagonal = jnp.sum(jnp.where(eye_mask(), second, 0.0), axis=0)]
    all_gather x1 -> x2, waiting for transfers between devices: 1.9 us -> 2.51 us  [the longest x1 2.51 us: local(): others = lax.all_gather(jnp.concatenate(pieces, 0), 'tokens', axis=0)]
  transfers between devices with their start and end apart: 7 -> 8, of which waited for: 5 -> 4; matrix products, arithmetic and copies ran while one was open for 6% -> 9% of each run, Pallas kernels for 0% -> 0%
where the time goes in v3:
time: 98.2 us; the launch traced here: 97.9 us
  Pallas kernels  42.2 us (43%)
  waiting for transfers between devices  17.1 us (17%)
  between operations  13.5 us (14%)
  starting transfers between devices  10.3 us (10%)
  matrix products  5.99 us (6%)
  blocking collectives  5.56 us (6%)
  other arithmetic  1.8 us (2%)
  local copies, waits for them, and re-layouts  1.43 us (1%)
    pallas_call x1, Pallas kernels, solve(): pl.pallas_call(functools.partial(solve_kernel, halves), out_shape=jax.Sha...  40.3 us
    ppermute x6, waiting for transfers between devices, exchange(): lax.ppermute(value, axis, [(i, i ^ s) for i in range(count)])  14.6 us
    ppermute x6, starting transfers between devices, exchange(): lax.ppermute(value, axis, [(i, i ^ s) for i in range(count)])  10.3 us
    all_gather x1, blocking collectives, local(): all_grads = lax.all_gather(vectors, 'tokens', axis=0, tiled=True)  5.56 us
    dot_general x1, matrix products, local(): lax.dot_general(proj_in, layer_inputs, features, preferred_element_type=f32)  5.3 us
    all_gather x1, waiting for transfers between devices, local(): others = lax.all_gather(jnp.concatenate(pieces, 0), 'tokens', axis=0)  2.51 us
  transfers between devices with their start and end apart: 8, of which 4 were waited for; matrix products, arithmetic and copies ran while one was open for 9% of the time, Pallas kernels for 0%

profile of v3, /device:TPU:0, one launch (start us, length us, event | category | flops | bytes accessed | tf_op | source)
XLA Modules:
  0.0 97.9 jit_solution(4614832335110139113)
XLA Ops:
  6.5 0.0 copy-start
  6.5 0.0 all-gather.6.cloned.1.call-start
  6.5 1.9 %shard_map.91 = (f32[136,256]{1,0:T(8,128)}, f32[264,256]{1,0:T(8,128)}) custom-call(f32[256,256]{1,0:T(8,128)} %prior_ref.1, f32[32,1024]{1,0:T(8,128)} %bank_ref.1), custom_call_target="tpu_custom_call" | custom-call | tf_op jit(solution)/shard_map/pallas_call | solution.py:143
  8.4 0.0 all-gather.6.cloned.1.call-update
  8.5 0.0 all-gather.8.cloned.1.call-start
  8.5 0.0 copy-start.1
  8.5 3.1 %collective-permute-start = (f32[136,256]{1,0:T(8,128)}, f32[136,256]{1,0:T(8,128)S(1)}, u32[]{:S(2)}, u32[]{:S(2)}) collective-permute-start(f32[136,256]{1,0:T(8,128)} %get-tuple-element.12), channel_id=1, source_target_pairs={{0,4},{4,0},{8,12},{12,8},{1,5},{5,1},{9,13},{13,9},{2,6},{6,2},{1... | collective-permute-start | bytes 417800 | tf_op jit(solution)/shard_map/ppermute | solution.py:157
  11.6 2.6 %collective-permute-start.1 = (f32[136,256]{1,0:T(8,128)}, f32[136,256]{1,0:T(8,128)S(1)}, u32[]{:S(2)}, u32[]{:S(2)}) collective-permute-start(f32[136,256]{1,0:T(8,128)} %get-tuple-element.12), channel_id=1, source_target_pairs={{0,8},{4,12},{8,0},{12,4},{1,9},{5,13},{9,1},{13,5},{2,10},{6,14},... | collective-permute-start | bytes 417800 | tf_op jit(solution)/shard_map/ppermute | solution.py:157
  14.2 0.0 collective-permute-start.2
  14.2 5.3 %fusion.7 = f32[32,512]{1,0:T(8,128)S(1)} fusion(bf16[32,6912]{1,0:T(8,128)(2,1)} %param.11, bf16[512,6912]{1,0:T(8,128)(2,1)} %param.9), kind=kOutput, calls=%fused_computation.17 | convolution fusion | flops 226492416 | bytes 7585792 | tf_op jit(solution)/shard_map/dot_general | solution.py:337
  19.5 0.0 copy-done
  19.5 0.0 copy-done.1
  19.5 0.0 copy-start.2
  19.6 0.0 copy-start.3
  19.6 0.0 copy-start.4
  19.6 0.5 fusion.8
  20.1 0.0 collective-permute-done
  20.1 5.2 %collective-permute-done.1 = f32[136,256]{1,0:T(8,128)S(1)} collective-permute-done((f32[136,256]{1,0:T(8,128)}, f32[136,256]{1,0:T(8,128)S(1)}, u32[]{:S(2)}, u32[]{:S(2)}) %collective-permute-start.1) | collective-permute-done | bytes 139296 | tf_op jit(solution)/shard_map/ppermute | solution.py:157
  25.3 0.0 collective-permute-done.2
  25.3 0.8 pad_maximum_fusion
  26.1 0.0 all-gather.8.cloned.1.call-update
  26.1 0.0 copy-done.2
  26.1 0.1 dynamic_slice.7
  26.2 0.0 copy-done.3
  26.2 0.6 dynamic_slice.6.ids_ref
  26.8 0.0 copy-done.4
  26.8 0.2 select_reduce_fusion
  27.0 0.7 compare_convert_fusion.refs_3_
  27.7 2.1 %collective-permute-start.3 = (f32[64,512]{1,0:T(8,128)S(1)}, f32[64,512]{1,0:T(8,128)S(1)}, u32[]{:S(2)}, u32[]{:S(2)}) collective-permute-start(f32[64,512]{1,0:T(8,128)S(1)} %pad_maximum_fusion.1), channel_id=1, source_target_pairs={{0,4},{4,0},{8,12},{12,8},{1,5},{5,1},{9,13},{13,9},{2,6},{6,2},{1... | collective-permute-start | bytes 393224 | tf_op jit(solution)/shard_map/ppermute | solution.py:157
  29.8 1.0 %collective-permute-start.4 = (f32[64,512]{1,0:T(8,128)S(1)}, f32[64,512]{1,0:T(8,128)S(1)}, u32[]{:S(2)}, u32[]{:S(2)}) collective-permute-start(f32[64,512]{1,0:T(8,128)S(1)} %pad_maximum_fusion.1), channel_id=1, source_target_pairs={{0,8},{4,12},{8,0},{12,4},{1,9},{5,13},{9,1},{13,5},{2,10},{6,14},... | collective-permute-start | bytes 393224 | tf_op jit(solution)/shard_map/ppermute | solution.py:157
  30.8 1.5 %collective-permute-start.5 = (f32[64,512]{1,0:T(8,128)S(1)}, f32[64,512]{1,0:T(8,128)S(1)}, u32[]{:S(2)}, u32[]{:S(2)}) collective-permute-start(f32[64,512]{1,0:T(8,128)S(1)} %pad_maximum_fusion.1), channel_id=1, source_target_pairs={{0,12},{4,8},{8,4},{12,0},{1,13},{5,9},{9,5},{13,1},{2,14},{6,10},... | collective-permute-start | bytes 393224 | tf_op jit(solution)/shard_map/ppermute | solution.py:157
  32.3 0.1 fusion.6
  32.3 1.8 %collective-permute-done.3 = f32[64,512]{1,0:T(8,128)S(1)} collective-permute-done((f32[64,512]{1,0:T(8,128)S(1)}, f32[64,512]{1,0:T(8,128)S(1)}, u32[]{:S(2)}, u32[]{:S(2)}) %collective-permute-start.3) | collective-permute-done | bytes 131104 | tf_op jit(solution)/shard_map/ppermute | solution.py:157
  34.2 7.6 %collective-permute-done.4 = f32[64,512]{1,0:T(8,128)S(1)} collective-permute-done((f32[64,512]{1,0:T(8,128)S(1)}, f32[64,512]{1,0:T(8,128)S(1)}, u32[]{:S(2)}, u32[]{:S(2)}) %collective-permute-start.4) | collective-permute-done | bytes 131104 | tf_op jit(solution)/shard_map/ppermute | solution.py:157
  41.7 0.0 collective-permute-done.5
  41.8 0.2 fusion
  42.0 0.1 reshape.37
  42.1 5.6 %all-gather.2 = f32[4,4,1024]{2,1,0:T(4,128)S(1)} all-gather(f32[1,4,1024]{2,1,0:T(4,128)S(1)} %reshape.37), channel_id=1, replica_groups=mesh['groups'=2,'width'=4,'tokens'=4] {'tokens'}, dimensions={0}, use_global_device_ids=true | all-gather | bytes 81920 | tf_op jit(solution)/shard_map/all_gather | solution.py:359
  47.7 0.6 reshape.38.refs_2_
  48.3 0.0 all-gather.6.cloned.1.call-done
  48.3 2.5 %all-gather.8.cloned.1.call-done = f32[1632,256]{1,0:T(8,128)} async-done(((f32[408,256]{1,0:T(8,128)}), f32[1632,256]{1,0:T(8,128)}) %all-gather.8.cloned.1.call-update) | async-done | bytes 1671184 | tf_op jit(solution)/shard_map/all_gather | solution.py:344
  50.8 40.3 %shard_map.92 = f32[4,32]{1,0:T(4,128)} custom-call(s32[32]{0:T(128)} %dynamic_slice.6.ids_ref, f32[4,264,256]{2,1,0:T(8,128)} %bitcast.20, f32[4,408,256]{2,1,0:T(8,128)} %bitcast.19, f32[16,1024]{1,0:T(8,128)} %reshape.38.refs_2_, f32[4,16]{1,0:T(4,128)} %compare_convert_fusion.refs_3_), custom_call_target="tpu_custom_call" | custom-call | flops 4294967296 | bytes 4194304 | tf_op jit(solution)/shard_map/pallas_call | solution.py:286
  (4 shorter events, 0.1 us)
Async XLA Ops:
  6.5 13.0 %copy-start = (bf16[512,1280]{1,0:T(8,128)(2,1)S(1)}, bf16[512,1280]{1,0:T(8,128)(2,1)}, u32[]{:S(2)}) copy-start(bf16[512,1280]{1,0:T(8,128)(2,1)} %param.10) | copy-start | bytes 3932164
  6.5 41.8 %all-gather.6.cloned.1.call-start = ((), (), s32[]{:S(2)}) async-start(), calls=%async_computation | async-start | bytes 1351680 | tf_op jit(solution)/shard_map/all_gather | solution.py:324
  8.5 42.3 %all-gather.8.cloned.1.call-start = ((), (), s32[]{:S(2)}) async-start(), calls=%async_computation.1 | async-start | bytes 2088960 | tf_op jit(solution)/shard_map/all_gather | solution.py:344
  8.5 11.0 %copy-start.1 = (bf16[32,1280]{1,0:T(8,128)(2,1)S(1)}, bf16[32,1280]{1,0:T(8,128)(2,1)}, u32[]{:S(2)}) copy-start(bf16[32,1280]{1,0:T(8,128)(2,1)} %param.12) | copy-start | bytes 245764
  8.5 11.6 %collective-permute-start = (f32[136,256]{1,0:T(8,128)}, f32[136,256]{1,0:T(8,128)S(1)}, u32[]{:S(2)}, u32[]{:S(2)}) collective-permute-start(f32[136,256]{1,0:T(8,128)} %get-tuple-element.12), channel_id=1, source_target_pairs={{0,4},{4,0},{8,12},{12,8},{1,5},{5,1},{9,13},{13,9},{2,6},{6,2},{1... | collective-permute-start | bytes 417800 | tf_op jit(solution)/shard_map/ppermute | solution.py:157
  11.6 13.7 %collective-permute-start.1 = (f32[136,256]{1,0:T(8,128)}, f32[136,256]{1,0:T(8,128)S(1)}, u32[]{:S(2)}, u32[]{:S(2)}) collective-permute-start(f32[136,256]{1,0:T(8,128)} %get-tuple-element.12), channel_id=1, source_target_pairs={{0,8},{4,12},{8,0},{12,4},{1,9},{5,13},{9,1},{13,5},{2,10},{6,14},... | collective-permute-start | bytes 417800 | tf_op jit(solution)/shard_map/ppermute | solution.py:157
  14.2 11.1 %collective-permute-start.2 = (f32[136,256]{1,0:T(8,128)}, f32[136,256]{1,0:T(8,128)S(1)}, u32[]{:S(2)}, u32[]{:S(2)}) collective-permute-start(f32[136,256]{1,0:T(8,128)} %get-tuple-element.12), channel_id=1, source_target_pairs={{0,12},{4,8},{8,4},{12,0},{1,13},{5,9},{9,5},{13,1},{2,14},{6,10},... | collective-permute-start | bytes 417800 | tf_op jit(solution)/shard_map/ppermute | solution.py:157
  19.5 6.6 %copy-start.2 = (s32[16]{0:T(128)S(1)}, s32[16]{0:T(128)}, u32[]{:S(2)}) copy-start(s32[16]{0:T(128)} %param.15) | copy-start | bytes 196
  19.6 6.7 %copy-start.3 = (s32[128]{0:T(128)S(1)}, s32[128]{0:T(128)}, u32[]{:S(2)}) copy-start(s32[128]{0:T(128)} %param.17) | copy-start | bytes 1540
  19.6 7.3 %copy-start.4 = (s32[16]{0:T(128)S(1)}, s32[16]{0:T(128)}, u32[]{:S(2)}) copy-start(s32[16]{0:T(128)} %param.16) | copy-start | bytes 196
  27.7 6.5 %collective-permute-start.3 = (f32[64,512]{1,0:T(8,128)S(1)}, f32[64,512]{1,0:T(8,128)S(1)}, u32[]{:S(2)}, u32[]{:S(2)}) collective-permute-start(f32[64,512]{1,0:T(8,128)S(1)} %pad_maximum_fusion.1), channel_id=1, source_target_pairs={{0,4},{4,0},{8,12},{12,8},{1,5},{5,1},{9,13},{13,9},{2,6},{6,2},{1... | collective-permute-start | bytes 393224 | tf_op jit(solution)/shard_map/ppermute | solution.py:157
  29.8 11.9 %collective-permute-start.4 = (f32[64,512]{1,0:T(8,128)S(1)}, f32[64,512]{1,0:T(8,128)S(1)}, u32[]{:S(2)}, u32[]{:S(2)}) collective-permute-start(f32[64,512]{1,0:T(8,128)S(1)} %pad_maximum_fusion.1), channel_id=1, source_target_pairs={{0,8},{4,12},{8,0},{12,4},{1,9},{5,13},{9,1},{13,5},{2,10},{6,14},... | collective-permute-start | bytes 393224 | tf_op jit(solution)/shard_map/ppermute | solution.py:157
  30.8 10.9 %collective-permute-start.5 = (f32[64,512]{1,0:T(8,128)S(1)}, f32[64,512]{1,0:T(8,128)S(1)}, u32[]{:S(2)}, u32[]{:S(2)}) collective-permute-start(f32[64,512]{1,0:T(8,128)S(1)} %pad_maximum_fusion.1), channel_id=1, source_target_pairs={{0,12},{4,8},{8,4},{12,0},{1,13},{5,9},{9,5},{13,1},{2,14},{6,10},... | collective-permute-start | bytes 393224 | tf_op jit(solution)/shard_map/ppermute | solution.py:157
Sparse Core Ops, SparseCore 0:
  8.9 19.5 all-gather.5
  30.1 20.6 all-gather.7

commit v4 on v3

--- a/solution.py
+++ b/solution.py
@@ -12,6 +12,7 @@
 K = 1024
 BLOCK = 128
 PIVOTS = 16
+WINDOW = 32
 TERMS = 6
 f32 = jnp.float32
 
@@ -55,47 +56,52 @@
     return lax.broadcasted_iota(jnp.int32, shape, 0) == lax.broadcasted_iota(jnp.int32, shape, 1)
 
 
-def factor_block(work):
-    work[:, BLOCK:] = eye_mask().astype(f32)
-    tiles = PIVOTS // 8
-    row = lax.broadcasted_iota(jnp.int32, (8, 2 * BLOCK), 0)
-    for group in range(BLOCK // PIVOTS):
-        base = group * PIVOTS
+def factor_block(work, pending):
+    row = lax.broadcasted_iota(jnp.int32, (8, BLOCK), 0)
+    lane = lax.broadcasted_iota(jnp.int32, (8, BLOCK), 1)
+    tiles = WINDOW // 8
+    for base in range(0, BLOCK, WINDOW):
         rows = [work[base + 8 * h : base + 8 * h + 8, :] for h in range(tiles)]
-        columns = [
-            [
-                jnp.broadcast_to(
-                    work[base + 8 * h : base + 8 * h + 8, base + j : base + j + 1], (8, BLOCK)
-                )
-                for h in range(tiles)
+        for group in range(0, WINDOW, PIVOTS):
+            columns = [
+                {
+                    h: jnp.broadcast_to(rows[h][:, column : column + 1], (8, BLOCK))
+                    for h in range(group // 8, tiles)
+                }
+                for column in range(base + group, base + group + PIVOTS)
             ]
-            for j in range(PIVOTS)
-        ]
-        for j in range(PIVOTS):
-            hj, jj = divmod(j, 8)
-            scale = lax.rsqrt(jnp.broadcast_to(columns[j][hj][jj : jj + 1, :], (8, BLOCK)))
-            lower = [columns[j][h] * scale for h in range(hj, tiles)]
-            pivot_row = jnp.broadcast_to(rows[hj][jj : jj + 1, :], (8, 2 * BLOCK)) * jnp.concatenate(
-                [scale, scale], 1
+            pending()
+            for j in range(PIVOTS):
+                hj, jj = divmod(group + j, 8)
+                here = lane == base + group + j
+                scale = lax.rsqrt(jnp.broadcast_to(columns[j][hj][jj : jj + 1, :], (8, BLOCK)))
+                lower = {h: columns[j][h] * scale for h in range(hj, tiles)}
+                for l in range(j + 1, PIVOTS):
+                    entry = jnp.broadcast_to(columns[l][hj][jj : jj + 1, :], (8, BLOCK)) * scale
+                    for h in range(hj, tiles):
+                        columns[l][h] = columns[l][h] - lower[h] * entry
+                pivot_row = jnp.broadcast_to(rows[hj][jj : jj + 1, :], (8, BLOCK))
+                pivot_row = jnp.where(here, 1.0, pivot_row) * scale
+                for h in range(hj, tiles):
+                    changed = jnp.where(here, 0.0, rows[h]) - lower[h] * pivot_row
+                    if h == hj:
+                        changed = jnp.where(
+                            row > jj, changed, jnp.where(row == jj, pivot_row, rows[h])
+                        )
+                    rows[h] = changed
+        done = jnp.concatenate(rows, 0)
+        end = base + WINDOW
+        work[base:end, :] = done
+        if end < BLOCK:
+            window_row = base + lax.broadcasted_iota(jnp.int32, (WINDOW, BLOCK), 0)
+            window_lane = lax.broadcasted_iota(jnp.int32, (WINDOW, BLOCK), 1)
+            above = (window_lane > window_row) & (window_lane < end)
+            change = contract(
+                left_terms(done, 0), right_terms(jnp.where(above, 0.0, done), 0), 0, 0
             )
-            for l in range(j + 1, PIVOTS):
-                entry = jnp.broadcast_to(columns[l][hj][jj : jj + 1, :], (8, BLOCK)) * scale
-                for h in range(hj, tiles):
-                    columns[l][h] = columns[l][h] - lower[h - hj] * entry
-            for h in range(hj, tiles):
-                wide = jnp.concatenate([lower[h - hj], lower[h - hj]], 1)
-                changed = rows[h] - wide * pivot_row
-                if h == hj:
-                    changed = jnp.where(
-                        row > jj, changed, jnp.where(row == jj, pivot_row, rows[h])
-                    )
-                rows[h] = changed
-        done = jnp.concatenate(rows, 0)
-        work[base : base + PIVOTS, :] = done
-        if base + PIVOTS < BLOCK:
-            left, right = both_terms(done, 0)
-            change = contract(left[:, :BLOCK], right, 0, 0)
-            work[base + PIVOTS :, :] = work[base + PIVOTS :, :] - change[base + PIVOTS :, :]
+            rest_lane = lax.broadcasted_iota(jnp.int32, (BLOCK - end, BLOCK), 1)
+            taken = (rest_lane >= base) & (rest_lane < end)
+            work[end:, :] = jnp.where(taken, 0.0, work[end:, :]) - change[end:, :]
 
 
 def pack_kernel(prior_ref, bank_ref, half_ref, first_ref):
@@ -244,28 +250,62 @@
         )
         if high < size:
             gram[low:high, high:] = gram[low:high, high:] + product[:, BLOCK:]
-    scores = jnp.zeros((ids_ref.shape[0], sequences), f32)
-    for k in range(blocks):
-        low, high = k * BLOCK, (k + 1) * BLOCK
-        work[:, :BLOCK] = gram[low:high, low:high]
-        factor_block(work)
-        inverse_left, inverse_right = both_terms(work[:, BLOCK:], 1)
+    scores = [jnp.zeros((ids_ref.shape[0], sequences), f32)]
+    lower = lax.broadcasted_iota(jnp.int32, (BLOCK, BLOCK), 0) >= lax.broadcasted_iota(
+        jnp.int32, (BLOCK, BLOCK), 1
+    )
+    waiting = []
+
+    def pending():
+        if waiting:
+            waiting.pop(0)()
+
+    def panel(inverse_left, block, low, high):
+        left, right = both_terms(
+            contract(inverse_left, right_terms(gram[block : block + BLOCK, low:high], 0), 1, 0), 0
+        )
+        left_ref[:, low:high] = left
+        right_ref[:, low:high] = right
+        return left, right
+
+    def update(row, low):
+        gram[row : row + BLOCK, low:] = gram[row : row + BLOCK, low:] - contract(
+            left_ref[:, row : row + BLOCK], right_ref[:, low:], 0, 0
+        )
+
+    def update_extra(inverse_right, low, high):
         solved = contract(left_terms(extra[:, low:high], 1), inverse_right, 1, 1)
         solved_left, solved_right = both_terms(solved, 1)
-        scores = scores + contract(solved_left[sequences:], solved_right[:sequences], 1, 1)
-        if k == blocks - 1:
-            break
-        panel = contract(inverse_left, right_terms(gram[low:high, high:], 0), 1, 0)
-        panel_left, panel_right = both_terms(panel, 0)
-        left_ref[:, high:] = panel_left
-        right_ref[:, high:] = panel_right
-        extra[:, high:] = extra[:, high:] - contract(solved_left, panel_right, 1, 0)
-        for i in range(high, size, BLOCK):
-            gram[i : i + BLOCK, i:] = gram[i : i + BLOCK, i:] - contract(
-                left_ref[:, i : i + BLOCK], right_ref[:, i:], 0, 0
+        scores[0] = scores[0] + contract(solved_left[sequences:], solved_right[:sequences], 1, 1)
+        if high < size:
+            extra[:, high:] = extra[:, high:] - contract(solved_left, right_ref[:, high:], 1, 0)
+
+    for low in range(0, size, BLOCK):
+        high = low + BLOCK
+        work[...] = gram[low:high, low:high]
+        factor_block(work, pending)
+        while waiting:
+            pending()
+        inverse_left, inverse_right = both_terms(jnp.where(lower, work[...], 0.0), 1)
+        if high < size:
+            after = high + BLOCK
+            left, right = panel(inverse_left, low, high, after)
+            gram[high:after, high:after] = gram[high:after, high:after] - contract(
+                left, right, 0, 0
             )
+            if after < size:
+                middle = after + ((size - after) // BLOCK + 1) // 2 * BLOCK
+                waiting.append(functools.partial(panel, inverse_left, low, after, middle))
+                if middle < size:
+                    waiting.append(functools.partial(panel, inverse_left, low, middle, size))
+                waiting.append(functools.partial(update, high, after))
+        waiting.append(functools.partial(update_extra, inverse_right, low, high))
+        for row in range(high + BLOCK, size, BLOCK):
+            waiting.append(functools.partial(update, row, row))
+    while waiting:
+        pending()
     out_ref[...] = lax.dot_general(
-        choose_ref[...], scores, (((1,), (1,)), ((), ())), precision=highest
+        choose_ref[...], scores[0], (((1,), (1,)), ((), ())), precision=highest
     )
 
 
@@ -277,7 +317,7 @@
     scratch = [
         pltpu.VMEM((size, size), f32),
         pltpu.VMEM((rows, size), f32),
-        pltpu.VMEM((BLOCK, 2 * BLOCK), f32),
+        pltpu.VMEM((BLOCK, BLOCK), f32),
         pltpu.VMEM((TERMS * BLOCK, size), jnp.bfloat16),
         pltpu.VMEM((TERMS * BLOCK, size), jnp.bfloat16),
     ]

time: 98.2 us -> 92.8 us (0.945)
  Pallas kernels: 42.2 us -> 36.8 us
    pallas_call x1, Pallas kernels: 40.3 us -> 34.9 us  [solve(): pl.pallas_call(functools.partial(solve_kernel, halves), out_shape=jax.Sha...]
  transfers between devices with their start and end apart: 8 -> 8, of which waited for: 4 -> 4; matrix products, arithmetic and copies ran while one was open for 9% -> 10% of each run, Pallas kernels for 0% -> 0%
where the time goes in v4:
time: 92.8 us; the launch traced here: 92.6 us
  Pallas kernels  36.8 us (40%)
  waiting for transfers between devices  17.1 us (18%)
  between operations  13.5 us (15%)
  starting transfers between devices  10.3 us (11%)
  matrix products  5.99 us (6%)
  blocking collectives  5.56 us (6%)
  other arithmetic  1.8 us (2%)
  local copies, waits for them, and re-layouts  1.43 us (2%)
    pallas_call x1, Pallas kernels, solve(): pl.pallas_call(functools.partial(solve_kernel, halves), out_shape=jax.Sha...  34.9 us
    ppermute x6, waiting for transfers between devices, exchange(): lax.ppermute(value, axis, [(i, i ^ s) for i in range(count)])  14.6 us
    ppermute x6, starting transfers between devices, exchange(): lax.ppermute(value, axis, [(i, i ^ s) for i in range(count)])  10.3 us
    all_gather x1, blocking collectives, local(): all_grads = lax.all_gather(vectors, 'tokens', axis=0, tiled=True)  5.56 us
    dot_general x1, matrix products, local(): lax.dot_general(proj_in, layer_inputs, features, preferred_element_type=f32)  5.3 us
    all_gather x1, waiting for transfers between devices, local(): others = lax.all_gather(jnp.concatenate(pieces, 0), 'tokens', axis=0)  2.51 us
    pallas_call x1, Pallas kernels, pack(): pl.pallas_call(pack_kernel, out_shape=(jax.ShapeDtypeStruct((span, 2 * BL...  1.9 us
  transfers between devices with their start and end apart: 8, of which 4 were waited for; matrix products, arithmetic and copies ran while one was open for 10% of the time, Pallas kernels for 0%

profile of v4, /device:TPU:0, one launch (start us, length us, event | category | flops | bytes accessed | tf_op | source)
XLA Modules:
  0.0 92.6 jit_solution(15435926218073372593)
XLA Ops:
  6.5 0.0 copy-start
  6.5 0.0 all-gather.6.cloned.1.call-start
  6.5 1.9 %shard_map.91 = (f32[136,256]{1,0:T(8,128)}, f32[264,256]{1,0:T(8,128)}) custom-call(f32[256,256]{1,0:T(8,128)} %prior_ref.1, f32[32,1024]{1,0:T(8,128)} %bank_ref.1), custom_call_target="tpu_custom_call" | custom-call | tf_op jit(solution)/shard_map/pallas_call | solution.py:149
  8.4 0.0 all-gather.6.cloned.1.call-update
  8.5 0.0 all-gather.8.cloned.1.call-start
  8.5 0.0 copy-start.1
  8.5 3.1 %collective-permute-start = (f32[136,256]{1,0:T(8,128)}, f32[136,256]{1,0:T(8,128)S(1)}, u32[]{:S(2)}, u32[]{:S(2)}) collective-permute-start(f32[136,256]{1,0:T(8,128)} %get-tuple-element.12), channel_id=1, source_target_pairs={{0,4},{4,0},{8,12},{12,8},{1,5},{5,1},{9,13},{13,9},{2,6},{6,2},{1... | collective-permute-start | bytes 417800 | tf_op jit(solution)/shard_map/ppermute | solution.py:163
  11.6 2.6 %collective-permute-start.1 = (f32[136,256]{1,0:T(8,128)}, f32[136,256]{1,0:T(8,128)S(1)}, u32[]{:S(2)}, u32[]{:S(2)}) collective-permute-start(f32[136,256]{1,0:T(8,128)} %get-tuple-element.12), channel_id=1, source_target_pairs={{0,8},{4,12},{8,0},{12,4},{1,9},{5,13},{9,1},{13,5},{2,10},{6,14},... | collective-permute-start | bytes 417800 | tf_op jit(solution)/shard_map/ppermute | solution.py:163
  14.2 0.0 collective-permute-start.2
  14.2 5.3 %fusion.7 = f32[32,512]{1,0:T(8,128)S(1)} fusion(bf16[32,6912]{1,0:T(8,128)(2,1)} %param.11, bf16[512,6912]{1,0:T(8,128)(2,1)} %param.9), kind=kOutput, calls=%fused_computation.17 | convolution fusion | flops 226492416 | bytes 7585792 | tf_op jit(solution)/shard_map/dot_general | solution.py:377
  19.5 0.0 copy-done
  19.5 0.0 copy-done.1
  19.5 0.0 copy-start.2
  19.6 0.0 copy-start.3
  19.6 0.0 copy-start.4
  19.6 0.5 fusion.8
  20.1 0.0 collective-permute-done
  20.1 5.2 %collective-permute-done.1 = f32[136,256]{1,0:T(8,128)S(1)} collective-permute-done((f32[136,256]{1,0:T(8,128)}, f32[136,256]{1,0:T(8,128)S(1)}, u32[]{:S(2)}, u32[]{:S(2)}) %collective-permute-start.1) | collective-permute-done | bytes 139296 | tf_op jit(solution)/shard_map/ppermute | solution.py:163
  25.3 0.0 collective-permute-done.2
  25.3 0.8 pad_maximum_fusion
  26.1 0.0 all-gather.8.cloned.1.call-update
  26.1 0.0 copy-done.2
  26.1 0.1 dynamic_slice.7
  26.2 0.0 copy-done.3
  26.2 0.6 dynamic_slice.6.ids_ref
  26.8 0.0 copy-done.4
  26.8 0.2 select_reduce_fusion
  27.0 0.7 compare_convert_fusion.refs_3_
  27.7 2.1 %collective-permute-start.3 = (f32[64,512]{1,0:T(8,128)S(1)}, f32[64,512]{1,0:T(8,128)S(1)}, u32[]{:S(2)}, u32[]{:S(2)}) collective-permute-start(f32[64,512]{1,0:T(8,128)S(1)} %pad_maximum_fusion.1), channel_id=1, source_target_pairs={{0,4},{4,0},{8,12},{12,8},{1,5},{5,1},{9,13},{13,9},{2,6},{6,2},{1... | collective-permute-start | bytes 393224 | tf_op jit(solution)/shard_map/ppermute | solution.py:163
  29.8 1.0 %collective-permute-start.4 = (f32[64,512]{1,0:T(8,128)S(1)}, f32[64,512]{1,0:T(8,128)S(1)}, u32[]{:S(2)}, u32[]{:S(2)}) collective-permute-start(f32[64,512]{1,0:T(8,128)S(1)} %pad_maximum_fusion.1), channel_id=1, source_target_pairs={{0,8},{4,12},{8,0},{12,4},{1,9},{5,13},{9,1},{13,5},{2,10},{6,14},... | collective-permute-start | bytes 393224 | tf_op jit(solution)/shard_map/ppermute | solution.py:163
  30.8 1.5 %collective-permute-start.5 = (f32[64,512]{1,0:T(8,128)S(1)}, f32[64,512]{1,0:T(8,128)S(1)}, u32[]{:S(2)}, u32[]{:S(2)}) collective-permute-start(f32[64,512]{1,0:T(8,128)S(1)} %pad_maximum_fusion.1), channel_id=1, source_target_pairs={{0,12},{4,8},{8,4},{12,0},{1,13},{5,9},{9,5},{13,1},{2,14},{6,10},... | collective-permute-start | bytes 393224 | tf_op jit(solution)/shard_map/ppermute | solution.py:163
  32.3 0.1 fusion.6
  32.3 1.8 %collective-permute-done.3 = f32[64,512]{1,0:T(8,128)S(1)} collective-permute-done((f32[64,512]{1,0:T(8,128)S(1)}, f32[64,512]{1,0:T(8,128)S(1)}, u32[]{:S(2)}, u32[]{:S(2)}) %collective-permute-start.3) | collective-permute-done | bytes 131104 | tf_op jit(solution)/shard_map/ppermute | solution.py:163
  34.2 7.6 %collective-permute-done.4 = f32[64,512]{1,0:T(8,128)S(1)} collective-permute-done((f32[64,512]{1,0:T(8,128)S(1)}, f32[64,512]{1,0:T(8,128)S(1)}, u32[]{:S(2)}, u32[]{:S(2)}) %collective-permute-start.4) | collective-permute-done | bytes 131104 | tf_op jit(solution)/shard_map/ppermute | solution.py:163
  41.7 0.0 collective-permute-done.5
  41.8 0.2 fusion
  42.0 0.1 reshape.37
  42.1 5.6 %all-gather.2 = f32[4,4,1024]{2,1,0:T(4,128)S(1)} all-gather(f32[1,4,1024]{2,1,0:T(4,128)S(1)} %reshape.37), channel_id=1, replica_groups=mesh['groups'=2,'width'=4,'tokens'=4] {'tokens'}, dimensions={0}, use_global_device_ids=true | all-gather | bytes 81920 | tf_op jit(solution)/shard_map/all_gather | solution.py:399
  47.7 0.6 reshape.38.refs_2_
  48.3 0.0 all-gather.6.cloned.1.call-done
  48.3 2.5 %all-gather.8.cloned.1.call-done = f32[1632,256]{1,0:T(8,128)} async-done(((f32[408,256]{1,0:T(8,128)}), f32[1632,256]{1,0:T(8,128)}) %all-gather.8.cloned.1.call-update) | async-done | bytes 1671184 | tf_op jit(solution)/shard_map/all_gather | solution.py:384
  50.8 34.9 %shard_map.92 = f32[4,32]{1,0:T(4,128)} custom-call(s32[32]{0:T(128)} %dynamic_slice.6.ids_ref, f32[4,264,256]{2,1,0:T(8,128)} %bitcast.20, f32[4,408,256]{2,1,0:T(8,128)} %bitcast.19, f32[16,1024]{1,0:T(8,128)} %reshape.38.refs_2_, f32[4,16]{1,0:T(4,128)} %compare_convert_fusion.refs_3_), custom_call_target="tpu_custom_call" | custom-call | flops 4294967296 | bytes 4194304 | tf_op jit(solution)/shard_map/pallas_call | solution.py:326
  (4 shorter events, 0.1 us)
Async XLA Ops:
  6.5 13.0 %copy-start = (bf16[512,1280]{1,0:T(8,128)(2,1)S(1)}, bf16[512,1280]{1,0:T(8,128)(2,1)}, u32[]{:S(2)}) copy-start(bf16[512,1280]{1,0:T(8,128)(2,1)} %param.10) | copy-start | bytes 3932164
  6.5 41.8 %all-gather.6.cloned.1.call-start = ((), (), s32[]{:S(2)}) async-start(), calls=%async_computation | async-start | bytes 1351680 | tf_op jit(solution)/shard_map/all_gather | solution.py:364
  8.5 42.3 %all-gather.8.cloned.1.call-start = ((), (), s32[]{:S(2)}) async-start(), calls=%async_computation.1 | async-start | bytes 2088960 | tf_op jit(solution)/shard_map/all_gather | solution.py:384
  8.5 11.0 %copy-start.1 = (bf16[32,1280]{1,0:T(8,128)(2,1)S(1)}, bf16[32,1280]{1,0:T(8,128)(2,1)}, u32[]{:S(2)}) copy-start(bf16[32,1280]{1,0:T(8,128)(2,1)} %param.12) | copy-start | bytes 245764
  8.5 11.6 %collective-permute-start = (f32[136,256]{1,0:T(8,128)}, f32[136,256]{1,0:T(8,128)S(1)}, u32[]{:S(2)}, u32[]{:S(2)}) collective-permute-start(f32[136,256]{1,0:T(8,128)} %get-tuple-element.12), channel_id=1, source_target_pairs={{0,4},{4,0},{8,12},{12,8},{1,5},{5,1},{9,13},{13,9},{2,6},{6,2},{1... | collective-permute-start | bytes 417800 | tf_op jit(solution)/shard_map/ppermute | solution.py:163
  11.6 13.7 %collective-permute-start.1 = (f32[136,256]{1,0:T(8,128)}, f32[136,256]{1,0:T(8,128)S(1)}, u32[]{:S(2)}, u32[]{:S(2)}) collective-permute-start(f32[136,256]{1,0:T(8,128)} %get-tuple-element.12), channel_id=1, source_target_pairs={{0,8},{4,12},{8,0},{12,4},{1,9},{5,13},{9,1},{13,5},{2,10},{6,14},... | collective-permute-start | bytes 417800 | tf_op jit(solution)/shard_map/ppermute | solution.py:163
  14.2 11.1 %collective-permute-start.2 = (f32[136,256]{1,0:T(8,128)}, f32[136,256]{1,0:T(8,128)S(1)}, u32[]{:S(2)}, u32[]{:S(2)}) collective-permute-start(f32[136,256]{1,0:T(8,128)} %get-tuple-element.12), channel_id=1, source_target_pairs={{0,12},{4,8},{8,4},{12,0},{1,13},{5,9},{9,5},{13,1},{2,14},{6,10},... | collective-permute-start | bytes 417800 | tf_op jit(solution)/shard_map/ppermute | solution.py:163
  19.5 6.6 %copy-start.2 = (s32[16]{0:T(128)S(1)}, s32[16]{0:T(128)}, u32[]{:S(2)}) copy-start(s32[16]{0:T(128)} %param.15) | copy-start | bytes 196
  19.6 6.7 %copy-start.3 = (s32[128]{0:T(128)S(1)}, s32[128]{0:T(128)}, u32[]{:S(2)}) copy-start(s32[128]{0:T(128)} %param.17) | copy-start | bytes 1540
  19.6 7.3 %copy-start.4 = (s32[16]{0:T(128)S(1)}, s32[16]{0:T(128)}, u32[]{:S(2)}) copy-start(s32[16]{0:T(128)} %param.16) | copy-start | bytes 196
  27.7 6.5 %collective-permute-start.3 = (f32[64,512]{1,0:T(8,128)S(1)}, f32[64,512]{1,0:T(8,128)S(1)}, u32[]{:S(2)}, u32[]{:S(2)}) collective-permute-start(f32[64,512]{1,0:T(8,128)S(1)} %pad_maximum_fusion.1), channel_id=1, source_target_pairs={{0,4},{4,0},{8,12},{12,8},{1,5},{5,1},{9,13},{13,9},{2,6},{6,2},{1... | collective-permute-start | bytes 393224 | tf_op jit(solution)/shard_map/ppermute | solution.py:163
  29.8 11.9 %collective-permute-start.4 = (f32[64,512]{1,0:T(8,128)S(1)}, f32[64,512]{1,0:T(8,128)S(1)}, u32[]{:S(2)}, u32[]{:S(2)}) collective-permute-start(f32[64,512]{1,0:T(8,128)S(1)} %pad_maximum_fusion.1), channel_id=1, source_target_pairs={{0,8},{4,12},{8,0},{12,4},{1,9},{5,13},{9,1},{13,5},{2,10},{6,14},... | collective-permute-start | bytes 393224 | tf_op jit(solution)/shard_map/ppermute | solution.py:163
  30.8 10.9 %collective-permute-start.5 = (f32[64,512]{1,0:T(8,128)S(1)}, f32[64,512]{1,0:T(8,128)S(1)}, u32[]{:S(2)}, u32[]{:S(2)}) collective-permute-start(f32[64,512]{1,0:T(8,128)S(1)} %pad_maximum_fusion.1), channel_id=1, source_target_pairs={{0,12},{4,8},{8,4},{12,0},{1,13},{5,9},{9,5},{13,1},{2,14},{6,10},... | collective-permute-start | bytes 393224 | tf_op jit(solution)/shard_map/ppermute | solution.py:163
Sparse Core Ops, SparseCore 0:
  8.9 19.5 all-gather.5
  30.1 20.6 all-gather.7

commit v5 on v4

--- a/solution.py
+++ b/solution.py
@@ -157,24 +157,27 @@
     )(prior, bank)
 
 
+def swap(value, axis, s):
+    return lax.ppermute(value, axis, [(i, i ^ s) for i in range(lax.axis_size(axis))])
+
+
 def exchange(value, axis):
-    count = lax.axis_size(axis)
-    return [value] + [
-        lax.ppermute(value, axis, [(i, i ^ s) for i in range(count)]) for s in range(1, count)
-    ]
-
-
-def solve_kernel(halves, ids_ref, *refs):
-    if halves:
-        own_ref, others_ref, grads_ref, choose_ref, out_ref = refs[:5]
-        gram, extra, work, left_ref, right_ref, tails, bank, sems = refs[5:]
+    return [value] + [swap(value, axis, s) for s in range(1, lax.axis_size(axis))]
+
+
+def solve_kernel(halves, ids_ref, order_ref, *refs):
+    if halves:
+        own_ref, others_ref, near_ref, far_ref, grads_ref, out_ref = refs[:6]
+        gram, extra, work, left_ref, right_ref, tails, bank, sems = refs[6:]
     else:
-        prior_ref, bank_ref, grads_ref, choose_ref, out_ref = refs[:5]
-        gram, extra, work, left_ref, right_ref, bank, sems = refs[5:]
+        prior_ref, bank_ref, grads_ref, out_ref = refs[:4]
+        gram, extra, work, left_ref, right_ref, bank, sems = refs[4:]
     size = gram.shape[0]
     blocks = size // BLOCK
-    sequences = grads_ref.shape[0]
+    sequences = order_ref.shape[0]
+    columns_here, queries = out_ref.shape
     bank_chunks, bank_rows, chunk = bank.shape[1:]
+    width_index, token_index = lax.axis_index("width"), lax.axis_index("tokens")
     copies = []
 
     def start(source, target):
@@ -185,38 +188,51 @@
     if halves:
         parts = own_ref.shape[0]
         span = BLOCK + 8
-        me = lax.axis_index("width")
-        for s in range(parts):
-            j = lax.bitwise_xor(me, s)
-            source, place = (own_ref, 0) if s == 0 else (others_ref, (s - 1) * span)
-            for i in range(parts):
-                row = 2 * BLOCK * lax.min(i, j) + jnp.where(i > j, BLOCK, 0)
-                row = pl.multiple_of(row, BLOCK)
-                column = pl.multiple_of(2 * BLOCK * lax.max(i, j), BLOCK)
-                start(
-                    source.at[i, place : place + BLOCK, :],
-                    gram.at[pl.ds(row, BLOCK), pl.ds(column, 2 * BLOCK)],
+
+        def place(source, i, j):
+            row = 2 * BLOCK * lax.min(i, j) + jnp.where(i > j, BLOCK, 0)
+            row = pl.multiple_of(row, BLOCK)
+            column = pl.multiple_of(2 * BLOCK * lax.max(i, j), BLOCK)
+            start(
+                source.at[:BLOCK, :], gram.at[pl.ds(row, BLOCK), pl.ds(column, 2 * BLOCK)]
+            )
+            start(source.at[BLOCK:, :], tails.at[i, j])
+
+        for i in range(parts):
+            place(own_ref.at[i, :span, :], i, width_index)
+            for s in range(2, parts):
+                first = (s - 2) * span
+                place(
+                    others_ref.at[i, first : first + span, :], i, lax.bitwise_xor(width_index, s)
                 )
-                start(source.at[i, place + BLOCK : place + span, :], tails.at[i, j])
-        for i in range(parts):
             for c in range(bank_chunks):
                 first = span + c * bank_rows
                 start(own_ref.at[i, first : first + bank_rows, :], bank.at[i, c])
+        for sibling, source in enumerate((near_ref, far_ref)):
+            for across in range(2):
+                place(
+                    source.at[across],
+                    lax.bitwise_xor(token_index, 2 * across + sibling),
+                    lax.bitwise_xor(width_index, 1),
+                )
     else:
         start(prior_ref, gram)
         start(bank_ref, bank)
-    grads = grads_ref[...]
+    slabs = grads_ref.shape[1]
+    for i in range(grads_ref.shape[0]):
+        extra[i * slabs : (i + 1) * slabs, :] = grads_ref[i]
+    grads = extra[:sequences, :]
     left, right = both_terms(grads, 0)
     on_diagonal = eye_mask()
     for copy in copies:
         copy.wait()
-    for q in range(ids_ref.shape[0]):
-        part, row = ids_ref[q] // bank_rows, ids_ref[q] % bank_rows
+    for q in range(queries):
+        id_here = ids_ref[token_index * queries + q]
+        part, row = id_here // bank_rows, id_here % bank_rows
         for c in range(bank_chunks):
             extra[sequences + q : sequences + q + 1, c * chunk : (c + 1) * chunk] = bank[
                 part, c, pl.ds(row, 1), :
             ]
-    extra[:sequences, :] = grads
     diagonal = jnp.zeros((BLOCK, BLOCK), f32)
     if halves:
         upper = lax.broadcasted_iota(jnp.int32, (BLOCK, BLOCK), 0) <= lax.broadcasted_iota(
@@ -250,7 +266,7 @@
         )
         if high < size:
             gram[low:high, high:] = gram[low:high, high:] + product[:, BLOCK:]
-    scores = [jnp.zeros((ids_ref.shape[0], sequences), f32)]
+    scores = [jnp.zeros((queries, sequences), f32)]
     lower = lax.broadcasted_iota(jnp.int32, (BLOCK, BLOCK), 0) >= lax.broadcasted_iota(
         jnp.int32, (BLOCK, BLOCK), 1
     )
@@ -304,14 +320,20 @@
             waiting.append(functools.partial(update, row, row))
     while waiting:
         pending()
+    shape = (columns_here, sequences)
+    column_id = width_index * columns_here + lax.broadcasted_iota(jnp.int32, shape, 0)
+    slab_id = lax.broadcasted_iota(jnp.int32, shape, 1)
+    choose = jnp.zeros(shape, f32)
+    for n in range(sequences):
+        choose = jnp.where((slab_id == n) & (column_id == order_ref[n]), 1.0, choose)
     out_ref[...] = lax.dot_general(
-        choose_ref[...], scores[0], (((1,), (1,)), ((), ())), precision=highest
-    )
-
-
-def solve(halves, ids, prior_operands, bank_shape, grads, choose):
-    sequences, size = grads.shape
-    rows = sequences + ids.shape[0]
+        choose, scores[0], (((1,), (1,)), ((), ())), precision=highest
+    )
+
+
+def solve(halves, ids, order, prior_operands, bank_shape, grads, out_shape):
+    size = grads.shape[2]
+    rows = order.shape[0] + out_shape[1]
     copies = 2 + bank_shape[0] * (2 * bank_shape[0] + bank_shape[1])
     vmem = pl.BlockSpec(memory_space=pltpu.VMEM)
     scratch = [
@@ -325,10 +347,10 @@
         scratch.append(pltpu.VMEM((bank_shape[0], bank_shape[0], 8, 2 * BLOCK), f32))
     return pl.pallas_call(
         functools.partial(solve_kernel, halves),
-        out_shape=jax.ShapeDtypeStruct((choose.shape[0], ids.shape[0]), f32),
-        in_specs=[pl.BlockSpec(memory_space=pltpu.SMEM)]
+        out_shape=jax.ShapeDtypeStruct(out_shape, f32),
+        in_specs=[pl.BlockSpec(memory_space=pltpu.SMEM)] * 2
         + [pl.BlockSpec(memory_space=pl.ANY)] * len(prior_operands)
-        + [vmem, vmem],
+        + [vmem],
         out_specs=vmem,
         scratch_shapes=scratch
         + [pltpu.VMEM(bank_shape, f32), pltpu.SemaphoreType.DMA((copies,))],
@@ -336,7 +358,7 @@
         cost_estimate=pl.CostEstimate(
             flops=4 * size**3, bytes_accessed=4 * size * size, transcendentals=size
         ),
-    )(ids, *prior_operands, grads, choose)
+    )(ids, order, *prior_operands, grads)
 
 
 def local(
@@ -352,7 +374,6 @@
 ):
     width_count = lax.axis_size("width")
     token_count = lax.axis_size("tokens")
-    width_index = lax.axis_index("width")
     token_index = lax.axis_index("tokens")
     slab_count = layer_inputs.shape[0] // SEQ_LEN
     sequence_count = slab_sequence.shape[0]
@@ -380,10 +401,14 @@
         axis=0,
     )
     if halves:
-        projected, pieces = lax.optimization_barrier((projected, pieces))
-        others = lax.all_gather(jnp.concatenate(pieces, 0), "tokens", axis=0)
-        prior_operands = (own, others)
-    total = sum(exchange(projected, "width"))
+        projected, pieces[0] = lax.optimization_barrier((projected, pieces[0]))
+    received = exchange(projected, "width")
+    if halves:
+        received[1], pieces = lax.optimization_barrier((received[1], pieces))
+        others = lax.all_gather(jnp.concatenate(pieces[1:], 0), "tokens", axis=0)
+        near = jnp.stack([pieces[0], swap(pieces[0], "tokens", 2)])
+        prior_operands = (own, others, near, swap(near, "tokens", 1))
+    total = sum(received)
     local_slabs = lax.dynamic_slice_in_dim(slab_sequence, token_index * slab_count, slab_count)
     seq_numbers = jnp.arange(sequence_count, dtype=jnp.int32)
     local_lengths = jnp.sum(
@@ -396,14 +421,11 @@
     vectors = lax.dot_general(
         total_in, total_out, (((2,), (2,)), ((1,), (1,))), precision=highest
     ).reshape(slab_count, K)
-    all_grads = lax.all_gather(vectors, "tokens", axis=0, tiled=True)
-
-    column_count = sequence_count // width_count
-    column_ids = width_index * column_count + jnp.arange(column_count, dtype=jnp.int32)
-    choose = (column_ids[:, None] == slab_sequence[None, :]).astype(f32)
-    query_count = query_ids.shape[0] // token_count
-    local_ids = lax.dynamic_slice_in_dim(query_ids, token_index * query_count, query_count)
-    return solve(halves, local_ids, prior_operands, bank_shape, all_grads, choose).T
+    all_grads = lax.all_gather(vectors, "tokens", axis=0)
+    out_shape = (sequence_count // width_count, query_ids.shape[0] // token_count)
+    return solve(
+        halves, query_ids, slab_sequence, prior_operands, bank_shape, all_grads, out_shape
+    ).T
 
 
 def solution(mesh):

time: 92.8 us -> 92.3 us (level)
  starting transfers between devices: 10.3 us -> 13.1 us
  waiting for transfers between devices: 17.1 us -> 14.6 us
    ppermute x6 -> x8, starting transfers between devices: 10.3 us -> 13 us  [swap(): lax.ppermute(value, axis, [(i, i ^ s) for i in range(lax.axis_size(axis))])]
    all_gather x1, waiting for transfers between devices: 2.51 us -> 0.01 us  [local(): others = lax.all_gather(jnp.concatenate(pieces[1:], 0), 'tokens', axis=0)]
    ppermute x6 -> x8, waiting for transfers between devices: 14.6 us -> 14.5 us  [swap(): lax.ppermute(value, axis, [(i, i ^ s) for i in range(lax.axis_size(axis))])]
  transfers between devices with their start and end apart: 8 -> 10, of which waited for: 4 -> 5; matrix products, arithmetic and copies ran while one was open for 10% -> 8% of each run, Pallas kernels for 0% -> 0%
where the time goes in v5:
time: 92.3 us; the launch traced here: 92.1 us
  Pallas kernels  37 us (40%)
  waiting for transfers between devices  14.6 us (16%)
  between operations  13.6 us (15%)
  starting transfers between devices  13.1 us (14%)
  matrix products  5.99 us (6%)
  blocking collectives  5.87 us (6%)
  other arithmetic  1.12 us (1%)
    pallas_call x1, Pallas kernels, solve(): pl.pallas_call(functools.partial(solve_kernel, halves), out_shape=jax.Sha...  35.1 us
    ppermute x8, waiting for transfers between devices, swap(): lax.ppermute(value, axis, [(i, i ^ s) for i in range(lax.axis_size(axis))])  14.5 us
    ppermute x8, starting transfers between devices, swap(): lax.ppermute(value, axis, [(i, i ^ s) for i in range(lax.axis_size(axis))])  13 us
    all_gather x1, blocking collectives, local(): all_grads = lax.all_gather(vectors, 'tokens', axis=0)  5.87 us
    dot_general x1, matrix products, local(): lax.dot_general(proj_in, layer_inputs, features, preferred_element_type=f32)  5.3 us
    pallas_call x1, Pallas kernels, pack(): pl.pallas_call(pack_kernel, out_shape=(jax.ShapeDtypeStruct((span, 2 * BL...  1.89 us
  transfers between devices with their start and end apart: 10, of which 5 were waited for; matrix products, arithmetic and copies ran while one was open for 8% of the time, Pallas kernels for 0%

profile of v5, /device:TPU:0, one launch (start us, length us, event | category | flops | bytes accessed | tf_op | source)
XLA Modules:
  0.0 92.1 jit_solution(1256401669416953732)
XLA Ops:
  6.5 0.0 copy-start
  6.5 0.0 all-gather.5.cloned.1.call-start
  6.5 1.9 %shard_map.91 = (f32[136,256]{1,0:T(8,128)}, f32[264,256]{1,0:T(8,128)}) custom-call(f32[256,256]{1,0:T(8,128)} %prior_ref.1, f32[32,1024]{1,0:T(8,128)} %bank_ref.1), custom_call_target="tpu_custom_call" | custom-call | tf_op jit(solution)/shard_map/pallas_call | solution.py:149
  8.4 0.0 all-gather.5.cloned.1.call-update
  8.5 0.0 all-gather.7.cloned.1.call-start
  8.5 0.0 copy-start.2
  8.5 5.1 %collective-permute-start.3 = (f32[136,256]{1,0:T(8,128)}, f32[136,256]{1,0:T(8,128)S(1)}, u32[]{:S(2)}, u32[]{:S(2)}) collective-permute-start(f32[136,256]{1,0:T(8,128)} %get-tuple-element.14), channel_id=1, source_target_pairs={{0,12},{4,8},{8,4},{12,0},{1,13},{5,9},{9,5},{13,1},{2,14},{6,10},... | collective-permute-start | bytes 417800 | tf_op jit(solution)/shard_map/ppermute | solution.py:161
  13.6 0.0 collective-permute-start.2
  13.6 0.6 collective-permute-start
  14.3 5.3 %fusion.7 = f32[32,512]{1,0:T(8,128)S(1)} fusion(bf16[32,6912]{1,0:T(8,128)(2,1)} %param.11, bf16[512,6912]{1,0:T(8,128)(2,1)} %param.9), kind=kOutput, calls=%fused_computation.16 | convolution fusion | flops 226492416 | bytes 7585792 | tf_op jit(solution)/shard_map/dot_general | solution.py:398
  19.6 0.0 copy-done
  19.6 0.0 copy-done.2
  19.6 0.0 copy-start.5
  19.6 0.0 copy-start.4
  19.6 0.5 fusion.8
  20.1 2.8 %collective-permute-done = f32[136,256]{1,0:T(8,128)S(1)} collective-permute-done((f32[136,256]{1,0:T(8,128)}, f32[136,256]{1,0:T(8,128)S(1)}, u32[]{:S(2)}, u32[]{:S(2)}) %collective-permute-start) | collective-permute-done | bytes 139296 | tf_op jit(solution)/shard_map/ppermute | solution.py:161
  22.9 2.4 %collective-permute-start.1 = (f32[64,512]{1,0:T(8,128)S(1)}, f32[64,512]{1,0:T(8,128)S(1)}, u32[]{:S(2)}, u32[]{:S(2)}) collective-permute-start(f32[64,512]{1,0:T(8,128)S(1)} %pad_maximum_fusion.2), channel_id=1, source_target_pairs={{0,4},{4,0},{8,12},{12,8},{1,5},{5,1},{9,13},{13,9},{2,6},{6,2},{1... | collective-permute-start | bytes 393224 | tf_op jit(solution)/shard_map/ppermute | solution.py:161
  25.3 0.0 collective-permute-done.3
  25.3 0.4 collective-permute-done.2
  25.7 2.8 %collective-permute-done.1 = f32[64,512]{1,0:T(8,128)S(1)} collective-permute-done((f32[64,512]{1,0:T(8,128)S(1)}, f32[64,512]{1,0:T(8,128)S(1)}, u32[]{:S(2)}, u32[]{:S(2)}) %collective-permute-start.1) | collective-permute-done | bytes 131104 | tf_op jit(solution)/shard_map/ppermute | solution.py:161
  28.4 0.8 pad_maximum_fusion
  29.2 0.0 all-gather.7.cloned.1.call-update
  29.2 0.0 copy-done.5
  29.2 0.1 dynamic_slice.3
  29.3 0.0 copy-done.4
  29.3 0.2 select_reduce_fusion
  29.5 2.5 %collective-permute-start.7 = (f32[64,512]{1,0:T(8,128)S(1)}, f32[64,512]{1,0:T(8,128)S(1)}, u32[]{:S(2)}, u32[]{:S(2)}) collective-permute-start(f32[64,512]{1,0:T(8,128)S(1)} %pad_maximum_fusion.2), channel_id=1, source_target_pairs={{0,12},{4,8},{8,4},{12,0},{1,13},{5,9},{9,5},{13,1},{2,14},{6,10},... | collective-permute-start | bytes 393224 | tf_op jit(solution)/shard_map/ppermute | solution.py:161
  32.0 0.8 collective-permute-start.6
  32.8 0.1 fusion.6
  32.9 1.5 %collective-permute-start.4 = (f32[136,256]{1,0:T(8,128)S(1)}, f32[136,256]{1,0:T(8,128)S(1)}, u32[]{:S(2)}, u32[]{:S(2)}) collective-permute-start(f32[136,256]{1,0:T(8,128)S(1)} %collective-permute-done), channel_id=1, source_target_pairs={{0,2},{1,3},{2,0},{3,1},{4,6},{5,7},{6,4},{7,5},{8,10},{9,11},{10,... | collective-permute-start | bytes 417800 | tf_op jit(solution)/shard_map/ppermute | solution.py:161
  34.4 2.8 %collective-permute-done.7 = f32[64,512]{1,0:T(8,128)S(1)} collective-permute-done((f32[64,512]{1,0:T(8,128)S(1)}, f32[64,512]{1,0:T(8,128)S(1)}, u32[]{:S(2)}, u32[]{:S(2)}) %collective-permute-start.7) | collective-permute-done | bytes 131104 | tf_op jit(solution)/shard_map/ppermute | solution.py:161
  37.2 5.8 %collective-permute-done.6 = f32[64,512]{1,0:T(8,128)S(1)} collective-permute-done((f32[64,512]{1,0:T(8,128)S(1)}, f32[64,512]{1,0:T(8,128)S(1)}, u32[]{:S(2)}, u32[]{:S(2)}) %collective-permute-start.6) | collective-permute-done | bytes 131104 | tf_op jit(solution)/shard_map/ppermute | solution.py:161
  43.1 0.0 collective-permute-done.4
  43.1 0.0 copy-start.1
  43.1 0.1 collective-permute-start.5
  43.2 0.2 fusion
  43.4 0.1 all_gather_reshape.3
  43.5 5.9 %all_gather.19.refs_4_ = f32[4,4,1024]{2,1,0:T(4,128)} all-gather(f32[1,4,1024]{2,1,0:T(4,128)S(1)} %all_gather_reshape.3), channel_id=1, replica_groups=mesh['groups'=2,'width'=4,'tokens'=4] {'tokens'}, dimensions={0}, use_global_device_ids=true | all-gather | bytes 81920 | tf_op jit(solution)/shard_map/all_gather | solution.py:424
  49.4 0.0 collective-permute-done.5.refs_3_
  49.4 0.0 copy-start.3
  49.4 0.0 all-gather.5.cloned.1.call-done
  49.4 0.0 all-gather.7.cloned.1.call-done
  49.4 0.0 copy-done.1
  49.4 0.7 copy-done.3
  50.1 35.1 %shard_map.92 = f32[4,32]{1,0:T(4,128)} custom-call(s32[128]{0:T(128)} %ids_ref.1, s32[16]{0:T(128)} %order_ref.1, f32[4,264,256]{2,1,0:T(8,128)} %bitcast.24, f32[4,272,256]{2,1,0:T(8,128)} %bitcast.23, f32[2,136,256]{2,1,0:T(8,128)} %copy-done.1, f32[2,136,256]{2,1,0:T(8,128)} %copy-done.3, f32[4,4,1024]{2,1,0:T(4,128)} %all_gather.19.refs_4_), custom_call_target="tpu_custom_call" | custom-call | flops 4294967296 | bytes 4194304 | tf_op jit(solution)/shard_map/pallas_call | solution.py:348
  (4 shorter events, 0.1 us)
Async XLA Ops:
  6.5 13.1 %copy-start = (bf16[512,1280]{1,0:T(8,128)(2,1)S(1)}, bf16[512,1280]{1,0:T(8,128)(2,1)}, u32[]{:S(2)}) copy-start(bf16[512,1280]{1,0:T(8,128)(2,1)} %param.10) | copy-start | bytes 3932164
  6.5 42.9 %all-gather.5.cloned.1.call-start = ((), (), s32[]{:S(2)}) async-start(), calls=%async_computation | async-start | bytes 1351680 | tf_op jit(solution)/shard_map/all_gather | solution.py:385
  8.5 41.0 %all-gather.7.cloned.1.call-start = ((), (), s32[]{:S(2)}) async-start(), calls=%async_computation.1 | async-start | bytes 1392640 | tf_op jit(solution)/shard_map/all_gather | solution.py:408
  8.5 11.1 %copy-start.2 = (bf16[32,1280]{1,0:T(8,128)(2,1)S(1)}, bf16[32,1280]{1,0:T(8,128)(2,1)}, u32[]{:S(2)}) copy-start(bf16[32,1280]{1,0:T(8,128)(2,1)} %param.12) | copy-start | bytes 245764
  8.5 16.8 %collective-permute-start.3 = (f32[136,256]{1,0:T(8,128)}, f32[136,256]{1,0:T(8,128)S(1)}, u32[]{:S(2)}, u32[]{:S(2)}) collective-permute-start(f32[136,256]{1,0:T(8,128)} %get-tuple-element.14), channel_id=1, source_target_pairs={{0,12},{4,8},{8,4},{12,0},{1,13},{5,9},{9,5},{13,1},{2,14},{6,10},... | collective-permute-start | bytes 417800 | tf_op jit(solution)/shard_map/ppermute | solution.py:161
  13.6 12.0 %collective-permute-start.2 = (f32[136,256]{1,0:T(8,128)}, f32[136,256]{1,0:T(8,128)S(1)}, u32[]{:S(2)}, u32[]{:S(2)}) collective-permute-start(f32[136,256]{1,0:T(8,128)} %get-tuple-element.14), channel_id=1, source_target_pairs={{0,8},{4,12},{8,0},{12,4},{1,9},{5,13},{9,1},{13,5},{2,10},{6,14},... | collective-permute-start | bytes 417800 | tf_op jit(solution)/shard_map/ppermute | solution.py:161
  13.6 9.3 %collective-permute-start = (f32[136,256]{1,0:T(8,128)}, f32[136,256]{1,0:T(8,128)S(1)}, u32[]{:S(2)}, u32[]{:S(2)}) collective-permute-start(f32[136,256]{1,0:T(8,128)} %get-tuple-element.14), channel_id=1, source_target_pairs={{0,4},{4,0},{8,12},{12,8},{1,5},{5,1},{9,13},{13,9},{2,6},{6,2},{1... | collective-permute-start | bytes 417800 | tf_op jit(solution)/shard_map/ppermute | solution.py:161
  19.6 9.6 %copy-start.5 = (s32[16]{0:T(128)S(1)}, s32[16]{0:T(128)}, u32[]{:S(2)}) copy-start(s32[16]{0:T(128)} %order_ref.1) | copy-start | bytes 196
  19.6 9.7 %copy-start.4 = (s32[16]{0:T(128)S(1)}, s32[16]{0:T(128)}, u32[]{:S(2)}) copy-start(s32[16]{0:T(128)} %param.16) | copy-start | bytes 196
  22.9 5.5 %collective-permute-start.1 = (f32[64,512]{1,0:T(8,128)S(1)}, f32[64,512]{1,0:T(8,128)S(1)}, u32[]{:S(2)}, u32[]{:S(2)}) collective-permute-start(f32[64,512]{1,0:T(8,128)S(1)} %pad_maximum_fusion.2), channel_id=1, source_target_pairs={{0,4},{4,0},{8,12},{12,8},{1,5},{5,1},{9,13},{13,9},{2,6},{6,2},{1... | collective-permute-start | bytes 393224 | tf_op jit(solution)/shard_map/ppermute | solution.py:161
  29.5 7.7 %collective-permute-start.7 = (f32[64,512]{1,0:T(8,128)S(1)}, f32[64,512]{1,0:T(8,128)S(1)}, u32[]{:S(2)}, u32[]{:S(2)}) collective-permute-start(f32[64,512]{1,0:T(8,128)S(1)} %pad_maximum_fusion.2), channel_id=1, source_target_pairs={{0,12},{4,8},{8,4},{12,0},{1,13},{5,9},{9,5},{13,1},{2,14},{6,10},... | collective-permute-start | bytes 393224 | tf_op jit(solution)/shard_map/ppermute | solution.py:161
  32.0 11.0 %collective-permute-start.6 = (f32[64,512]{1,0:T(8,128)S(1)}, f32[64,512]{1,0:T(8,128)S(1)}, u32[]{:S(2)}, u32[]{:S(2)}) collective-permute-start(f32[64,512]{1,0:T(8,128)S(1)} %pad_maximum_fusion.2), channel_id=1, source_target_pairs={{0,8},{4,12},{8,0},{12,4},{1,9},{5,13},{9,1},{13,5},{2,10},{6,14},... | collective-permute-start | bytes 393224 | tf_op jit(solution)/shard_map/ppermute | solution.py:161
  32.9 10.1 %collective-permute-start.4 = (f32[136,256]{1,0:T(8,128)S(1)}, f32[136,256]{1,0:T(8,128)S(1)}, u32[]{:S(2)}, u32[]{:S(2)}) collective-permute-start(f32[136,256]{1,0:T(8,128)S(1)} %collective-permute-done), channel_id=1, source_target_pairs={{0,2},{1,3},{2,0},{3,1},{4,6},{5,7},{6,4},{7,5},{8,10},{9,11},{10,... | collective-permute-start | bytes 417800 | tf_op jit(solution)/shard_map/ppermute | solution.py:161
  43.1 6.3 %copy-start.1 = (f32[2,136,256]{2,1,0:T(8,128)}, f32[2,136,256]{2,1,0:T(8,128)S(1)}, u32[]{:S(2)}) copy-start(f32[2,136,256]{2,1,0:T(8,128)S(1)} %pad_maximum_fusion.1.refs_2_) | copy-start | bytes 835588
  43.1 6.3 %collective-permute-start.5 = (f32[2,136,256]{2,1,0:T(8,128)S(1)}, f32[2,136,256]{2,1,0:T(8,128)S(1)}, u32[]{:S(2)}, u32[]{:S(2)}) collective-permute-start(f32[2,136,256]{2,1,0:T(8,128)S(1)} %pad_maximum_fusion.1.refs_2_), channel_id=1, source_target_pairs={{0,1},{1,0},{2,3},{3,2},{4,5},{5,4},{6,7},{7,6},{8,9},{9,8},{10,11... | collective-permute-start | bytes 835592 | tf_op jit(solution)/shard_map/ppermute | solution.py:161
  49.4 0.7 copy-start.3
Sparse Core Ops, SparseCore 0:
  8.9 19.5 all-gather.4
  30.1 17.2 all-gather.6

commit v6 on v5

--- a/solution.py
+++ b/solution.py
@@ -161,14 +161,10 @@
     return lax.ppermute(value, axis, [(i, i ^ s) for i in range(lax.axis_size(axis))])
 
 
-def exchange(value, axis):
-    return [value] + [swap(value, axis, s) for s in range(1, lax.axis_size(axis))]
-
-
 def solve_kernel(halves, ids_ref, order_ref, *refs):
     if halves:
-        own_ref, others_ref, near_ref, far_ref, grads_ref, out_ref = refs[:6]
-        gram, extra, work, left_ref, right_ref, tails, bank, sems = refs[6:]
+        own_ref, *piece_refs, grads_ref, out_ref = refs[:7]
+        gram, extra, work, left_ref, right_ref, tails, bank, sems = refs[7:]
     else:
         prior_ref, bank_ref, grads_ref, out_ref = refs[:4]
         gram, extra, work, left_ref, right_ref, bank, sems = refs[4:]
@@ -200,20 +196,15 @@
 
         for i in range(parts):
             place(own_ref.at[i, :span, :], i, width_index)
-            for s in range(2, parts):
-                first = (s - 2) * span
-                place(
-                    others_ref.at[i, first : first + span, :], i, lax.bitwise_xor(width_index, s)
-                )
             for c in range(bank_chunks):
                 first = span + c * bank_rows
                 start(own_ref.at[i, first : first + bank_rows, :], bank.at[i, c])
-        for sibling, source in enumerate((near_ref, far_ref)):
-            for across in range(2):
+        for distance, source in enumerate(piece_refs):
+            for s in range(1, parts):
                 place(
-                    source.at[across],
-                    lax.bitwise_xor(token_index, 2 * across + sibling),
-                    lax.bitwise_xor(width_index, 1),
+                    source.at[(s - 1) * span : s * span, :],
+                    lax.bitwise_xor(token_index, distance),
+                    lax.bitwise_xor(width_index, s),
                 )
     else:
         start(prior_ref, gram)
@@ -335,6 +326,7 @@
     size = grads.shape[2]
     rows = order.shape[0] + out_shape[1]
     copies = 2 + bank_shape[0] * (2 * bank_shape[0] + bank_shape[1])
+    near = len(prior_operands) - 1 if halves else 0
     vmem = pl.BlockSpec(memory_space=pltpu.VMEM)
     scratch = [
         pltpu.VMEM((size, size), f32),
@@ -349,12 +341,13 @@
         functools.partial(solve_kernel, halves),
         out_shape=jax.ShapeDtypeStruct(out_shape, f32),
         in_specs=[pl.BlockSpec(memory_space=pltpu.SMEM)] * 2
-        + [pl.BlockSpec(memory_space=pl.ANY)] * len(prior_operands)
+        + [pl.BlockSpec(memory_space=pltpu.HBM)] * (len(prior_operands) - near)
+        + [vmem] * near
         + [vmem],
         out_specs=vmem,
         scratch_shapes=scratch
         + [pltpu.VMEM(bank_shape, f32), pltpu.SemaphoreType.DMA((copies,))],
-        compiler_params=pltpu.CompilerParams(vmem_limit_bytes=60 * 2**20),
+        compiler_params=pltpu.CompilerParams(vmem_limit_bytes=40 * 2**20),
         cost_estimate=pl.CostEstimate(
             flops=4 * size**3, bytes_accessed=4 * size * size, transcendentals=size
         ),
@@ -383,7 +376,7 @@
     if halves:
         half, first = pack(prior_gram, query_bank)
         own = lax.all_gather(first, "tokens", axis=0)
-        pieces = exchange(half, "width")[1:]
+        pieces = [swap(half, "width", s) for s in range(1, width_count)]
         bank_shape = (token_count, query_bank.shape[1] // (2 * BLOCK), bank_rows, 2 * BLOCK)
     else:
         prior_block = lax.all_gather(prior_gram, "width", axis=1, tiled=True)
@@ -402,13 +395,22 @@
     )
     if halves:
         projected, pieces[0] = lax.optimization_barrier((projected, pieces[0]))
-    received = exchange(projected, "width")
-    if halves:
-        received[1], pieces = lax.optimization_barrier((received[1], pieces))
-        others = lax.all_gather(jnp.concatenate(pieces[1:], 0), "tokens", axis=0)
-        near = jnp.stack([pieces[0], swap(pieces[0], "tokens", 2)])
-        prior_operands = (own, others, near, swap(near, "tokens", 1))
-    total = sum(received)
+    total = projected + swap(projected, "width", 1)
+    if halves:
+        total, pieces = lax.optimization_barrier((total, pieces))
+        pieces = jnp.concatenate(pieces, 0)
+        across = swap(pieces, "tokens", 2)
+        prior_operands = (
+            own,
+            pieces,
+            swap(pieces, "tokens", 1),
+            across,
+            swap(across, "tokens", 1),
+        )
+    distance = 2
+    while distance < width_count:
+        total = total + swap(total, "width", distance)
+        distance *= 2
     local_slabs = lax.dynamic_slice_in_dim(slab_sequence, token_index * slab_count, slab_count)
     seq_numbers = jnp.arange(sequence_count, dtype=jnp.int32)
     local_lengths = jnp.sum(

time: 92.3 us -> 88.3 us (0.957)
  starting transfers between devices: 13.1 us -> 10.3 us
    ppermute x8, starting transfers between devices: 13 us -> 10.3 us  [swap(): lax.ppermute(value, axis, [(i, i ^ s) for i in range(lax.axis_size(axis))])]
  transfers between devices with their start and end apart: 10 -> 9, of which waited for: 5 -> 4; matrix products, arithmetic and copies ran while one was open for 8% -> 7% of each run, Pallas kernels for 0% -> 0%
where the time goes in v6:
time: 88.3 us; the launch traced here: 88.1 us
  Pallas kernels  36.3 us (41%)
  waiting for transfers between devices  15 us (17%)
  between operations  13.5 us (15%)
  starting transfers between devices  10.3 us (12%)
  matrix products  6.05 us (7%)
  blocking collectives  5.24 us (6%)
  local copies, waits for them, and re-layouts  1.46 us (2%)
    pallas_call x1, Pallas kernels, solve(): pl.pallas_call(functools.partial(solve_kernel, halves), out_shape=jax.Sha...  34.3 us
    ppermute x8, waiting for transfers between devices, swap(): lax.ppermute(value, axis, [(i, i ^ s) for i in range(lax.axis_size(axis))])  15 us
    ppermute x8, starting transfers between devices, swap(): lax.ppermute(value, axis, [(i, i ^ s) for i in range(lax.axis_size(axis))])  10.3 us
    dot_general x1, matrix products, local(): lax.dot_general(proj_in, layer_inputs, features, preferred_element_type=f32)  5.35 us
    all_gather x1, blocking collectives, local(): all_grads = lax.all_gather(vectors, 'tokens', axis=0)  5.24 us
    pallas_call x1, Pallas kernels, pack(): pl.pallas_call(pack_kernel, out_shape=(jax.ShapeDtypeStruct((span, 2 * BL...  1.93 us
  transfers between devices with their start and end apart: 9, of which 4 were waited for; matrix products, arithmetic and copies ran while one was open for 7% of the time, Pallas kernels for 0%

profile of v6, /device:TPU:0, one launch (start us, length us, event | category | flops | bytes accessed | tf_op | source)
XLA Modules:
  0.0 88.1 jit_solution(14367061279473027722)
XLA Ops:
  6.5 0.0 copy-start
  6.5 0.0 all-gather.3.cloned.1.call-start
  6.5 1.9 %shard_map.91 = (f32[136,256]{1,0:T(8,128)}, f32[264,256]{1,0:T(8,128)}) custom-call(f32[256,256]{1,0:T(8,128)} %prior_ref.1, f32[32,1024]{1,0:T(8,128)} %bank_ref.1), custom_call_target="tpu_custom_call" | custom-call | tf_op jit(solution)/shard_map/pallas_call | solution.py:149
  8.5 5.0 %collective-permute-start.3 = (f32[136,256]{1,0:T(8,128)}, f32[136,256]{1,0:T(8,128)S(1)}, u32[]{:S(2)}, u32[]{:S(2)}) collective-permute-start(f32[136,256]{1,0:T(8,128)} %get-tuple-element.14), channel_id=1, source_target_pairs={{0,12},{4,8},{8,4},{12,0},{1,13},{5,9},{9,5},{13,1},{2,14},{6,10},... | collective-permute-start | bytes 417800 | tf_op jit(solution)/shard_map/ppermute | solution.py:161
  13.5 0.0 collective-permute-start.2
  13.5 0.6 collective-permute-start
  14.1 0.0 all-gather.3.cloned.1.call-update
  14.1 0.0 copy-start.4
  14.1 5.4 %fusion.7 = f32[32,512]{1,0:T(8,128)S(1)} fusion(bf16[32,6912]{1,0:T(8,128)(2,1)} %param.11, bf16[512,6912]{1,0:T(8,128)(2,1)} %param.9), kind=kOutput, calls=%fused_computation.16 | convolution fusion | flops 226492416 | bytes 7585792 | tf_op jit(solution)/shard_map/dot_general | solution.py:391
  19.5 0.0 copy-done
  19.5 0.0 copy-done.4
  19.5 0.0 copy-start.3
  19.5 0.0 copy-start.5
  19.5 0.5 fusion.8
  20.0 0.0 copy-start.2
  20.0 2.8 %collective-permute-done = f32[136,256]{1,0:T(8,128)S(1)} collective-permute-done((f32[136,256]{1,0:T(8,128)}, f32[136,256]{1,0:T(8,128)S(1)}, u32[]{:S(2)}, u32[]{:S(2)}) %collective-permute-start) | collective-permute-done | bytes 139296 | tf_op jit(solution)/shard_map/ppermute | solution.py:161
  22.8 2.4 %collective-permute-start.1 = (f32[64,512]{1,0:T(8,128)S(1)}, f32[64,512]{1,0:T(8,128)S(1)}, u32[]{:S(2)}, u32[]{:S(2)}) collective-permute-start(f32[64,512]{1,0:T(8,128)S(1)} %pad_maximum_fusion), channel_id=1, source_target_pairs={{0,4},{4,0},{8,12},{12,8},{1,5},{5,1},{9,13},{13,9},{2,6},{6,2},{1... | collective-permute-start | bytes 393224 | tf_op jit(solution)/shard_map/ppermute | solution.py:161
  25.2 3.1 %collective-permute-done.1 = f32[64,512]{1,0:T(8,128)S(1)} collective-permute-done((f32[64,512]{1,0:T(8,128)S(1)}, f32[64,512]{1,0:T(8,128)S(1)}, u32[]{:S(2)}, u32[]{:S(2)}) %collective-permute-start.1) | collective-permute-done | bytes 131104 | tf_op jit(solution)/shard_map/ppermute | solution.py:161
  28.3 0.0 collective-permute-done.3
  28.3 0.0 collective-permute-done.2
  28.4 1.6 %collective-permute-start.5 = (f32[408,256]{1,0:T(8,128)S(1)}, f32[408,256]{1,0:T(8,128)S(1)}, u32[]{:S(2)}, u32[]{:S(2)}) collective-permute-start(f32[408,256]{1,0:T(8,128)S(1)} %constant_dynamic-update-slice_fusion.refs_1_), channel_id=1, source_target_pairs={{0,2},{1,3},{2,0},{3,1},{4,6},{5,7},{6,4},{7,5},{8,10},{9,11},{10,... | collective-permute-start | bytes 1253384 | tf_op jit(solution)/shard_map/ppermute | solution.py:161
  30.0 0.0 copy-done.3
  30.1 0.1 dynamic_slice.3
  30.1 0.0 copy-done.5
  30.1 0.2 select_reduce_fusion
  30.3 0.6 collective-permute-start.7
  30.9 0.1 fusion.6
  31.0 0.0 collective-permute-start.4
  31.0 7.2 %collective-permute-done.7 = f32[64,512]{1,0:T(8,128)S(1)} collective-permute-done((f32[64,512]{1,0:T(8,128)S(1)}, f32[64,512]{1,0:T(8,128)S(1)}, u32[]{:S(2)}, u32[]{:S(2)}) %collective-permute-start.7) | collective-permute-done | bytes 131104 | tf_op jit(solution)/shard_map/ppermute | solution.py:161
  38.2 1.9 %collective-permute-done.5.refs_3_ = f32[408,256]{1,0:T(8,128)S(1)} collective-permute-done((f32[408,256]{1,0:T(8,128)S(1)}, f32[408,256]{1,0:T(8,128)S(1)}, u32[]{:S(2)}, u32[]{:S(2)}) %collective-permute-start.5) | collective-permute-done | bytes 417824 | tf_op jit(solution)/shard_map/ppermute | solution.py:161
  40.1 0.0 collective-permute-start.6
  40.1 0.2 fusion
  40.3 0.1 all_gather_reshape.3
  40.4 5.2 %all_gather.11.refs_5_ = f32[4,4,1024]{2,1,0:T(4,128)S(1)} all-gather(f32[1,4,1024]{2,1,0:T(4,128)S(1)} %all_gather_reshape.3), channel_id=1, replica_groups=mesh['groups'=2,'width'=4,'tokens'=4] {'tokens'}, dimensions={0}, use_global_device_ids=true | all-gather | bytes 81920 | tf_op jit(solution)/shard_map/all_gather | solution.py:426
  45.7 0.0 collective-permute-done.4.refs_2_
  45.7 0.0 collective-permute-done.6.refs_4_
  45.7 0.0 all-gather.3.cloned.1.call-done
  45.7 0.0 copy-done.2
  45.7 0.0 copy-start.1
  45.7 1.2 %copy-done.1 = f32[1056,256]{1,0:T(8,128)S(1)} copy-done((f32[1056,256]{1,0:T(8,128)S(1)}, f32[1056,256]{1,0:T(8,128)}, u32[]{:S(2)}) %copy-start.1) | copy-done | bytes 1081368
  46.9 34.3 %shard_map.92 = f32[4,32]{1,0:T(4,128)} custom-call(s32[128]{0:T(128)S(1)} %copy-done.2, s32[16]{0:T(128)S(1)} %copy-done.3, f32[4,264,256]{2,1,0:T(8,128)S(1)} %bitcast.18, f32[408,256]{1,0:T(8,128)S(1)} %constant_dynamic-update-slice_fusion.refs_1_, f32[408,256]{1,0:T(8,128)S(1)} %collective-permute-done.4.refs_2_, ...), custom_call_target="tpu_custom_call" | custom-call | flops 4294967296 | bytes 4194304 | tf_op jit(solution)/shard_map/pallas_call | solution.py:340
  (7 shorter events, 0.1 us)
Async XLA Ops:
  6.5 12.9 %copy-start = (bf16[512,1280]{1,0:T(8,128)(2,1)S(1)}, bf16[512,1280]{1,0:T(8,128)(2,1)}, u32[]{:S(2)}) copy-start(bf16[512,1280]{1,0:T(8,128)(2,1)} %param.10) | copy-start | bytes 3932164
  6.5 39.2 %all-gather.3.cloned.1.call-start = ((), (), s32[]{:S(2)}) async-start(), calls=%async_computation | async-start | bytes 1351680 | tf_op jit(solution)/shard_map/all_gather | solution.py:378
  8.5 19.9 %collective-permute-start.3 = (f32[136,256]{1,0:T(8,128)}, f32[136,256]{1,0:T(8,128)S(1)}, u32[]{:S(2)}, u32[]{:S(2)}) collective-permute-start(f32[136,256]{1,0:T(8,128)} %get-tuple-element.14), channel_id=1, source_target_pairs={{0,12},{4,8},{8,4},{12,0},{1,13},{5,9},{9,5},{13,1},{2,14},{6,10},... | collective-permute-start | bytes 417800 | tf_op jit(solution)/shard_map/ppermute | solution.py:161
  13.5 14.8 %collective-permute-start.2 = (f32[136,256]{1,0:T(8,128)}, f32[136,256]{1,0:T(8,128)S(1)}, u32[]{:S(2)}, u32[]{:S(2)}) collective-permute-start(f32[136,256]{1,0:T(8,128)} %get-tuple-element.14), channel_id=1, source_target_pairs={{0,8},{4,12},{8,0},{12,4},{1,9},{5,13},{9,1},{13,5},{2,10},{6,14},... | collective-permute-start | bytes 417800 | tf_op jit(solution)/shard_map/ppermute | solution.py:161
  13.5 9.3 %collective-permute-start = (f32[136,256]{1,0:T(8,128)}, f32[136,256]{1,0:T(8,128)S(1)}, u32[]{:S(2)}, u32[]{:S(2)}) collective-permute-start(f32[136,256]{1,0:T(8,128)} %get-tuple-element.14), channel_id=1, source_target_pairs={{0,4},{4,0},{8,12},{12,8},{1,5},{5,1},{9,13},{13,9},{2,6},{6,2},{1... | collective-permute-start | bytes 417800 | tf_op jit(solution)/shard_map/ppermute | solution.py:161
  14.1 5.4 %copy-start.4 = (bf16[32,1280]{1,0:T(8,128)(2,1)S(1)}, bf16[32,1280]{1,0:T(8,128)(2,1)}, u32[]{:S(2)}) copy-start(bf16[32,1280]{1,0:T(8,128)(2,1)} %param.12) | copy-start | bytes 245764
  19.5 10.6 %copy-start.3 = (s32[16]{0:T(128)S(1)}, s32[16]{0:T(128)}, u32[]{:S(2)}) copy-start(s32[16]{0:T(128)} %order_ref.1) | copy-start | bytes 196
  19.5 10.6 %copy-start.5 = (s32[16]{0:T(128)S(1)}, s32[16]{0:T(128)}, u32[]{:S(2)}) copy-start(s32[16]{0:T(128)} %param.16) | copy-start | bytes 196
  20.0 25.7 %copy-start.2 = (s32[128]{0:T(128)S(1)}, s32[128]{0:T(128)}, u32[]{:S(2)}) copy-start(s32[128]{0:T(128)} %ids_ref.1) | copy-start | bytes 1540
  22.8 5.5 %collective-permute-start.1 = (f32[64,512]{1,0:T(8,128)S(1)}, f32[64,512]{1,0:T(8,128)S(1)}, u32[]{:S(2)}, u32[]{:S(2)}) collective-permute-start(f32[64,512]{1,0:T(8,128)S(1)} %pad_maximum_fusion), channel_id=1, source_target_pairs={{0,4},{4,0},{8,12},{12,8},{1,5},{5,1},{9,13},{13,9},{2,6},{6,2},{1... | collective-permute-start | bytes 393224 | tf_op jit(solution)/shard_map/ppermute | solution.py:161
  28.4 11.7 %collective-permute-start.5 = (f32[408,256]{1,0:T(8,128)S(1)}, f32[408,256]{1,0:T(8,128)S(1)}, u32[]{:S(2)}, u32[]{:S(2)}) collective-permute-start(f32[408,256]{1,0:T(8,128)S(1)} %constant_dynamic-update-slice_fusion.refs_1_), channel_id=1, source_target_pairs={{0,2},{1,3},{2,0},{3,1},{4,6},{5,7},{6,4},{7,5},{8,10},{9,11},{10,... | collective-permute-start | bytes 1253384 | tf_op jit(solution)/shard_map/ppermute | solution.py:161
  30.3 7.9 %collective-permute-start.7 = (f32[64,512]{1,0:T(8,128)S(1)}, f32[64,512]{1,0:T(8,128)S(1)}, u32[]{:S(2)}, u32[]{:S(2)}) collective-permute-start(f32[64,512]{1,0:T(8,128)S(1)} %add.9), channel_id=1, source_target_pairs={{0,8},{4,12},{8,0},{12,4},{1,9},{5,13},{9,1},{13,5},{2,10},{6,14},... | collective-permute-start | bytes 393224 | tf_op jit(solution)/shard_map/ppermute | solution.py:161
  31.0 14.7 %collective-permute-start.4 = (f32[408,256]{1,0:T(8,128)S(1)}, f32[408,256]{1,0:T(8,128)S(1)}, u32[]{:S(2)}, u32[]{:S(2)}) collective-permute-start(f32[408,256]{1,0:T(8,128)S(1)} %constant_dynamic-update-slice_fusion.refs_1_), channel_id=1, source_target_pairs={{0,1},{1,0},{2,3},{3,2},{4,5},{5,4},{6,7},{7,6},{8,9},{9,8},{10,11... | collective-permute-start | bytes 1253384 | tf_op jit(solution)/shard_map/ppermute | solution.py:161
  40.1 5.6 %collective-permute-start.6 = (f32[408,256]{1,0:T(8,128)S(1)}, f32[408,256]{1,0:T(8,128)S(1)}, u32[]{:S(2)}, u32[]{:S(2)}) collective-permute-start(f32[408,256]{1,0:T(8,128)S(1)} %collective-permute-done.5.refs_3_), channel_id=1, source_target_pairs={{0,1},{1,0},{2,3},{3,2},{4,5},{5,4},{6,7},{7,6},{8,9},{9,8},{10,11... | collective-permute-start | bytes 1253384 | tf_op jit(solution)/shard_map/ppermute | solution.py:161
  45.7 1.2 %copy-start.1 = (f32[1056,256]{1,0:T(8,128)S(1)}, f32[1056,256]{1,0:T(8,128)}, u32[]{:S(2)}) copy-start(f32[1056,256]{1,0:T(8,128)} %all-gather.3.cloned.1.call-done) | copy-start | bytes 3244036
Sparse Core Ops, SparseCore 0:
  14.2 19.0 all-gather.2

commit v7 on v6

--- a/solution.py
+++ b/solution.py
@@ -247,7 +247,13 @@
             )
     trace = jnp.sum(diagonal) + jnp.sum(grads * grads) / sequences
     damping = damping_ratio * trace / size
-    for low in range(0, size, BLOCK):
+    waiting = []
+
+    def pending():
+        if waiting:
+            waiting.pop(0)()
+
+    def add_product(low):
         high = low + BLOCK
         product = contract(left[:, low:high], right[:, low:], 0, 0) / sequences
         gram[low:high, low:high] = (
@@ -257,16 +263,14 @@
         )
         if high < size:
             gram[low:high, high:] = gram[low:high, high:] + product[:, BLOCK:]
+
+    add_product(0)
+    for low in range(BLOCK, size, BLOCK):
+        waiting.append(functools.partial(add_product, low))
     scores = [jnp.zeros((queries, sequences), f32)]
     lower = lax.broadcasted_iota(jnp.int32, (BLOCK, BLOCK), 0) >= lax.broadcasted_iota(
         jnp.int32, (BLOCK, BLOCK), 1
     )
-    waiting = []
-
-    def pending():
-        if waiting:
-            waiting.pop(0)()
-
     def panel(inverse_left, block, low, high):
         left, right = both_terms(
             contract(inverse_left, right_terms(gram[block : block + BLOCK, low:high], 0), 1, 0), 0
@@ -347,7 +351,7 @@
         out_specs=vmem,
         scratch_shapes=scratch
         + [pltpu.VMEM(bank_shape, f32), pltpu.SemaphoreType.DMA((copies,))],
-        compiler_params=pltpu.CompilerParams(vmem_limit_bytes=40 * 2**20),
+        compiler_params=pltpu.CompilerParams(vmem_limit_bytes=52 * 2**20),
         cost_estimate=pl.CostEstimate(
             flops=4 * size**3, bytes_accessed=4 * size * size, transcendentals=size
         ),

time: 88.3 us -> 87.1 us (0.986)
  local copies, waits for them, and re-layouts: 1.46 us -> 0.23 us
    unnamed x14 -> x12, local copies, waits for them, and re-layouts: 1.28 us -> 0.05 us
  transfers between devices with their start and end apart: 9 -> 9, of which waited for: 4 -> 4; matrix products, arithmetic and copies ran while one was open for 7% -> 8% of each run, Pallas kernels for 0% -> 0%
where the time goes in v7:
time: 87.1 us; the launch traced here: 86.9 us
  Pallas kernels  36.3 us (42%)
  waiting for transfers between devices  15 us (17%)
  between operations  13.5 us (15%)
  starting transfers between devices  10.3 us (12%)
  matrix products  6.04 us (7%)
  blocking collectives  5.24 us (6%)
    pallas_call x1, Pallas kernels, solve(): pl.pallas_call(functools.partial(solve_kernel, halves), out_shape=jax.Sha...  34.3 us
    ppermute x8, waiting for transfers between devices, swap(): lax.ppermute(value, axis, [(i, i ^ s) for i in range(lax.axis_size(axis))])  15 us
    ppermute x8, starting transfers between devices, swap(): lax.ppermute(value, axis, [(i, i ^ s) for i in range(lax.axis_size(axis))])  10.3 us
    dot_general x1, matrix products, local(): lax.dot_general(proj_in, layer_inputs, features, preferred_element_type=f32)  5.35 us
    all_gather x1, blocking collectives, local(): all_grads = lax.all_gather(vectors, 'tokens', axis=0)  5.24 us
    pallas_call x1, Pallas kernels, pack(): pl.pallas_call(pack_kernel, out_shape=(jax.ShapeDtypeStruct((span, 2 * BL...  1.92 us
  transfers between devices with their start and end apart: 9, of which 4 were waited for; matrix products, arithmetic and copies ran while one was open for 8% of the time, Pallas kernels for 0%

profile of v7, /device:TPU:0, one launch (start us, length us, event | category | flops | bytes accessed | tf_op | source)
XLA Modules:
  0.0 86.9 jit_solution(12057583669490467857)
XLA Ops:
  6.5 0.0 copy-start
  6.5 0.0 all-gather.3.cloned.1.call-start
  6.5 1.9 %shard_map.91 = (f32[136,256]{1,0:T(8,128)}, f32[264,256]{1,0:T(8,128)}) custom-call(f32[256,256]{1,0:T(8,128)} %prior_ref.1, f32[32,1024]{1,0:T(8,128)} %bank_ref.1), custom_call_target="tpu_custom_call" | custom-call | tf_op jit(solution)/shard_map/pallas_call | solution.py:149
  8.5 5.0 %collective-permute-start.3 = (f32[136,256]{1,0:T(8,128)}, f32[136,256]{1,0:T(8,128)S(1)}, u32[]{:S(2)}, u32[]{:S(2)}) collective-permute-start(f32[136,256]{1,0:T(8,128)} %get-tuple-element.14), channel_id=1, source_target_pairs={{0,12},{4,8},{8,4},{12,0},{1,13},{5,9},{9,5},{13,1},{2,14},{6,10},... | collective-permute-start | bytes 417800 | tf_op jit(solution)/shard_map/ppermute | solution.py:161
  13.5 0.0 collective-permute-start.2
  13.5 0.6 collective-permute-start
  14.1 0.0 all-gather.3.cloned.1.call-update
  14.1 0.0 copy-start.3
  14.1 5.3 %fusion.7 = f32[32,512]{1,0:T(8,128)S(1)} fusion(bf16[32,6912]{1,0:T(8,128)(2,1)} %param.11, bf16[512,6912]{1,0:T(8,128)(2,1)} %param.9), kind=kOutput, calls=%fused_computation.16 | convolution fusion | flops 226492416 | bytes 7585792 | tf_op jit(solution)/shard_map/dot_general | solution.py:395
  19.5 0.0 copy-done
  19.5 0.0 copy-done.3
  19.5 0.0 copy-start.2
  19.5 0.0 copy-start.4
  19.5 0.5 fusion.8
  20.0 0.0 copy-start.1
  20.0 2.8 %collective-permute-done = f32[136,256]{1,0:T(8,128)S(1)} collective-permute-done((f32[136,256]{1,0:T(8,128)}, f32[136,256]{1,0:T(8,128)S(1)}, u32[]{:S(2)}, u32[]{:S(2)}) %collective-permute-start) | collective-permute-done | bytes 139296 | tf_op jit(solution)/shard_map/ppermute | solution.py:161
  22.8 2.4 %collective-permute-start.1 = (f32[64,512]{1,0:T(8,128)S(1)}, f32[64,512]{1,0:T(8,128)S(1)}, u32[]{:S(2)}, u32[]{:S(2)}) collective-permute-start(f32[64,512]{1,0:T(8,128)S(1)} %pad_maximum_fusion), channel_id=1, source_target_pairs={{0,4},{4,0},{8,12},{12,8},{1,5},{5,1},{9,13},{13,9},{2,6},{6,2},{1... | collective-permute-start | bytes 393224 | tf_op jit(solution)/shard_map/ppermute | solution.py:161
  25.2 3.1 %collective-permute-done.1 = f32[64,512]{1,0:T(8,128)S(1)} collective-permute-done((f32[64,512]{1,0:T(8,128)S(1)}, f32[64,512]{1,0:T(8,128)S(1)}, u32[]{:S(2)}, u32[]{:S(2)}) %collective-permute-start.1) | collective-permute-done | bytes 131104 | tf_op jit(solution)/shard_map/ppermute | solution.py:161
  28.3 0.0 collective-permute-done.3
  28.3 0.0 collective-permute-done.2
  28.4 1.6 %collective-permute-start.5 = (f32[408,256]{1,0:T(8,128)S(1)}, f32[408,256]{1,0:T(8,128)S(1)}, u32[]{:S(2)}, u32[]{:S(2)}) collective-permute-start(f32[408,256]{1,0:T(8,128)S(1)} %constant_dynamic-update-slice_fusion.refs_1_), channel_id=1, source_target_pairs={{0,2},{1,3},{2,0},{3,1},{4,6},{5,7},{6,4},{7,5},{8,10},{9,11},{10,... | collective-permute-start | bytes 1253384 | tf_op jit(solution)/shard_map/ppermute | solution.py:161
  30.0 0.0 copy-done.2
  30.0 0.1 dynamic_slice.3
  30.1 0.0 copy-done.4
  30.1 0.2 select_reduce_fusion
  30.3 0.6 collective-permute-start.7
  30.9 0.1 fusion.6
  31.0 0.0 collective-permute-start.4
  31.0 7.2 %collective-permute-done.7 = f32[64,512]{1,0:T(8,128)S(1)} collective-permute-done((f32[64,512]{1,0:T(8,128)S(1)}, f32[64,512]{1,0:T(8,128)S(1)}, u32[]{:S(2)}, u32[]{:S(2)}) %collective-permute-start.7) | collective-permute-done | bytes 131104 | tf_op jit(solution)/shard_map/ppermute | solution.py:161
  38.2 1.9 %collective-permute-done.5.refs_3_ = f32[408,256]{1,0:T(8,128)S(1)} collective-permute-done((f32[408,256]{1,0:T(8,128)S(1)}, f32[408,256]{1,0:T(8,128)S(1)}, u32[]{:S(2)}, u32[]{:S(2)}) %collective-permute-start.5) | collective-permute-done | bytes 417824 | tf_op jit(solution)/shard_map/ppermute | solution.py:161
  40.1 0.0 collective-permute-start.6
  40.1 0.2 fusion
  40.3 0.1 all_gather_reshape.3
  40.4 5.2 %all_gather.11.refs_5_ = f32[4,4,1024]{2,1,0:T(4,128)S(1)} all-gather(f32[1,4,1024]{2,1,0:T(4,128)S(1)} %all_gather_reshape.3), channel_id=1, replica_groups=mesh['groups'=2,'width'=4,'tokens'=4] {'tokens'}, dimensions={0}, use_global_device_ids=true | all-gather | bytes 81920 | tf_op jit(solution)/shard_map/all_gather | solution.py:430
  45.7 0.0 collective-permute-done.4.refs_2_
  45.7 0.0 collective-permute-done.6.refs_4_
  45.7 0.0 all-gather.3.cloned.1.call-done
  45.7 0.0 copy-done.1
  45.7 34.3 %shard_map.92 = f32[4,32]{1,0:T(4,128)} custom-call(s32[128]{0:T(128)S(1)} %copy-done.1, s32[16]{0:T(128)S(1)} %copy-done.2, f32[4,264,256]{2,1,0:T(8,128)} %bitcast.18, f32[408,256]{1,0:T(8,128)S(1)} %constant_dynamic-update-slice_fusion.refs_1_, f32[408,256]{1,0:T(8,128)S(1)} %collective-permute-done.4.refs_2_, ...), custom_call_target="tpu_custom_call" | custom-call | flops 4294967296 | bytes 4194304 | tf_op jit(solution)/shard_map/pallas_call | solution.py:344
  (7 shorter events, 0.1 us)
Async XLA Ops:
  6.5 12.9 %copy-start = (bf16[512,1280]{1,0:T(8,128)(2,1)S(1)}, bf16[512,1280]{1,0:T(8,128)(2,1)}, u32[]{:S(2)}) copy-start(bf16[512,1280]{1,0:T(8,128)(2,1)} %param.10) | copy-start | bytes 3932164
  6.5 39.2 %all-gather.3.cloned.1.call-start = ((), (), s32[]{:S(2)}) async-start(), calls=%async_computation | async-start | bytes 1351680 | tf_op jit(solution)/shard_map/all_gather | solution.py:382
  8.5 19.9 %collective-permute-start.3 = (f32[136,256]{1,0:T(8,128)}, f32[136,256]{1,0:T(8,128)S(1)}, u32[]{:S(2)}, u32[]{:S(2)}) collective-permute-start(f32[136,256]{1,0:T(8,128)} %get-tuple-element.14), channel_id=1, source_target_pairs={{0,12},{4,8},{8,4},{12,0},{1,13},{5,9},{9,5},{13,1},{2,14},{6,10},... | collective-permute-start | bytes 417800 | tf_op jit(solution)/shard_map/ppermute | solution.py:161
  13.5 14.8 %collective-permute-start.2 = (f32[136,256]{1,0:T(8,128)}, f32[136,256]{1,0:T(8,128)S(1)}, u32[]{:S(2)}, u32[]{:S(2)}) collective-permute-start(f32[136,256]{1,0:T(8,128)} %get-tuple-element.14), channel_id=1, source_target_pairs={{0,8},{4,12},{8,0},{12,4},{1,9},{5,13},{9,1},{13,5},{2,10},{6,14},... | collective-permute-start | bytes 417800 | tf_op jit(solution)/shard_map/ppermute | solution.py:161
  13.5 9.3 %collective-permute-start = (f32[136,256]{1,0:T(8,128)}, f32[136,256]{1,0:T(8,128)S(1)}, u32[]{:S(2)}, u32[]{:S(2)}) collective-permute-start(f32[136,256]{1,0:T(8,128)} %get-tuple-element.14), channel_id=1, source_target_pairs={{0,4},{4,0},{8,12},{12,8},{1,5},{5,1},{9,13},{13,9},{2,6},{6,2},{1... | collective-permute-start | bytes 417800 | tf_op jit(solution)/shard_map/ppermute | solution.py:161
  14.1 5.4 %copy-start.3 = (bf16[32,1280]{1,0:T(8,128)(2,1)S(1)}, bf16[32,1280]{1,0:T(8,128)(2,1)}, u32[]{:S(2)}) copy-start(bf16[32,1280]{1,0:T(8,128)(2,1)} %param.12) | copy-start | bytes 245764
  19.5 10.6 %copy-start.2 = (s32[16]{0:T(128)S(1)}, s32[16]{0:T(128)}, u32[]{:S(2)}) copy-start(s32[16]{0:T(128)} %order_ref.1) | copy-start | bytes 196
  19.5 10.6 %copy-start.4 = (s32[16]{0:T(128)S(1)}, s32[16]{0:T(128)}, u32[]{:S(2)}) copy-start(s32[16]{0:T(128)} %param.16) | copy-start | bytes 196
  20.0 25.7 %copy-start.1 = (s32[128]{0:T(128)S(1)}, s32[128]{0:T(128)}, u32[]{:S(2)}) copy-start(s32[128]{0:T(128)} %ids_ref.1) | copy-start | bytes 1540
  22.8 5.5 %collective-permute-start.1 = (f32[64,512]{1,0:T(8,128)S(1)}, f32[64,512]{1,0:T(8,128)S(1)}, u32[]{:S(2)}, u32[]{:S(2)}) collective-permute-start(f32[64,512]{1,0:T(8,128)S(1)} %pad_maximum_fusion), channel_id=1, source_target_pairs={{0,4},{4,0},{8,12},{12,8},{1,5},{5,1},{9,13},{13,9},{2,6},{6,2},{1... | collective-permute-start | bytes 393224 | tf_op jit(solution)/shard_map/ppermute | solution.py:161
  28.4 11.7 %collective-permute-start.5 = (f32[408,256]{1,0:T(8,128)S(1)}, f32[408,256]{1,0:T(8,128)S(1)}, u32[]{:S(2)}, u32[]{:S(2)}) collective-permute-start(f32[408,256]{1,0:T(8,128)S(1)} %constant_dynamic-update-slice_fusion.refs_1_), channel_id=1, source_target_pairs={{0,2},{1,3},{2,0},{3,1},{4,6},{5,7},{6,4},{7,5},{8,10},{9,11},{10,... | collective-permute-start | bytes 1253384 | tf_op jit(solution)/shard_map/ppermute | solution.py:161
  30.3 7.9 %collective-permute-start.7 = (f32[64,512]{1,0:T(8,128)S(1)}, f32[64,512]{1,0:T(8,128)S(1)}, u32[]{:S(2)}, u32[]{:S(2)}) collective-permute-start(f32[64,512]{1,0:T(8,128)S(1)} %add.9), channel_id=1, source_target_pairs={{0,8},{4,12},{8,0},{12,4},{1,9},{5,13},{9,1},{13,5},{2,10},{6,14},... | collective-permute-start | bytes 393224 | tf_op jit(solution)/shard_map/ppermute | solution.py:161
  31.0 14.7 %collective-permute-start.4 = (f32[408,256]{1,0:T(8,128)S(1)}, f32[408,256]{1,0:T(8,128)S(1)}, u32[]{:S(2)}, u32[]{:S(2)}) collective-permute-start(f32[408,256]{1,0:T(8,128)S(1)} %constant_dynamic-update-slice_fusion.refs_1_), channel_id=1, source_target_pairs={{0,1},{1,0},{2,3},{3,2},{4,5},{5,4},{6,7},{7,6},{8,9},{9,8},{10,11... | collective-permute-start | bytes 1253384 | tf_op jit(solution)/shard_map/ppermute | solution.py:161
  40.1 5.6 %collective-permute-start.6 = (f32[408,256]{1,0:T(8,128)S(1)}, f32[408,256]{1,0:T(8,128)S(1)}, u32[]{:S(2)}, u32[]{:S(2)}) collective-permute-start(f32[408,256]{1,0:T(8,128)S(1)} %collective-permute-done.5.refs_3_), channel_id=1, source_target_pairs={{0,1},{1,0},{2,3},{3,2},{4,5},{5,4},{6,7},{7,6},{8,9},{9,8},{10,11... | collective-permute-start | bytes 1253384 | tf_op jit(solution)/shard_map/ppermute | solution.py:161
Sparse Core Ops, SparseCore 0:
  14.2 19.0 all-gather.2

commit v8 on v7

--- a/solution.py
+++ b/solution.py
@@ -397,8 +397,6 @@
         ],
         axis=0,
     )
-    if halves:
-        projected, pieces[0] = lax.optimization_barrier((projected, pieces[0]))
     total = projected + swap(projected, "width", 1)
     if halves:
         total, pieces = lax.optimization_barrier((total, pieces))

time: 87.1 us -> 90.2 us (1.036)
  waiting for transfers between devices: 15 us -> 18.9 us
    ppermute x8, waiting for transfers between devices: 15 us -> 18.9 us  [swap(): lax.ppermute(value, axis, [(i, i ^ s) for i in range(lax.axis_size(axis))])]
  transfers between devices with their start and end apart: 9 -> 9, of which waited for: 4 -> 4; matrix products, arithmetic and copies ran while one was open for 8% -> 7% of each run, Pallas kernels for 0% -> 0%
where the time goes in v8:
time: 90.2 us; the launch traced here: 90.1 us
  Pallas kernels  36.3 us (40%)
  waiting for transfers between devices  18.9 us (21%)
  between operations  13.5 us (15%)
  starting transfers between devices  9.49 us (11%)
  matrix products  6.06 us (7%)
  blocking collectives  5.27 us (6%)
    pallas_call x1, Pallas kernels, solve(): pl.pallas_call(functools.partial(solve_kernel, halves), out_shape=jax.Sha...  34.3 us
    ppermute x8, waiting for transfers between devices, swap(): lax.ppermute(value, axis, [(i, i ^ s) for i in range(lax.axis_size(axis))])  18.9 us
    ppermute x8, starting transfers between devices, swap(): lax.ppermute(value, axis, [(i, i ^ s) for i in range(lax.axis_size(axis))])  9.49 us
    dot_general x1, matrix products, local(): lax.dot_general(proj_in, layer_inputs, features, preferred_element_type=f32)  5.35 us
    all_gather x1, blocking collectives, local(): all_grads = lax.all_gather(vectors, 'tokens', axis=0)  5.27 us
    pallas_call x1, Pallas kernels, pack(): pl.pallas_call(pack_kernel, out_shape=(jax.ShapeDtypeStruct((span, 2 * BL...  1.93 us
  transfers between devices with their start and end apart: 9, of which 4 were waited for; matrix products, arithmetic and copies ran while one was open for 7% of the time, Pallas kernels for 0%

profile of v8, /device:TPU:0, one launch (start us, length us, event | category | flops | bytes accessed | tf_op | source)
XLA Modules:
  0.0 90.1 jit_solution(1739003789189136772)
XLA Ops:
  6.5 0.0 copy-start
  6.5 0.0 all-gather.3.cloned.1.call-start
  6.5 1.9 %shard_map.91 = (f32[136,256]{1,0:T(8,128)}, f32[264,256]{1,0:T(8,128)}) custom-call(f32[256,256]{1,0:T(8,128)} %prior_ref.1, f32[32,1024]{1,0:T(8,128)} %bank_ref.1), custom_call_target="tpu_custom_call" | custom-call | tf_op jit(solution)/shard_map/pallas_call | solution.py:149
  8.5 0.0 all-gather.3.cloned.1.call-update
  8.5 0.0 copy-start.3
  8.5 5.3 %fusion.8 = f32[32,512]{1,0:T(8,128)S(1)} fusion(bf16[32,6912]{1,0:T(8,128)(2,1)} %param.11, bf16[512,6912]{1,0:T(8,128)(2,1)} %param.9), kind=kOutput, calls=%fused_computation.17 | convolution fusion | flops 226492416 | bytes 7585792 | tf_op jit(solution)/shard_map/dot_general | solution.py:395
  13.9 0.0 copy-done
  13.9 0.0 copy-done.3
  13.9 0.0 copy-start.4
  13.9 0.0 copy-start.2
  13.9 0.0 copy-start.5
  13.9 0.5 fusion.9
  14.4 0.0 copy-start.1
  14.4 3.1 %collective-permute-start = (f32[64,512]{1,0:T(8,128)S(1)}, f32[64,512]{1,0:T(8,128)S(1)}, u32[]{:S(2)}, u32[]{:S(2)}) collective-permute-start(f32[64,512]{1,0:T(8,128)S(1)} %pad_maximum_fusion), channel_id=1, source_target_pairs={{0,4},{4,0},{8,12},{12,8},{1,5},{5,1},{9,13},{13,9},{2,6},{6,2},{1... | collective-permute-start | bytes 393224 | tf_op jit(solution)/shard_map/ppermute | solution.py:161
  17.5 0.0 copy-done.4
  17.5 2.5 %collective-permute-start.3 = (f32[136,256]{1,0:T(8,128)S(1)}, f32[136,256]{1,0:T(8,128)S(1)}, u32[]{:S(2)}, u32[]{:S(2)}) collective-permute-start(f32[136,256]{1,0:T(8,128)S(1)} %copy-done.4), channel_id=1, source_target_pairs={{0,12},{4,8},{8,4},{12,0},{1,13},{5,9},{9,5},{13,1},{2,14},{6,10},... | collective-permute-start | bytes 417800 | tf_op jit(solution)/shard_map/ppermute | solution.py:161
  20.0 0.1 collective-permute-start.2
  20.1 1.8 %collective-permute-start.1 = (f32[136,256]{1,0:T(8,128)S(1)}, f32[136,256]{1,0:T(8,128)S(1)}, u32[]{:S(2)}, u32[]{:S(2)}) collective-permute-start(f32[136,256]{1,0:T(8,128)S(1)} %copy-done.4), channel_id=1, source_target_pairs={{0,4},{4,0},{8,12},{12,8},{1,5},{5,1},{9,13},{13,9},{2,6},{6,2},{1... | collective-permute-start | bytes 417800 | tf_op jit(solution)/shard_map/ppermute | solution.py:161
  21.9 0.0 collective-permute-done
  21.9 5.5 %collective-permute-done.3 = f32[136,256]{1,0:T(8,128)S(1)} collective-permute-done((f32[136,256]{1,0:T(8,128)S(1)}, f32[136,256]{1,0:T(8,128)S(1)}, u32[]{:S(2)}, u32[]{:S(2)}) %collective-permute-start.3) | collective-permute-done | bytes 139296 | tf_op jit(solution)/shard_map/ppermute | solution.py:161
  27.4 5.0 %collective-permute-done.2 = f32[136,256]{1,0:T(8,128)S(1)} collective-permute-done((f32[136,256]{1,0:T(8,128)S(1)}, f32[136,256]{1,0:T(8,128)S(1)}, u32[]{:S(2)}, u32[]{:S(2)}) %collective-permute-start.2) | collective-permute-done | bytes 139296 | tf_op jit(solution)/shard_map/ppermute | solution.py:161
  32.4 0.0 collective-permute-done.1
  32.5 1.6 %collective-permute-start.5 = (f32[408,256]{1,0:T(8,128)S(1)}, f32[408,256]{1,0:T(8,128)S(1)}, u32[]{:S(2)}, u32[]{:S(2)}) collective-permute-start(f32[408,256]{1,0:T(8,128)S(1)} %constant_dynamic-update-slice_fusion.refs_1_), channel_id=1, source_target_pairs={{0,2},{1,3},{2,0},{3,1},{4,6},{5,7},{6,4},{7,5},{8,10},{9,11},{10,... | collective-permute-start | bytes 1253384 | tf_op jit(solution)/shard_map/ppermute | solution.py:161
  34.1 0.0 copy-done.2
  34.1 0.1 dynamic_slice.3
  34.1 0.0 copy-done.5
  34.1 0.2 select_reduce_fusion
  34.3 0.4 collective-permute-start.7
  34.8 0.1 fusion.6
  34.8 0.0 collective-permute-start.4
  34.8 7.3 %collective-permute-done.7 = f32[64,512]{1,0:T(8,128)S(1)} collective-permute-done((f32[64,512]{1,0:T(8,128)S(1)}, f32[64,512]{1,0:T(8,128)S(1)}, u32[]{:S(2)}, u32[]{:S(2)}) %collective-permute-start.7) | collective-permute-done | bytes 131104 | tf_op jit(solution)/shard_map/ppermute | solution.py:161
  42.1 1.1 %collective-permute-done.5.refs_3_ = f32[408,256]{1,0:T(8,128)S(1)} collective-permute-done((f32[408,256]{1,0:T(8,128)S(1)}, f32[408,256]{1,0:T(8,128)S(1)}, u32[]{:S(2)}, u32[]{:S(2)}) %collective-permute-start.5) | collective-permute-done | bytes 417824 | tf_op jit(solution)/shard_map/ppermute | solution.py:161
  43.2 0.0 collective-permute-start.6
  43.2 0.2 fusion
  43.5 0.1 all_gather_reshape.3
  43.6 5.3 %all_gather.11.refs_5_ = f32[4,4,1024]{2,1,0:T(4,128)S(1)} all-gather(f32[1,4,1024]{2,1,0:T(4,128)S(1)} %all_gather_reshape.3), channel_id=1, replica_groups=mesh['groups'=2,'width'=4,'tokens'=4] {'tokens'}, dimensions={0}, use_global_device_ids=true | all-gather | bytes 81920 | tf_op jit(solution)/shard_map/all_gather | solution.py:428
  48.8 0.0 collective-permute-done.4.refs_2_
  48.8 0.0 collective-permute-done.6.refs_4_
  48.8 0.0 all-gather.3.cloned.1.call-done
  48.8 0.0 copy-done.1
  48.8 34.3 %shard_map.92 = f32[4,32]{1,0:T(4,128)} custom-call(s32[128]{0:T(128)S(1)} %copy-done.1, s32[16]{0:T(128)S(1)} %copy-done.2, f32[4,264,256]{2,1,0:T(8,128)} %bitcast.18, f32[408,256]{1,0:T(8,128)S(1)} %constant_dynamic-update-slice_fusion.refs_1_, f32[408,256]{1,0:T(8,128)S(1)} %collective-permute-done.4.refs_2_, ...), custom_call_target="tpu_custom_call" | custom-call | flops 4294967296 | bytes 4194304 | tf_op jit(solution)/shard_map/pallas_call | solution.py:344
  (7 shorter events, 0.1 us)
Async XLA Ops:
  6.5 7.3 %copy-start = (bf16[512,1280]{1,0:T(8,128)(2,1)S(1)}, bf16[512,1280]{1,0:T(8,128)(2,1)}, u32[]{:S(2)}) copy-start(bf16[512,1280]{1,0:T(8,128)(2,1)} %param.10) | copy-start | bytes 3932164
  6.5 42.3 %all-gather.3.cloned.1.call-start = ((), (), s32[]{:S(2)}) async-start(), calls=%async_computation | async-start | bytes 1351680 | tf_op jit(solution)/shard_map/all_gather | solution.py:382
  8.5 5.4 %copy-start.3 = (bf16[32,1280]{1,0:T(8,128)(2,1)S(1)}, bf16[32,1280]{1,0:T(8,128)(2,1)}, u32[]{:S(2)}) copy-start(bf16[32,1280]{1,0:T(8,128)(2,1)} %param.12) | copy-start | bytes 245764
  13.9 3.6 %copy-start.4 = (f32[136,256]{1,0:T(8,128)S(1)}, f32[136,256]{1,0:T(8,128)}, u32[]{:S(2)}) copy-start(f32[136,256]{1,0:T(8,128)} %get-tuple-element.12) | copy-start | bytes 417796
  13.9 20.2 %copy-start.2 = (s32[16]{0:T(128)S(1)}, s32[16]{0:T(128)}, u32[]{:S(2)}) copy-start(s32[16]{0:T(128)} %order_ref.1) | copy-start | bytes 196
  13.9 20.2 %copy-start.5 = (s32[16]{0:T(128)S(1)}, s32[16]{0:T(128)}, u32[]{:S(2)}) copy-start(s32[16]{0:T(128)} %param.16) | copy-start | bytes 196
  14.4 34.5 %copy-start.1 = (s32[128]{0:T(128)S(1)}, s32[128]{0:T(128)}, u32[]{:S(2)}) copy-start(s32[128]{0:T(128)} %ids_ref.1) | copy-start | bytes 1540
  14.4 7.5 %collective-permute-start = (f32[64,512]{1,0:T(8,128)S(1)}, f32[64,512]{1,0:T(8,128)S(1)}, u32[]{:S(2)}, u32[]{:S(2)}) collective-permute-start(f32[64,512]{1,0:T(8,128)S(1)} %pad_maximum_fusion), channel_id=1, source_target_pairs={{0,4},{4,0},{8,12},{12,8},{1,5},{5,1},{9,13},{13,9},{2,6},{6,2},{1... | collective-permute-start | bytes 393224 | tf_op jit(solution)/shard_map/ppermute | solution.py:161
  17.5 9.9 %collective-permute-start.3 = (f32[136,256]{1,0:T(8,128)S(1)}, f32[136,256]{1,0:T(8,128)S(1)}, u32[]{:S(2)}, u32[]{:S(2)}) collective-permute-start(f32[136,256]{1,0:T(8,128)S(1)} %copy-done.4), channel_id=1, source_target_pairs={{0,12},{4,8},{8,4},{12,0},{1,13},{5,9},{9,5},{13,1},{2,14},{6,10},... | collective-permute-start | bytes 417800 | tf_op jit(solution)/shard_map/ppermute | solution.py:161
  20.0 12.5 %collective-permute-start.2 = (f32[136,256]{1,0:T(8,128)S(1)}, f32[136,256]{1,0:T(8,128)S(1)}, u32[]{:S(2)}, u32[]{:S(2)}) collective-permute-start(f32[136,256]{1,0:T(8,128)S(1)} %copy-done.4), channel_id=1, source_target_pairs={{0,8},{4,12},{8,0},{12,4},{1,9},{5,13},{9,1},{13,5},{2,10},{6,14},... | collective-permute-start | bytes 417800 | tf_op jit(solution)/shard_map/ppermute | solution.py:161
  20.1 12.3 %collective-permute-start.1 = (f32[136,256]{1,0:T(8,128)S(1)}, f32[136,256]{1,0:T(8,128)S(1)}, u32[]{:S(2)}, u32[]{:S(2)}) collective-permute-start(f32[136,256]{1,0:T(8,128)S(1)} %copy-done.4), channel_id=1, source_target_pairs={{0,4},{4,0},{8,12},{12,8},{1,5},{5,1},{9,13},{13,9},{2,6},{6,2},{1... | collective-permute-start | bytes 417800 | tf_op jit(solution)/shard_map/ppermute | solution.py:161
  32.5 10.7 %collective-permute-start.5 = (f32[408,256]{1,0:T(8,128)S(1)}, f32[408,256]{1,0:T(8,128)S(1)}, u32[]{:S(2)}, u32[]{:S(2)}) collective-permute-start(f32[408,256]{1,0:T(8,128)S(1)} %constant_dynamic-update-slice_fusion.refs_1_), channel_id=1, source_target_pairs={{0,2},{1,3},{2,0},{3,1},{4,6},{5,7},{6,4},{7,5},{8,10},{9,11},{10,... | collective-permute-start | bytes 1253384 | tf_op jit(solution)/shard_map/ppermute | solution.py:161
  34.3 7.8 %collective-permute-start.7 = (f32[64,512]{1,0:T(8,128)S(1)}, f32[64,512]{1,0:T(8,128)S(1)}, u32[]{:S(2)}, u32[]{:S(2)}) collective-permute-start(f32[64,512]{1,0:T(8,128)S(1)} %fusion.7), channel_id=1, source_target_pairs={{0,8},{4,12},{8,0},{12,4},{1,9},{5,13},{9,1},{13,5},{2,10},{6,14},... | collective-permute-start | bytes 393224 | tf_op jit(solution)/shard_map/ppermute | solution.py:161
  34.8 14.0 %collective-permute-start.4 = (f32[408,256]{1,0:T(8,128)S(1)}, f32[408,256]{1,0:T(8,128)S(1)}, u32[]{:S(2)}, u32[]{:S(2)}) collective-permute-start(f32[408,256]{1,0:T(8,128)S(1)} %constant_dynamic-update-slice_fusion.refs_1_), channel_id=1, source_target_pairs={{0,1},{1,0},{2,3},{3,2},{4,5},{5,4},{6,7},{7,6},{8,9},{9,8},{10,11... | collective-permute-start | bytes 1253384 | tf_op jit(solution)/shard_map/ppermute | solution.py:161
  43.2 5.6 %collective-permute-start.6 = (f32[408,256]{1,0:T(8,128)S(1)}, f32[408,256]{1,0:T(8,128)S(1)}, u32[]{:S(2)}, u32[]{:S(2)}) collective-permute-start(f32[408,256]{1,0:T(8,128)S(1)} %collective-permute-done.5.refs_3_), channel_id=1, source_target_pairs={{0,1},{1,0},{2,3},{3,2},{4,5},{5,4},{6,7},{7,6},{8,9},{9,8},{10,11... | collective-permute-start | bytes 1253384 | tf_op jit(solution)/shard_map/ppermute | solution.py:161
Sparse Core Ops, SparseCore 0:
  8.9 19.5 all-gather.2
